TPU v7x, 32 devices: a whole 2x2x4 slice. The times are simulated.
32 devices in a mesh: fs: 4 (over y, x), ep: 8 (over z, core).
Axes of the slice: x: 2, y: 2, z: 4, core: 2. Of those that a mesh axis runs over, the one named last changes fastest.
Arguments:
- tokens: bfloat16 [4096, 2880], P(('fs', 'ep')), may hold values from -6 to 6
- seq_lengths: int32 [32, 3], P(('fs', 'ep')), may hold values from 1 to 64, 128 in all within a row
- routes: int32 [4096, 4], P(('fs', 'ep')), may hold values from 0 to 15, all different within a row; in each aligned block of 128 rows (0 to 127, 128 to 255, ...) at most 48 rows name the same one
- attn_gain: bfloat16 [2880], P('fs'), may hold values from 0.5 to 1.5
- w_query: bfloat16 [2880, 4096], P('fs'), may hold values from -0.109375 to 0.109375
- b_query: bfloat16 [4096], P('fs'), may hold values from -3 to 3
- w_key: bfloat16 [2880, 512], P('fs'), may hold values from -0.109375 to 0.109375
- b_key: bfloat16 [512], P('fs'), may hold values from -3 to 3
- w_value: bfloat16 [2880, 512], P('fs'), may hold values from -0.109375 to 0.109375
- b_value: bfloat16 [512], P('fs'), may hold values from -3 to 3
- sinks: bfloat16 [64], P('fs'), may hold values from -1 to 2
- w_out: bfloat16 [4096, 2880], P('fs'), may hold values from -0.75 to 0.75
- b_out: bfloat16 [2880], P('fs'), may hold values from -2 to 2
- ffn_gain: bfloat16 [2880], P('fs'), may hold values from 0.5 to 1.5
- w_router: bfloat16 [2880, 16], P('fs'), may hold values from -0.0546875 to 0.0546875
- b_router: bfloat16 [16], P('fs'), may hold values from -1 to 1
- w_gate: bfloat16 [16, 2880, 2880], P('ep', None, 'fs'), may hold values from -0.109375 to 0.109375
- b_gate: bfloat16 [16, 2880], P('ep', 'fs'), may hold values from -1 to 1
- w_up: bfloat16 [16, 2880, 2880], P('ep', None, 'fs'), may hold values from -0.109375 to 0.109375
- b_up: bfloat16 [16, 2880], P('ep', 'fs'), may hold values from -1 to 1
- w_down: bfloat16 [16, 2880, 2880], P('ep', 'fs'), may hold values from -0.21875 to 0.21875
- b_down: bfloat16 [16, 2880], P('ep'), may hold values from -0.59765625 to 0.59765625
- cotangent: bfloat16 [4096, 2880], P(('fs', 'ep')), may hold values from -6 to 6
Outputs:
- block_out: bfloat16 [4096, 2880], P(('fs', 'ep'))
- grad_tokens: float32 [4096, 2880], P(('fs', 'ep'))
- grad_attn_gain: float32 [2880], P('fs')
- grad_w_query: float32 [2880, 4096], P('fs')
- grad_b_query: float32 [4096], P('fs')
- grad_w_key: float32 [2880, 512], P('fs')
- grad_b_key: float32 [512], P('fs')
- grad_w_value: float32 [2880, 512], P('fs')
- grad_b_value: float32 [512], P('fs')
- grad_sinks: float32 [64], P('fs')
- grad_w_out: float32 [4096, 2880], P('fs')
- grad_b_out: float32 [2880], P('fs')
- grad_ffn_gain: float32 [2880], P('fs')
- grad_w_router: float32 [2880, 16], P('fs')
- grad_b_router: float32 [16], P('fs')
- grad_w_gate: float32 [16, 2880, 2880], P('ep', None, 'fs')
- grad_b_gate: float32 [16, 2880], P('ep', 'fs')
- grad_w_up: float32 [16, 2880, 2880], P('ep', None, 'fs')
- grad_b_up: float32 [16, 2880], P('ep', 'fs')
- grad_w_down: float32 [16, 2880, 2880], P('ep', 'fs')
- grad_b_down: float32 [16, 2880], P('ep')
Inputs may be any that keep to these rules, and one draw needn't show every extreme that they name: `routes`: each row names 4 different experts; among the 128 rows of one device no expert is named more than 48 times. `seq_lengths`: each device's 3 lengths sum to 128.
All inputs are finite; a program needn't handle non-finite values.
Results may differ from a plain program's by a relative error of at most 0.028.
Values may be sent and summed in bfloat16 or wider, within the bound.
A program may use at most 704 MiB of HBM per device.

v0:
```python
from functools import partial

import jax
import jax.numpy as jnp
from jax import lax
from jax.sharding import PartitionSpec as P

QUERY_HEADS = 64
KEY_VALUE_HEADS = 8
HEAD_SIZE = 64
TOP = 4
EXP_DEV = 2


EPSILON = 1e-05
ROPE_BASE = 150000.0
SWIGLU_ALPHA = 1.702
CLAMP_LIMIT = 7.0
MASKED_SCORE = -1e30


def layout(lengths, card_rows):
    seq_ends = jnp.cumsum(lengths)
    places = jnp.arange(card_rows, dtype=jnp.int32)
    past_end = (places[:, None] >= seq_ends[None, :]).astype(jnp.int32)
    segment_ids = jnp.sum(past_end, axis=1)
    position = places - jnp.sum(past_end * lengths[None, :], axis=1)
    return (segment_ids, position)


def tables(position, half_dim):
    inv_freq = jnp.exp(-jnp.log(ROPE_BASE) * jnp.arange(half_dim, dtype=jnp.float32) / half_dim)
    angles = position.astype(jnp.float32)[:, None] * inv_freq[None, :]
    return (jnp.cos(angles)[:, None, :], jnp.sin(angles)[:, None, :])


def apply_rotation(value_matrix, cosine_table, sine_table):
    half_dim = value_matrix.shape[-1] // 2
    lower_half = value_matrix[..., :half_dim]
    upper_half = value_matrix[..., half_dim:]
    return jnp.concatenate(
        [
            lower_half * cosine_table - upper_half * sine_table,
            upper_half * cosine_table + lower_half * sine_table,
        ],
        axis=-1,
    )


def undo_rotation(value_matrix, cosine_table, sine_table):
    half_dim = value_matrix.shape[-1] // 2
    lower_half = value_matrix[..., :half_dim]
    upper_half = value_matrix[..., half_dim:]
    return jnp.concatenate(
        [
            lower_half * cosine_table + upper_half * sine_table,
            upper_half * cosine_table - lower_half * sine_table,
        ],
        axis=-1,
    )


def norm_scale(value_matrix):
    return lax.rsqrt(jnp.mean(value_matrix * value_matrix, axis=-1, keepdims=True) + EPSILON)


def norm_back(value_matrix, inv_scale, gain, grad_norm):
    weighted = grad_norm * gain
    grad_values = inv_scale * weighted - value_matrix * inv_scale**3 * jnp.mean(
        weighted * value_matrix, axis=-1, keepdims=True
    )
    grad_gain = jnp.sum(grad_norm * value_matrix * inv_scale, axis=0)
    return (grad_values, grad_gain)


def masked_scores(query, first_row, key_rot, segment_ids):
    rows_per_block = query.shape[0]
    raw_scores = jnp.einsum(
        "qhgd,khd->hgqk", query, key_rot, preferred_element_type=jnp.float32
    ) * HEAD_SIZE ** (-0.5)
    query_place = first_row + jnp.arange(rows_per_block, dtype=jnp.int32)
    key_place = jnp.arange(segment_ids.shape[0], dtype=jnp.int32)
    allowed = (segment_ids[:, None] == segment_ids[None, :]) & (
        query_place[:, None] >= key_place[None, :]
    )
    return jnp.where(allowed[None, None], raw_scores, MASKED_SCORE)


def attend_forward(block_item, key_rot, value_rot, segment_ids, sink_score):
    query, first_row = block_item
    masked = masked_scores(query, first_row, key_rot, segment_ids)
    top_score = jnp.maximum(jnp.max(masked, axis=-1), sink_score[:, :, None])
    exponent = jnp.exp(masked - top_score[..., None])
    denominator = jnp.sum(exponent, axis=-1) + jnp.exp(sink_score[:, :, None] - top_score)
    weights_att = (exponent / denominator[..., None]).astype(jnp.bfloat16)
    mixed_heads = jnp.einsum(
        "hgqk,khd->qhgd", weights_att, value_rot, preferred_element_type=jnp.float32
    )
    return (mixed_heads, top_score + jnp.log(denominator))


def attend_backward(running, block_item, key_rot, value_rot, segment_ids, sink_score):
    query, first_row, log_total, grad_mixed = block_item
    grad_key, grad_value, grad_sink = running
    masked = masked_scores(query, first_row, key_rot, segment_ids)
    probs = jnp.exp(masked - log_total[..., None])
    sink_prob = jnp.exp(sink_score[:, :, None] - log_total)
    grad_probs = jnp.einsum(
        "qhgd,khd->hgqk", grad_mixed, value_rot, preferred_element_type=jnp.float32
    )
    grad_value = grad_value + jnp.einsum(
        "hgqk,qhgd->khd", probs.astype(jnp.bfloat16), grad_mixed, preferred_element_type=jnp.float32
    )
    row_delta = jnp.sum(probs * grad_probs, axis=-1)
    grad_scores = (probs * (grad_probs - row_delta[..., None])).astype(jnp.bfloat16)
    grad_query = jnp.einsum(
        "hgqk,khd->qhgd", grad_scores, key_rot, preferred_element_type=jnp.float32
    ) * HEAD_SIZE ** (-0.5)
    grad_key = grad_key + jnp.einsum(
        "hgqk,qhgd->khd", grad_scores, query, preferred_element_type=jnp.float32
    ) * HEAD_SIZE ** (-0.5)
    grad_sink = grad_sink - jnp.sum(sink_prob * row_delta, axis=-1)
    return ((grad_key, grad_value, grad_sink), grad_query)


def left_dot(left, right):
    return jnp.dot(left.T, right, preferred_element_type=jnp.float32)


def per_device(
    tokens,
    seq_lengths,
    routes,
    attn_gain,
    w_query,
    b_query,
    w_key,
    b_key,
    w_value,
    b_value,
    sinks,
    w_out,
    b_out,
    ffn_gain,
    w_router,
    b_router,
    w_gate,
    b_gate,
    w_up,
    b_up,
    w_down,
    b_down,
    cotangent,
):
    card_rows = tokens.shape[0]
    query_group = QUERY_HEADS // KEY_VALUE_HEADS
    expert_count = w_gate.shape[0] * lax.axis_size("ep")
    capacity = 3 * card_rows * TOP // (2 * expert_count)
    slot_block = EXP_DEV * capacity
    pair_count = card_rows * TOP
    gathered = (
        lax.all_gather(w_query, "fs", axis=0, tiled=True),
        lax.all_gather(w_key, "fs", axis=0, tiled=True),
        lax.all_gather(w_value, "fs", axis=0, tiled=True),
        lax.all_gather(w_out, "fs", axis=0, tiled=True),
        lax.all_gather(w_router, "fs", axis=0, tiled=True),
        lax.all_gather(attn_gain, "fs", axis=0, tiled=True),
        lax.all_gather(ffn_gain, "fs", axis=0, tiled=True),
        lax.all_gather(b_query, "fs", axis=0, tiled=True),
        lax.all_gather(b_key, "fs", axis=0, tiled=True),
        lax.all_gather(b_value, "fs", axis=0, tiled=True),
        lax.all_gather(b_out, "fs", axis=0, tiled=True),
        lax.all_gather(sinks, "fs", axis=0, tiled=True),
        lax.all_gather(b_router, "fs", axis=0, tiled=True),
    )
    wq, wk, wv, wo, wr, gain_one_b, gain_two_b, bq, bk, bv, bo, sink_broadcast, br = gathered
    gain_one = gain_one_b.astype(jnp.float32)
    gain_two = gain_two_b.astype(jnp.float32)
    sink_score = sink_broadcast.astype(jnp.float32).reshape(KEY_VALUE_HEADS, query_group)
    x_float = tokens.astype(jnp.float32)
    segment_ids, position = layout(seq_lengths[0], card_rows)
    cosine_table, sine_table = tables(position, HEAD_SIZE // 2)
    scale_one = norm_scale(x_float)
    norm_attn = (x_float * scale_one * gain_one).astype(jnp.bfloat16)
    query_pre = jnp.dot(norm_attn, wq, preferred_element_type=jnp.float32) + bq.astype(jnp.float32)
    key_unrotated = jnp.dot(norm_attn, wk, preferred_element_type=jnp.float32) + bk.astype(
        jnp.float32
    )
    value_projected = jnp.dot(norm_attn, wv, preferred_element_type=jnp.float32) + bv.astype(
        jnp.float32
    )
    query_matrix = (
        apply_rotation(
            query_pre.reshape(card_rows, QUERY_HEADS, HEAD_SIZE), cosine_table, sine_table
        )
        .astype(jnp.bfloat16)
        .reshape(card_rows, KEY_VALUE_HEADS, query_group, HEAD_SIZE)
    )
    key_matrix = apply_rotation(
        key_unrotated.reshape(card_rows, KEY_VALUE_HEADS, HEAD_SIZE), cosine_table, sine_table
    ).astype(jnp.bfloat16)
    value_matrix = value_projected.astype(jnp.bfloat16).reshape(
        card_rows, KEY_VALUE_HEADS, HEAD_SIZE
    )
    rows_per_block = min(card_rows, 512)
    block_list = card_rows // rows_per_block
    query_block_list = query_matrix.reshape(
        block_list, rows_per_block, KEY_VALUE_HEADS, query_group, HEAD_SIZE
    )
    block_starts = jnp.arange(block_list, dtype=jnp.int32) * rows_per_block
    mixed_heads, log_total = lax.map(
        partial(
            attend_forward,
            key_rot=key_matrix,
            value_rot=value_matrix,
            segment_ids=segment_ids,
            sink_score=sink_score,
        ),
        (query_block_list, block_starts),
    )
    mixed_b = mixed_heads.reshape(card_rows, QUERY_HEADS * HEAD_SIZE).astype(jnp.bfloat16)
    resid = (
        x_float + jnp.dot(mixed_b, wo, preferred_element_type=jnp.float32) + bo.astype(jnp.float32)
    )
    scale_two = norm_scale(resid)
    norm_ffn = (resid * scale_two * gain_two).astype(jnp.bfloat16)
    logits = jnp.dot(norm_ffn, wr, preferred_element_type=jnp.float32) + br.astype(jnp.float32)
    one_hot = (
        routes[:, :, None] == jnp.arange(expert_count, dtype=jnp.int32)[None, None, :]
    ).astype(jnp.float32)
    chosen = jnp.sum(one_hot * logits[:, None, :], axis=-1)
    gate_exp = jnp.exp(chosen - jnp.max(chosen, axis=-1, keepdims=True))
    gate_probs = gate_exp / jnp.sum(gate_exp, axis=-1, keepdims=True)
    pair_expert = routes.reshape(pair_count)
    pair_hot = (pair_expert[:, None] == jnp.arange(expert_count, dtype=jnp.int32)[None, :]).astype(
        jnp.int32
    )
    pair_rank = jnp.sum((jnp.cumsum(pair_hot, axis=0) - pair_hot) * pair_hot, axis=1)
    slot_index = pair_expert * capacity + pair_rank
    slot_owner = (
        jnp.full((expert_count * capacity,), pair_count, jnp.int32)
        .at[slot_index]
        .set(jnp.arange(pair_count, dtype=jnp.int32))
    )
    slot_live = slot_owner < pair_count
    owner_pair = jnp.minimum(slot_owner, pair_count - 1)
    owner_token = owner_pair // TOP
    send_rows = jnp.where(slot_live[:, None], norm_ffn[owner_token], jnp.zeros((), jnp.bfloat16))
    arrived = lax.all_to_all(send_rows, "ep", split_axis=0, concat_axis=0, tiled=True)
    per_fs = arrived.shape[0]
    every_row = lax.all_gather(arrived, "fs", axis=0, tiled=True)
    groups = every_row.shape[0] // slot_block
    x_all = every_row.reshape(groups, EXP_DEV, capacity, every_row.shape[1])
    gate_pre = (
        jnp.einsum("secd,edf->secf", x_all, w_gate, preferred_element_type=jnp.float32)
        + b_gate.astype(jnp.float32)[None, :, None, :]
    )
    up_pre = (
        jnp.einsum("secd,edf->secf", x_all, w_up, preferred_element_type=jnp.float32)
        + b_up.astype(jnp.float32)[None, :, None, :]
    )
    gate_soft = CLAMP_LIMIT * jnp.tanh(gate_pre / CLAMP_LIMIT)
    up_soft = CLAMP_LIMIT * jnp.tanh(up_pre / CLAMP_LIMIT)
    gate_sig = jax.nn.sigmoid(SWIGLU_ALPHA * gate_soft)
    glu_part = gate_soft * gate_sig
    middle = ((up_soft + 1.0) * glu_part).astype(jnp.bfloat16)
    summed = lax.psum_scatter(
        jnp.einsum("secf,efd->secd", middle, w_down, preferred_element_type=jnp.float32)
        .reshape(lax.axis_size("fs") * per_fs, w_down.shape[2])
        .astype(jnp.bfloat16),
        "fs",
        scatter_dimension=0,
        tiled=True,
    ).astype(jnp.float32)
    results = (
        (
            summed.reshape(-1, EXP_DEV, capacity, summed.shape[1])
            + b_down.astype(jnp.float32)[None, :, None, :]
        )
        .reshape(per_fs, summed.shape[1])
        .astype(jnp.bfloat16)
    )
    returned = lax.all_to_all(results, "ep", split_axis=0, concat_axis=0, tiled=True)
    picked = returned[slot_index].astype(jnp.float32).reshape(card_rows, TOP, returned.shape[1])
    block_out = resid + jnp.sum(gate_probs[:, :, None] * picked, axis=1)
    grad_out = cotangent.astype(jnp.float32)
    pair_grad = (
        (gate_probs[:, :, None] * grad_out[:, None, :])
        .reshape(pair_count, grad_out.shape[1])
        .astype(jnp.bfloat16)
    )
    gate_grad = jnp.sum(grad_out[:, None, :] * picked, axis=-1)
    chosen_grad = gate_probs * (gate_grad - jnp.sum(gate_probs * gate_grad, axis=-1, keepdims=True))
    logit_grad = jnp.sum(one_hot * chosen_grad[:, :, None], axis=1).astype(jnp.bfloat16)
    grad_br = jnp.sum(logit_grad, axis=0, dtype=jnp.float32)
    norm_ffn_grad = jnp.dot(logit_grad, wr.T, preferred_element_type=jnp.float32)
    slot_grad = jnp.where(slot_live[:, None], pair_grad[owner_pair], jnp.zeros((), jnp.bfloat16))
    grad_arrived = lax.all_to_all(slot_grad, "ep", split_axis=0, concat_axis=0, tiled=True)
    grad_all = lax.all_gather(grad_arrived, "fs", axis=0, tiled=True).reshape(
        groups, EXP_DEV, capacity, grad_arrived.shape[1]
    )
    middle_grad = jnp.einsum("secd,efd->secf", grad_all, w_down, preferred_element_type=jnp.float32)
    grad_w_down = jnp.einsum("secf,secd->efd", middle, grad_all, preferred_element_type=jnp.float32)
    grad_b_down = jnp.sum(grad_all, axis=(0, 2), dtype=jnp.float32)
    up_grad = (middle_grad * glu_part * (1.0 - (up_soft / CLAMP_LIMIT) ** 2)).astype(jnp.bfloat16)
    gate_grad_pre = (
        middle_grad
        * (up_soft + 1.0)
        * (gate_sig + SWIGLU_ALPHA * gate_soft * gate_sig * (1.0 - gate_sig))
        * (1.0 - (gate_soft / CLAMP_LIMIT) ** 2)
    ).astype(jnp.bfloat16)
    grad_w_gate = jnp.einsum(
        "secd,secf->edf", x_all, gate_grad_pre, preferred_element_type=jnp.float32
    )
    grad_b_gate = jnp.sum(gate_grad_pre, axis=(0, 2), dtype=jnp.float32)
    grad_w_up = jnp.einsum("secd,secf->edf", x_all, up_grad, preferred_element_type=jnp.float32)
    grad_b_up = jnp.sum(up_grad, axis=(0, 2), dtype=jnp.float32)
    term = jnp.einsum("secf,edf->secd", gate_grad_pre, w_gate, preferred_element_type=jnp.float32)
    term = term + jnp.einsum("secf,edf->secd", up_grad, w_up, preferred_element_type=jnp.float32)
    row_grads = lax.psum_scatter(
        term.reshape(lax.axis_size("fs") * per_fs, w_gate.shape[1]).astype(jnp.bfloat16),
        "fs",
        scatter_dimension=0,
        tiled=True,
    )
    grad_back = lax.all_to_all(row_grads, "ep", split_axis=0, concat_axis=0, tiled=True)
    norm_ffn_grad = norm_ffn_grad + jnp.sum(
        grad_back[slot_index].astype(jnp.float32).reshape(card_rows, TOP, grad_back.shape[1]),
        axis=1,
    )
    resid_norm_grad, grad_gain_two = norm_back(resid, scale_two, gain_two, norm_ffn_grad)
    resid_grad = grad_out + resid_norm_grad
    branch_grad = resid_grad.astype(jnp.bfloat16)
    grad_bo = jnp.sum(branch_grad, axis=0, dtype=jnp.float32)
    mixed_heads_gradient = jnp.dot(branch_grad, wo.T, preferred_element_type=jnp.float32).astype(
        jnp.bfloat16
    )
    start_running = (
        jnp.zeros((card_rows, KEY_VALUE_HEADS, HEAD_SIZE), jnp.float32),
        jnp.zeros((card_rows, KEY_VALUE_HEADS, HEAD_SIZE), jnp.float32),
        jnp.zeros((KEY_VALUE_HEADS, query_group), jnp.float32),
    )
    running, query_grad = lax.scan(
        partial(
            attend_backward,
            key_rot=key_matrix,
            value_rot=value_matrix,
            segment_ids=segment_ids,
            sink_score=sink_score,
        ),
        start_running,
        (
            query_block_list,
            block_starts,
            log_total,
            mixed_heads_gradient.reshape(
                block_list, rows_per_block, KEY_VALUE_HEADS, query_group, HEAD_SIZE
            ),
        ),
    )
    key_gradient, value_gradient, sink_grad = running
    query_pre_grad = (
        undo_rotation(
            query_grad.reshape(card_rows, QUERY_HEADS, HEAD_SIZE), cosine_table, sine_table
        )
        .reshape(card_rows, QUERY_HEADS * HEAD_SIZE)
        .astype(jnp.bfloat16)
    )
    key_pre_grad = (
        undo_rotation(key_gradient, cosine_table, sine_table)
        .reshape(card_rows, KEY_VALUE_HEADS * HEAD_SIZE)
        .astype(jnp.bfloat16)
    )
    value_projected_gradient = value_gradient.reshape(
        card_rows, KEY_VALUE_HEADS * HEAD_SIZE
    ).astype(jnp.bfloat16)
    grad_bq = jnp.sum(query_pre_grad, axis=0, dtype=jnp.float32)
    grad_bk = jnp.sum(key_pre_grad, axis=0, dtype=jnp.float32)
    grad_bv = jnp.sum(value_projected_gradient, axis=0, dtype=jnp.float32)
    norm_attn_grad = jnp.dot(query_pre_grad, wq.T, preferred_element_type=jnp.float32)
    norm_attn_grad = norm_attn_grad + jnp.dot(
        key_pre_grad, wk.T, preferred_element_type=jnp.float32
    )
    norm_attn_grad = norm_attn_grad + jnp.dot(
        value_projected_gradient, wv.T, preferred_element_type=jnp.float32
    )
    input_norm_grad, grad_gain_one = norm_back(x_float, scale_one, gain_one, norm_attn_grad)
    grad_tokens = resid_grad + input_norm_grad
    grad_wq = left_dot(norm_attn, query_pre_grad)
    grad_wk = left_dot(norm_attn, key_pre_grad)
    grad_wv = left_dot(norm_attn, value_projected_gradient)
    grad_wo = left_dot(mixed_b, branch_grad)
    grad_wr = left_dot(norm_ffn, logit_grad)
    shared = (
        lax.psum_scatter(
            grad_wq.astype(jnp.bfloat16), "fs", scatter_dimension=0, tiled=True
        ).astype(jnp.float32),
        lax.psum_scatter(
            grad_wk.astype(jnp.bfloat16), "fs", scatter_dimension=0, tiled=True
        ).astype(jnp.float32),
        lax.psum_scatter(
            grad_wv.astype(jnp.bfloat16), "fs", scatter_dimension=0, tiled=True
        ).astype(jnp.float32),
        lax.psum_scatter(
            grad_wo.astype(jnp.bfloat16), "fs", scatter_dimension=0, tiled=True
        ).astype(jnp.float32),
        lax.psum_scatter(
            grad_wr.astype(jnp.bfloat16), "fs", scatter_dimension=0, tiled=True
        ).astype(jnp.float32),
        lax.psum_scatter(
            grad_gain_one.astype(jnp.bfloat16), "fs", scatter_dimension=0, tiled=True
        ).astype(jnp.float32),
        lax.psum_scatter(
            grad_gain_two.astype(jnp.bfloat16), "fs", scatter_dimension=0, tiled=True
        ).astype(jnp.float32),
        lax.psum_scatter(
            grad_bq.astype(jnp.bfloat16), "fs", scatter_dimension=0, tiled=True
        ).astype(jnp.float32),
        lax.psum_scatter(
            grad_bk.astype(jnp.bfloat16), "fs", scatter_dimension=0, tiled=True
        ).astype(jnp.float32),
        lax.psum_scatter(
            grad_bv.astype(jnp.bfloat16), "fs", scatter_dimension=0, tiled=True
        ).astype(jnp.float32),
        lax.psum_scatter(
            grad_bo.astype(jnp.bfloat16), "fs", scatter_dimension=0, tiled=True
        ).astype(jnp.float32),
        lax.psum_scatter(
            sink_grad.reshape(QUERY_HEADS).astype(jnp.bfloat16),
            "fs",
            scatter_dimension=0,
            tiled=True,
        ).astype(jnp.float32),
        lax.psum_scatter(
            grad_br.astype(jnp.bfloat16), "fs", scatter_dimension=0, tiled=True
        ).astype(jnp.float32),
    )
    totals = (
        lax.psum(shared[0].astype(jnp.bfloat16), "ep").astype(jnp.float32),
        lax.psum(shared[1].astype(jnp.bfloat16), "ep").astype(jnp.float32),
        lax.psum(shared[2].astype(jnp.bfloat16), "ep").astype(jnp.float32),
        lax.psum(shared[3].astype(jnp.bfloat16), "ep").astype(jnp.float32),
        lax.psum(shared[4].astype(jnp.bfloat16), "ep").astype(jnp.float32),
        lax.psum(shared[5].astype(jnp.bfloat16), "ep").astype(jnp.float32),
        lax.psum(shared[6].astype(jnp.bfloat16), "ep").astype(jnp.float32),
        lax.psum(shared[7].astype(jnp.bfloat16), "ep").astype(jnp.float32),
        lax.psum(shared[8].astype(jnp.bfloat16), "ep").astype(jnp.float32),
        lax.psum(shared[9].astype(jnp.bfloat16), "ep").astype(jnp.float32),
        lax.psum(shared[10].astype(jnp.bfloat16), "ep").astype(jnp.float32),
        lax.psum(shared[11].astype(jnp.bfloat16), "ep").astype(jnp.float32),
        lax.psum(shared[12].astype(jnp.bfloat16), "ep").astype(jnp.float32),
    )
    (
        sum_wq,
        sum_wk,
        sum_wv,
        sum_wo,
        sum_wr,
        sum_gain_one,
        sum_gain_two,
        sum_bq,
        sum_bk,
        sum_bv,
        sum_bo,
        sum_sink,
        sum_br,
    ) = totals
    return (
        block_out.astype(jnp.bfloat16),
        grad_tokens,
        sum_gain_one,
        sum_wq,
        sum_bq,
        sum_wk,
        sum_bk,
        sum_wv,
        sum_bv,
        sum_sink,
        sum_wo,
        sum_bo,
        sum_gain_two,
        sum_wr,
        sum_br,
        grad_w_gate,
        grad_b_gate,
        grad_w_up,
        grad_b_up,
        grad_w_down,
        grad_b_down,
    )


def solution(mesh):
    in_specs = (
        P(("fs", "ep"), None),
        P(("fs", "ep"), None),
        P(("fs", "ep"), None),
        P("fs"),
        P("fs", None),
        P("fs"),
        P("fs", None),
        P("fs"),
        P("fs", None),
        P("fs"),
        P("fs"),
        P("fs", None),
        P("fs"),
        P("fs"),
        P("fs", None),
        P("fs"),
        P("ep", None, "fs"),
        P("ep", "fs"),
        P("ep", None, "fs"),
        P("ep", "fs"),
        P("ep", "fs", None),
        P("ep", None),
        P(("fs", "ep"), None),
    )
    out_specs = (
        P(("fs", "ep"), None),
        P(("fs", "ep"), None),
        P("fs"),
        P("fs", None),
        P("fs"),
        P("fs", None),
        P("fs"),
        P("fs", None),
        P("fs"),
        P("fs"),
        P("fs", None),
        P("fs"),
        P("fs"),
        P("fs", None),
        P("fs"),
        P("ep", None, "fs"),
        P("ep", "fs"),
        P("ep", None, "fs"),
        P("ep", "fs"),
        P("ep", "fs", None),
        P("ep", None),
    )
    return jax.shard_map(
        per_device, mesh=mesh, in_specs=in_specs, out_specs=out_specs, check_vma=False
    )
```

profile of v0, /device:TPU:0, one launch (start us, length us, event | category | flops | bytes accessed | tf_op | source)
XLA Modules:
  0.0 2454.0 jit_solution(5191802771669722181)
XLA Ops:
  14.3 18.1 all-reduce.18
  32.4 7.2 all_gather.51
  39.6 7.8 all-gather.1
  47.5 7.0 all-gather
  54.6 8.3 all-gather.2
  68.1 7.8 mul.471
  85.2 14.8 all-gather.10.cloned.1.call-done
  103.3 213.3 %all-gather.14.cloned.1.call-done = bf16[2880,4096]{1,0:T(8,128)(2,1)} async-done(((bf16[720,4096]{1,0:T(8,128)(2,1)}), bf16[2880,4096]{1,0:T(8,128)(2,1)}) %all-gather.14.cloned.1.call-update) | async-done | bytes 23592976 | tf_op jit(solution)/shard_map/all_gather | solution.py:162
  316.7 11.2 convolution_add_fusion
  336.9 196.3 %all-gather.16.cloned.1.call-done = bf16[4096,2880]{0,1:T(8,128)(2,1)} async-done(((bf16[1024,2880]{0,1:T(8,128)(2,1)}), bf16[4096,2880]{0,1:T(8,128)(2,1)}) %all-gather.16.cloned.1.call-update) | async-done | bytes 23592976 | tf_op jit(solution)/shard_map/all_gather | solution.py:165
  533.2 11.2 multiply_reduce_fusion.4
  552.8 11.5 gather_fusion.2
  569.5 5.5 broadcast_select_fusion
  575.1 105.6 %all_to_all.42 = bf16[8,96,2880]{2,1,0:T(8,128)(2,1)} all-to-all(bf16[8,96,2880]{2,1,0:T(8,128)(2,1)S(1)} %get-tuple-element.141), channel_id=1, replica_groups=mesh['fs'=4,'ep'=8] {'ep'}, dimensions={0} | all-to-all | bytes 8847360 | tf_op jit(solution)/shard_map/all_to_all | solution.py:298
  680.7 105.6 %all_to_all.43 = bf16[8,96,2880]{2,1,0:T(8,128)(2,1)} all-to-all(bf16[8,96,2880]{2,1,0:T(8,128)(2,1)} %get-tuple-element.142), channel_id=1, replica_groups=mesh['fs'=4,'ep'=8] {'ep'}, dimensions={0} | all-to-all | bytes 8847360 | tf_op jit(solution)/shard_map/all_to_all | solution.py:249
  787.0 61.1 %all-gather.20.cloned.1.call-done = bf16[3072,2880]{1,0:T(8,128)(2,1)} async-done(((bf16[768,2880]{1,0:T(8,128)(2,1)}), bf16[3072,2880]{1,0:T(8,128)(2,1)}) %all-gather.20.cloned.1.call-update) | async-done | bytes 17694736 | tf_op jit(solution)/shard_map/all_gather | solution.py:299
  848.2 22.1 fusion.3
  870.2 149.2 %all-gather.18.cloned.1.call-done = bf16[3072,2880]{1,0:T(8,128)(2,1)} async-done(((bf16[768,2880]{1,0:T(8,128)(2,1)}), bf16[3072,2880]{1,0:T(8,128)(2,1)}) %all-gather.18.cloned.1.call-update) | async-done | bytes 17694736 | tf_op jit(solution)/shard_map/all_gather | solution.py:251
  1019.4 22.1 fusion.5
  1041.5 32.8 %convert_reduce_fusion.1 = (f32[2,720]{1,0:T(2,128)}, bf16[32,2,48,720]{3,2,0,1:T(8,128)(2,1)}, f32[2,720]{1,0:T(2,128)}, bf16[32,2,48,720]{3,2,0,1:T(8,128)(2,1)}, bf16[32,2,48,720]{3,2,0,1:T(8,128)(2,1)}) fusion(f32[2,720]{1,0:T(2,128)S(1)} %convert_element_type.309, f32[2,32,48,720]{3,2,1,0:T(8,128)} %fusion.5, f32[2,720]{1,0:T(2,128)S(1)} %convert_element_type.310, ...), kind=kOutput, calls=%fused_computation.36 | convolution fusion | flops 12813187072 | bytes 56977920 | tf_op jit(solution)/shard_map/secd,edf->secf/dot_general | solution.py:259
  1074.3 21.7 convert_bitcast_fusion
  1095.9 16.1 copy.156
  1112.1 23.7 fusion.21
  1135.8 30.3 %fusion = bf16[32,2,48,2880]{3,2,0,1:T(8,128)(2,1)} fusion(f32[2,32,48,2880]{3,2,1,0:T(8,128)} %fusion.21, bf16[32,2,48,720]{3,2,0,1:T(8,128)(2,1)} %get-tuple-element.116, bf16[2,2880,720]{1,2,0:T(8,128)(2,1)} %param.41), kind=kOutput, calls=%fused_computation.9 | convolution fusion | flops 12757893120 | bytes 65802240 | tf_op jit(solution)/shard_map/secf,edf->secd/dot_general | solution.py:319
  1166.1 16.4 copy.163
  1183.2 93.4 %reduce-scatter.10.cloned.1.call-done = bf16[768,2880]{1,0:T(8,128)(2,1)} async-done(((bf16[3072,2880]{1,0:T(8,128)(2,1)}), bf16[768,2880]{1,0:T(8,128)(2,1)}) %reduce-scatter.10.cloned.1.call-update) | async-done | bytes 4423696 | tf_op jit(solution)/shard_map/reduce_scatter | solution.py:267
  1286.5 158.2 %reduce-scatter.12.cloned.1.call-done = bf16[768,2880]{1,0:T(8,128)(2,1)} async-done(((bf16[3072,2880]{1,0:T(8,128)(2,1)}), bf16[768,2880]{1,0:T(8,128)(2,1)}) %reduce-scatter.12.cloned.1.call-update) | async-done | bytes 4423696 | tf_op jit(solution)/shard_map/reduce_scatter | solution.py:320
  1449.5 10.0 gather_fusion.1
  1459.5 6.6 reshape.480
  1466.1 8.6 multiply_reduce_fusion
  1474.9 75.6 %all-to-all-done.3 = bf16[8,96,2880]{2,1,0:T(8,128)(2,1)} async-done(((bf16[8,96,2880]{2,1,0:T(8,128)(2,1)}), bf16[8,96,2880]{2,1,0:T(8,128)(2,1)}, u32[]{:S(2)}, u32[]{:S(2)}) %all-to-all-start.3) | async-done | bytes 4423712 | tf_op jit(solution)/shard_map/all_to_all | solution.py:326
  1550.5 8.7 gather_fusion.3
  1562.9 7.5 reduce_sum.282
  1581.2 11.2 convolution_convert_fusion.2
  1616.3 11.1 convolution_convert_fusion.1
  1628.6 11.2 convolution_convert_fusion
  1643.5 20.9 convolution_bitcast_fusion
  1664.5 21.1 fusion.26
  1686.8 7.8 convert_reduce_fusion
  1694.7 204.8 %reduce-scatter.20.cloned.1.call-done = bf16[720,4096]{1,0:T(8,128)(2,1)} async-done(((bf16[2880,4096]{1,0:T(8,128)(2,1)}), bf16[720,4096]{1,0:T(8,128)(2,1)}) %reduce-scatter.20.cloned.1.call-update) | async-done | bytes 5898256
  1899.4 212.4 %reduce-scatter.18.cloned.1.call-done = bf16[1024,2880]{0,1:T(8,128)(2,1)} async-done(((bf16[4096,2880]{0,1:T(8,128)(2,1)}), bf16[1024,2880]{0,1:T(8,128)(2,1)}) %reduce-scatter.18.cloned.1.call-update) | async-done | bytes 5898256 | tf_op jit(solution)/shard_map/reduce_scatter | solution.py:404
  2111.9 21.0 convolution_bitcast_fusion.1
  2133.6 11.2 fusion.91
  2149.0 15.3 all-reduce.17
  2168.9 28.4 %all-reduce.15 = (bf16[720]{0:T(1024)(128)(2,1)S(1)}, bf16[1024]{0:T(1024)(128)(2,1)S(1)}, bf16[128]{0:T(256)(128)(2,1)S(1)}, bf16[128]{0:T(256)(128)(2,1)S(1)},...) all-reduce(bf16[720]{0:T(1024)(128)(2,1)S(1)} %dynamic-slice.7, ...), channel_id=1, replica_groups=mesh['fs'=4,'ep'=8] {'ep'}, use_global_device_ids=true, to_apply=%region_26.27 | all-reduce | flops 14980 | bytes 59920 | tf_op jit(solution)/shard_map/psum | solution.py:444
  2202.3 227.4 %all-reduce.24.cloned.1.call-done = (bf16[720,4096]{1,0:T(8,128)(2,1)}, bf16[720,512]{1,0:T(8,128)(2,1)}, bf16[720,512]{1,0:T(8,128)(2,1)}, bf16[1024,2880]{0,1:T(8,128)(2,1)}) async-done(((bf16[720,4096]{1,0:T(8,128)(2,1)}, bf16[720,512]{1,0:T(8,128)(2,1)}, bf16[720,512]{1,0:T(8,128)(2,1)}, bf16[1024,2880]{0,1:T(8,128)(2,1)}), (bf16[720,4096]{1,0:T(8,128)(2,1)}, bf16[720,512]{1,0:T(8,128)(2,1)}, ...) | async-done | bytes 13271056 | tf_op jit(solution)/shard_map/psum | solution.py:439
  2429.7 9.0 convert_element_type.345
  2438.7 5.9 convert_element_type.357
  (364 shorter events, 119.6 us)
Async XLA Ops:
  7.2 74.8 %all-gather.12.cloned.1.call-start = ((), (), s32[]{:S(2)}) async-start(), calls=%async_computation.11 | async-start | bytes 3686400 | tf_op jit(solution)/shard_map/all_gather | solution.py:163
  7.9 92.1 %all-gather.10.cloned.1.call-start = ((), (), s32[]{:S(2)}) async-start(), calls=%async_computation.10 | async-start | bytes 3686400 | tf_op jit(solution)/shard_map/all_gather | solution.py:164
  8.7 308.0 %all-gather.14.cloned.1.call-start = ((), (), s32[]{:S(2)}) async-start(), calls=%async_computation.12 | async-start | bytes 29491200 | tf_op jit(solution)/shard_map/all_gather | solution.py:162
  9.5 22.9 copy-start.86
  9.5 30.1 %copy-start.93 = (bf16[128]{0:T(256)(128)(2,1)S(1)}, bf16[128]{0:T(256)(128)(2,1)}, u32[]{:S(2)}) copy-start(bf16[128]{0:T(256)(128)(2,1)} %param.30) | copy-start | bytes 772
  9.5 38.0 %copy-start.94 = (bf16[128]{0:T(256)(128)(2,1)S(1)}, bf16[128]{0:T(256)(128)(2,1)}, u32[]{:S(2)}) copy-start(bf16[128]{0:T(256)(128)(2,1)} %param.32) | copy-start | bytes 772
  9.5 45.0 %copy-start.70 = (bf16[720,16]{0,1:T(8,128)(2,1)S(1)}, bf16[720,16]{0,1:T(8,128)(2,1)}, u32[]{:S(2)}) copy-start(bf16[720,16]{0,1:T(8,128)(2,1)} %param.37) | copy-start | bytes 69124
  9.5 53.5 %copy-start.21 = (bf16[128,2880]{0,1:T(8,128)(2,1)S(1)}, bf16[128,2880]{0,1:T(8,128)(2,1)}, u32[]{:S(2)}) copy-start(bf16[128,2880]{0,1:T(8,128)(2,1)} %param.45) | copy-start | bytes 2211844
  9.5 523.6 %all-gather.16.cloned.1.call-start = ((), (), s32[]{:S(2)}) async-start(), calls=%async_computation.13 | async-start | bytes 29491200 | tf_op jit(solution)/shard_map/all_gather | solution.py:165
  10.1 838.0 %all-gather.20.cloned.1.call-start = ((), (), s32[]{:S(2)}) async-start(), calls=%async_computation.16 | async-start | bytes 22609920 | tf_op jit(solution)/shard_map/all_gather | solution.py:299
  32.4 284.2 %copy-start.23 = (f32[2880]{0:T(1024)}, f32[2880]{0:T(1024)S(1)}, u32[]{:S(2)}) copy-start(f32[2880]{0:T(1024)S(1)} %convert_element_type.291) | copy-start | bytes 34564
  47.5 286.8 %copy-start.61 = (f32[8,8]{1,0:T(8,128)}, f32[8,8]{1,0:T(8,128)S(1)}, u32[]{:S(2)}) copy-start(f32[8,8]{1,0:T(8,128)S(1)} %reshape.479) | copy-start | bytes 772
  54.5 490.4 %copy-start.56 = (f32[2880]{0:T(1024)}, f32[2880]{0:T(1024)S(1)}, u32[]{:S(2)}) copy-start(f32[2880]{0:T(1024)S(1)} %convert_element_type.304) | copy-start | bytes 34564
  63.0 483.2 %copy-start.32 = (bf16[2880,16]{0,1:T(8,128)(2,1)}, bf16[2880,16]{0,1:T(8,128)(2,1)S(1)}, u32[]{:S(2)}) copy-start(bf16[2880,16]{0,1:T(8,128)(2,1)S(1)} %reshape.544) | copy-start | bytes 276484
  68.1 12.7 copy-start
  81.7 234.9 %copy-start.65 = (f32[128]{0:T(128)}, f32[128]{0:T(128)S(1)}, u32[]{:S(2)}) copy-start(f32[128]{0:T(128)S(1)} %get-tuple-element.148) | copy-start | bytes 1540
  82.0 248.0 %copy-start.46 = (f32[128,32]{0,1:T(8,128)}, f32[128,32]{0,1:T(8,128)S(1)}, u32[]{:S(2)}) copy-start(f32[128,32]{0,1:T(8,128)S(1)} %get-tuple-element.143) | copy-start | bytes 49156
  82.0 248.0 %copy-start.48 = (f32[128,32]{0,1:T(8,128)}, f32[128,32]{0,1:T(8,128)S(1)}, u32[]{:S(2)}) copy-start(f32[128,32]{0,1:T(8,128)S(1)} %get-tuple-element.144) | copy-start | bytes 49156
  103.2 231.9 %copy-start.40 = (bf16[128,512]{0,1:T(8,128)(2,1)}, bf16[128,512]{0,1:T(8,128)(2,1)S(1)}, u32[]{:S(2)}) copy-start(bf16[128,512]{0,1:T(8,128)(2,1)S(1)} %copy.143) | copy-start | bytes 393220
  103.3 229.0 %copy-start.52 = (bf16[128,8,32]{0,2,1:T(8,128)(2,1)}, bf16[128,8,32]{0,2,1:T(8,128)(2,1)S(1)}, u32[]{:S(2)}) copy-start(bf16[128,8,32]{0,2,1:T(8,128)(2,1)S(1)} %get-tuple-element.137) | copy-start | bytes 196612
  103.3 229.0 %copy-start.54 = (bf16[128,8,32]{0,2,1:T(8,128)(2,1)}, bf16[128,8,32]{0,2,1:T(8,128)(2,1)S(1)}, u32[]{:S(2)}) copy-start(bf16[128,8,32]{0,2,1:T(8,128)(2,1)S(1)} %get-tuple-element.138) | copy-start | bytes 196612
  336.9 207.5 %copy-start.26 = (bf16[8,64,8,128]{3,1,2,0:T(8,128)(2,1)}, bf16[8,64,8,128]{3,1,2,0:T(8,128)(2,1)S(1)}, u32[]{:S(2)}) copy-start(bf16[8,64,8,128]{3,1,2,0:T(8,128)(2,1)S(1)} %fusion.41) | copy-start | bytes 3145732
  680.7 338.7 %all-gather.18.cloned.1.call-start = ((), (), s32[]{:S(2)}) async-start(), calls=%async_computation.14 | async-start | bytes 22609920 | tf_op jit(solution)/shard_map/all_gather | solution.py:251
  786.4 490.3 %reduce-scatter.10.cloned.1.call-start = ((), (), s32[]{:S(2)}) async-start(), calls=%async_computation.15 | async-start | bytes 22609920 | tf_op jit(solution)/shard_map/reduce_scatter | solution.py:267
  1112.0 332.6 %reduce-scatter.12.cloned.1.call-start = ((), (), s32[]{:S(2)}) async-start(), calls=%async_computation.17 | async-start | bytes 22609920 | tf_op jit(solution)/shard_map/reduce_scatter | solution.py:320
  1281.9 162.8 %all-to-all-start.1 = ((bf16[8,96,2880]{2,1,0:T(8,128)(2,1)}), bf16[8,96,2880]{2,1,0:T(8,128)(2,1)}, u32[]{:S(2)}, u32[]{:S(2)}) async-start(bf16[8,96,2880]{2,1,0:T(8,128)(2,1)} %bitcast.241), calls=%async_computation.2 | async-start | bytes 9043968 | tf_op jit(solution)/shard_map/all_to_all | solution.py:283
  1444.7 105.9 %all-to-all-start.3 = ((bf16[8,96,2880]{2,1,0:T(8,128)(2,1)}), bf16[8,96,2880]{2,1,0:T(8,128)(2,1)}, u32[]{:S(2)}, u32[]{:S(2)}) async-start(bf16[8,96,2880]{2,1,0:T(8,128)(2,1)} %bitcast.248), calls=%async_computation.5 | async-start | bytes 9043968 | tf_op jit(solution)/shard_map/all_to_all | solution.py:326
  1449.4 245.3 %reduce-scatter.16.cloned.1.call-start = ((), (), s32[]{:S(2)}) async-start(), calls=%async_computation.19 | async-start | bytes 3686400 | tf_op jit(solution)/shard_map/reduce_scatter | solution.py:401
  1474.9 100.2 %copy-start.63 = (bf16[128,16]{0,1:T(8,128)(2,1)}, bf16[128,16]{0,1:T(8,128)(2,1)S(1)}, u32[]{:S(2)}) copy-start(bf16[128,16]{0,1:T(8,128)(2,1)S(1)} %select_reduce_fusion) | copy-start | bytes 12292
  1581.2 46.3 %copy-start.5 = (f32[128,2880]{0,1:T(8,128)}, f32[128,2880]{0,1:T(8,128)S(1)}, u32[]{:S(2)}) copy-start(f32[128,2880]{0,1:T(8,128)S(1)} %get-tuple-element.120) | copy-start | bytes 4423684
  1581.2 12.9 copy-start.34
  1601.0 93.6 %reduce-scatter.14.cloned.1.call-start = ((), (), s32[]{:S(2)}) async-start(), calls=%async_computation.18 | async-start | bytes 3686400 | tf_op jit(solution)/shard_map/reduce_scatter | solution.py:398
  1611.7 287.8 %reduce-scatter.20.cloned.1.call-start = ((), (), s32[]{:S(2)}) async-start(), calls=%async_computation.22 | async-start | bytes 29491200
  1627.4 484.4 %reduce-scatter.18.cloned.1.call-start = ((), (), s32[]{:S(2)}) async-start(), calls=%async_computation.20 | async-start | bytes 29491200 | tf_op jit(solution)/shard_map/reduce_scatter | solution.py:404
  1639.9 528.2 %all-reduce.22.cloned.1.call-start = ((), (), s32[]{:S(2)}) async-start(), calls=%async_computation.21 | async-start | bytes 188416
  1664.5 21.1 copy-start.14
  1664.5 21.1 copy-start.64
  1686.6 743.1 %all-reduce.24.cloned.1.call-start = ((), (), s32[]{:S(2)}) async-start(), calls=%async_computation.23 | async-start | bytes 26542080 | tf_op jit(solution)/shard_map/psum | solution.py:439
  2111.8 21.1 copy-start.35
  2111.9 21.1 copy-start.51
  2111.9 21.1 copy-start.62
  2111.9 21.3 copy-start.76
  2111.9 21.4 copy-start.77
  2111.9 21.5 copy-start.60
  2111.9 21.7 copy-start.20
  2133.6 11.2 copy-start.7
  2146.9 18.0 copy-start.6
  2146.9 18.0 copy-start.91
  (66 other events, 264.8 us)
Sparse Core Ops, SparseCore 0:
  9.9 45.8 all-gather.11
  57.6 42.4 all-gather.9
  101.9 214.7 all-gather.13
  318.4 214.7 all-gather.15
  680.8 167.3 all-gather.19
  849.9 169.4 all-gather.17
  1112.2 164.4 reduce-scatter.9
  1280.2 164.4 reduce-scatter.11
  1601.2 40.2 reduce-scatter.15
  1644.9 42.2 reduce-scatter.13
  1690.4 209.0 reduce-scatter.19
  1902.7 209.0 reduce-scatter.17
  2114.7 41.7 all-reduce.21
  2159.2 270.4 all-reduce.23
where the time goes:
time: 2460 us; the launch traced here: 2450 us
  waiting for transfers between devices  1610 us (65%)
  matrix products  315 us (13%)
  blocking collectives  303 us (12%)
  local copies, waits for them, and re-layouts  117 us (5%)
  other arithmetic  79 us (3%)
    psum x1, waiting for transfers between devices, per_device(): lax.psum(shared[0].astype(jnp.bfloat16), 'ep').astype(jnp.float32)  227 us
    all_gather x1, waiting for transfers between devices, per_device(): lax.all_gather(w_query, 'fs', axis=0, tiled=True)  213 us
    reduce_scatter x1, waiting for transfers between devices, per_device(): lax.psum_scatter(grad_wo.astype(jnp.bfloat16), 'fs', scatter_dimension=0,...  212 us
    unnamed x16, waiting for transfers between devices  208 us
    all_gather x1, waiting for transfers between devices, per_device(): lax.all_gather(w_out, 'fs', axis=0, tiled=True)  196 us
    reduce_scatter x1, waiting for transfers between devices, per_device(): lax.psum_scatter(term.reshape(lax.axis_size('fs') * per_fs, w_gate.shape[...  158 us
    all_gather x1, waiting for transfers between devices, per_device(): every_row = lax.all_gather(arrived, 'fs', axis=0, tiled=True)  149 us
    all_to_all x1, blocking collectives, per_device(): lax.all_to_all(send_rows, 'ep', split_axis=0, concat_axis=0, tiled=True)  106 us
  transfers between devices with their start and end apart: 16, of which 11 were waited for; matrix products, arithmetic and copies ran while one was open for 12% of the time, Pallas kernels for 0%

commit v1 on v0

v1 whole, which is shorter than its diff:
```python
from functools import partial

import jax
import jax.numpy as jnp
from jax import lax
from jax.experimental import pallas as pl
from jax.experimental.pallas import tpu as pltpu
from jax.sharding import PartitionSpec as P

QUERY_HEADS = 64
KEY_VALUE_HEADS = 8
HEAD_SIZE = 64
TOP = 4
EXP_DEV = 2


EPSILON = 1e-05
ROPE_BASE = 150000.0
SWIGLU_ALPHA = 1.702
CLAMP_LIMIT = 7.0
MASKED_SCORE = -1e30


F32 = jnp.float32
BF = jnp.bfloat16
MESH = pl.DeviceIdType.MESH


def layout(lengths, card_rows):
    seq_ends = jnp.cumsum(lengths)
    places = jnp.arange(card_rows, dtype=jnp.int32)
    past_end = (places[:, None] >= seq_ends[None, :]).astype(jnp.int32)
    segment_ids = jnp.sum(past_end, axis=1)
    position = places - jnp.sum(past_end * lengths[None, :], axis=1)
    return (segment_ids, position)


def tables(position, half_dim):
    inv_freq = jnp.exp(-jnp.log(ROPE_BASE) * jnp.arange(half_dim, dtype=jnp.float32) / half_dim)
    angles = position.astype(jnp.float32)[:, None] * inv_freq[None, :]
    return (jnp.cos(angles)[:, None, :], jnp.sin(angles)[:, None, :])


def apply_rotation(value_matrix, cosine_table, sine_table):
    half_dim = value_matrix.shape[-1] // 2
    lower_half = value_matrix[..., :half_dim]
    upper_half = value_matrix[..., half_dim:]
    return jnp.concatenate(
        [
            lower_half * cosine_table - upper_half * sine_table,
            upper_half * cosine_table + lower_half * sine_table,
        ],
        axis=-1,
    )


def undo_rotation(value_matrix, cosine_table, sine_table):
    half_dim = value_matrix.shape[-1] // 2
    lower_half = value_matrix[..., :half_dim]
    upper_half = value_matrix[..., half_dim:]
    return jnp.concatenate(
        [
            lower_half * cosine_table + upper_half * sine_table,
            upper_half * cosine_table - lower_half * sine_table,
        ],
        axis=-1,
    )


def norm_scale(value_matrix):
    return lax.rsqrt(jnp.mean(value_matrix * value_matrix, axis=-1, keepdims=True) + EPSILON)


def norm_back(value_matrix, inv_scale, gain, grad_norm):
    weighted = grad_norm * gain
    grad_values = inv_scale * weighted - value_matrix * inv_scale**3 * jnp.mean(
        weighted * value_matrix, axis=-1, keepdims=True
    )
    grad_gain = jnp.sum(grad_norm * value_matrix * inv_scale, axis=0)
    return (grad_values, grad_gain)


def left_dot(left, right):
    return jnp.dot(left.T, right, preferred_element_type=jnp.float32)


def mm(spec, left, right):
    return jnp.einsum(spec, left, right, preferred_element_type=jnp.float32)


def gather_all(value):
    return lax.all_gather(value, ("fs", "ep"), axis=0, tiled=True)


def scatter_all(value):
    return lax.psum_scatter(value, ("fs", "ep"), scatter_dimension=0, tiled=True)


def gather_fs(value):
    return lax.all_gather(value, "fs", axis=0, tiled=True)


def scatter_fs(value):
    return lax.psum_scatter(value, "fs", scatter_dimension=0, tiled=True)


def spot():
    fs=lax.axis_index("fs"); ep=lax.axis_index("ep")
    return fs, ep, fs//2, fs%2, ep//2, ep%2

def greet(fs, ep, z, more=0):
    y, x, c = fs//2, fs%2, ep%2
    bar=pltpu.get_barrier_semaphore()
    def hi(f,e): pl.semaphore_signal(bar,inc=1,device_id=(f,e),device_id_type=MESH)
    hi(fs+1-2*x,ep); hi(fs+2-4*y,ep); hi(fs,ep+1-2*c)
    if more: hi(3-fs,ep)
    @pl.when(z>0)
    def _(): hi(fs,ep-2)
    @pl.when(z<3)
    def _(): hi(fs,ep+2)
    @pl.when((z>0)&(z<3))
    def _(): pl.semaphore_wait(bar,5+more)
    @pl.when((z==0)|(z==3))
    def _(): pl.semaphore_wait(bar,4+more)

def scatter_kernel(na, parts, *refs):
    ps=refs[:na]; out=refs[na]; far=refs[na+1]
    q,v1,v2,vu,vd,stg,load,s0,r0,gsem,s1,r1,s2,r2,su,ru,sd,rd,osem = refs[na+2:]
    fs,ep,y,x,z,c = spot()
    rows=ps[0].shape[2]; pr=rows//parts; half=pr//2
    items=na*4*parts
    xn=(fs+1-2*x,ep); yn=(fs+2-4*y,ep); cn=(fs,ep+1-2*c)
    A=pl.ds(0,half); B=pl.ds(half,half)
    def rem(src,dst,s,r,dev): return pltpu.make_async_remote_copy(src,dst,s,r,device_id=dev,device_id_type=MESH)
    def where(i):
        a=i//(4*parts); j=i%(4*parts); k=j//parts; part=j%parts
        zz=(k%2)*(k//2)+(1-k%2)*(3-k//2)
        return a,part,zz
    def block(i,par):
        a,part,zz=where(i)
        return a,zz*2+par,pl.ds(part*pr,pr)
    def on_array(i,f):
        if na==1: f(ps[0])
        else:
            a=i//(4*parts)
            for n in range(na):
                @pl.when(a==n)
                def _(): f(ps[n])
    def give(i,p):
        _,e,r=block(i,1-c)
        return rem(p.at[:,e,r],far.at[i],s0.at[i],r0.at[i],cn)
    def mine(i,p):
        _,e,r=block(i,c)
        return pltpu.make_async_copy(p.at[:,e,r],q.at[i],load.at[i])
    def fetch(i):
        return pltpu.make_async_copy(far.at[i],stg.at[i%2],gsem.at[i%2])
    def one(i):
        return ([rem(q.at[i,2*j+1-x,A],v1.at[i,0,j],s1.at[i,j],r1.at[i,j],xn) for j in range(2)],
                rem(q.at[i,pl.ds((1-y)*2,2),B],v1.at[i,1],s1.at[i,2],r1.at[i,2],yn))
    def two(i):
        return (rem(q.at[i,(1-y)*2+x,A],v2.at[i,0],s2.at[i,0],r2.at[i,0],yn),
                rem(q.at[i,y*2+1-x,B],v2.at[i,1],s2.at[i,1],r2.at[i,1],xn))
    def up(i): return rem(q.at[i,fs],vu.at[i],su.at[i],ru.at[i],(fs,ep+2))
    def down(i): return rem(q.at[i,fs],vd.at[i],sd.at[i],rd.at[i],(fs,ep-2))
    greet(fs,ep,z)
    @pl.loop(0,items)
    def _(i):
        on_array(i,lambda p: give(i,p).start())
        on_array(i,lambda p: mine(i,p).start())
    def valid(i): return (i>=0)&(i<items)
    def add(dst,src,n):
        for lo in range(0,n,16):
            s=pl.ds(lo,16)
            dst(s,src(s))
    def getfar(i):
        on_array(i,lambda p: give(i,p).wait_recv())
        fetch(i).start()
    getfar(0)
    @pl.loop(0,items+6)
    def _(t):
        @pl.when(t<items)
        def _():
            i=t
            @pl.when(i+1<items)
            def _(): getfar(i+1)
            fetch(i).wait()
            on_array(i,lambda p: mine(i,p).wait())
            for g in range(4):
                q[i,g]=q[i,g]+stg[i%2,g]
            a,b=one(i)
            for k in a: k.start()
            b.start()
        i=t-1
        @pl.when(valid(i))
        def _():
            a,b=one(i)
            for k in a: k.wait_recv()
            for j in range(2):
                q[i,2*j+x,A]=q[i,2*j+x,A]+v1[i,0,j]
            ta,tb=two(i)
            ta.start()
            b.wait_recv()
            for j in range(2):
                q[i,2*y+j,B]=q[i,2*y+j,B]+v1[i,1,j]
            tb.start()
        i2=t-2
        @pl.when(valid(i2))
        def _():
            ta,tb=two(i2)
            ta.wait_recv()
            q[i2,fs,A]=q[i2,fs,A]+v2[i2,0]
            tb.wait_recv()
            q[i2,fs,B]=q[i2,fs,B]+v2[i2,1]
        iu=t-2-z
        @pl.when(valid(iu))
        def _():
            _,_,zz=where(iu)
            @pl.when(zz>=z)
            def _():
                @pl.when(z>0)
                def _():
                    up(iu).wait_recv()
                    q[iu,fs]=q[iu,fs]+vu[iu]
                @pl.when(zz>z)
                def _(): up(iu).start()
        idn=t-2-(3-z)
        @pl.when(valid(idn))
        def _():
            _,_,zz=where(idn)
            @pl.when(zz<=z)
            def _():
                @pl.when(z<3)
                def _():
                    down(idn).wait_recv()
                    q[idn,fs]=q[idn,fs]+vd[idn]
                @pl.when(zz<z)
                def _(): down(idn).start()
    @pl.loop(0,items)
    def _(i):
        a,part,zz=where(i)
        @pl.when(zz==z)
        def _():
            pltpu.make_async_copy(q.at[i,fs],out.at[a,pl.ds(part*pr,pr)],osem.at[i]).start()
    @pl.loop(0,items)
    def _(i):
        a,part,zz=where(i)
        on_array(i,lambda p: give(i,p).wait_send())
        a1,b1=one(i)
        for k in a1: k.wait_send()
        b1.wait_send()
        ta,tb=two(i); ta.wait_send(); tb.wait_send()
        @pl.when(zz>z)
        def _(): up(i).wait_send()
        @pl.when(zz<z)
        def _(): down(i).wait_send()
        @pl.when(zz==z)
        def _(): pltpu.make_async_copy(q.at[i,fs],out.at[a,pl.ds(part*pr,pr)],osem.at[i]).wait()

def scatter_blocks(arrays, cid, parts=2):
    na=len(arrays); rows,width=arrays[0].shape[-2:]
    arrays=[a.reshape(4,8,rows,width) for a in arrays]
    pr=rows//parts; items=na*4*parts; half=pr//2
    any_=pl.BlockSpec(memory_space=pl.ANY)
    D=pltpu.SemaphoreType.DMA
    V=lambda *s: pltpu.VMEM(s+(width,),BF)
    out,_=pl.pallas_call(partial(scatter_kernel,na,parts),
        out_shape=[jax.ShapeDtypeStruct((na,rows,width),BF),jax.ShapeDtypeStruct((items,4,pr,width),BF)],
        in_specs=[any_]*na,out_specs=[any_,any_],
        scratch_shapes=[V(items,4,pr),V(items,2,2,half),V(items,2,half),V(items,pr),V(items,pr),V(2,4,pr),
            D((items,)),D((items,)),D((items,)),D((2,)),D((items,3)),D((items,3)),D((items,2)),D((items,2)),
            D((items,)),D((items,)),D((items,)),D((items,)),D((items,))],
        compiler_params=pltpu.CompilerParams(collective_id=cid,has_side_effects=True,vmem_limit_bytes=63*1024*1024),
        name="scatter_blocks")(*arrays)
    return out


def reduce_kernel(
    wide_n, slab_n, gw, gq, tw, tq,
    own_w, own_q, all_q, far_w, far_q, pin_w, pin_q, pout_w, pout_q, din_w, din_q, dout_w, dout_q, tot_w, tot_q,
    wload, qload, s0w, r0w, s0q, r0q, sa, ra, su, ru, sd, rd, keep, sc, rc,
):
    fs, ep, y, x, z, c = spot()
    mate = (fs, ep + 1 - 2 * c)
    rows_w, rows_q = own_w.shape[1], own_q.shape[1]
    parts = slab_n // 4
    items = wide_n + slab_n

    def rem(src, dst, s, r, dev):
        return pltpu.make_async_remote_copy(src, dst, s, r, device_id=dev, device_id_type=MESH)

    def source(s):
        return ((y + s // 2) % 2) * 2 + (x + s) % 2

    def give_w(i):
        return rem(gw.at[1 - c, i], far_w.at[i], s0w.at[i], r0w.at[i], mate)

    def give_q(s):
        return rem(gq.at[source(s), 1 - c], far_q.at[s], s0q.at[s], r0q.at[s], mate)

    def load_w(i):
        return pltpu.make_async_copy(gw.at[c, i], own_w.at[i], wload.at[i])

    def load_q(s):
        return pltpu.make_async_copy(gq.at[source(s), c], all_q.at[s], qload.at[s])

    def pass_q(s):
        dev = (source(s), ep)
        return rem(all_q.at[s], own_q.at[pl.ds(s * parts, parts)], sa.at[s], ra.at[s], dev)

    def on_item(i, f):
        @pl.when(i < wide_n)
        def _():
            f(own_w, pin_w, pout_w, din_w, dout_w, tot_w, i)

        @pl.when(i >= wide_n)
        def _():
            f(own_q, pin_q, pout_q, din_q, dout_q, tot_q, i - wide_n)

    def valid(i):
        return (i >= 0) & (i < items)

    def back(i, f):
        @pl.when(i < wide_n)
        def _():
            dst = tw.at[c, i]
            f(pltpu.make_async_copy(tot_w.at[i], dst, keep.at[i]), rem(tot_w.at[i], dst, sc.at[i], rc.at[i], mate))

        @pl.when(i >= wide_n)
        def _():
            j = i - wide_n
            dst = tq.at[source(j // parts), c, j % parts]
            f(pltpu.make_async_copy(tot_q.at[j], dst, keep.at[i]), rem(tot_q.at[j], dst, sc.at[i], rc.at[i], mate))

    greet(fs, ep, z, 1)

    @pl.loop(0, wide_n)
    def _(i):
        give_w(i).start()
        load_w(i).start()

    for s in (1, 2, 3, 0):
        give_q(s).start()
        load_q(s).start()

    @pl.loop(0, items + 4)
    def _(t):
        @pl.when(t < wide_n)
        def _():
            load_w(t).wait()
            give_w(t).wait_recv()
            own_w[t] = own_w[t] + far_w[t]

        for n, s in enumerate((1, 2, 3, 0)):

            @pl.when(t == n)
            def _():
                load_q(s).wait()
                give_q(s).wait_recv()

                @pl.loop(0, parts)
                def _(j):
                    if s:
                        all_q[s, j] = all_q[s, j] + far_q[s, j]
                    else:
                        own_q[j] = all_q[0, j] + far_q[0, j]

                if s:
                    pass_q(s).start()

        for s in (1, 2, 3):

            @pl.when(t == wide_n + s * parts)
            def _():
                pass_q(s).wait_recv()

        iu = t - z

        @pl.when(valid(iu))
        def _():
            def go(own, pin, pout, din, dout, tot, i):
                @pl.when(z == 0)
                def _():
                    rem(own.at[i], pin.at[i], su.at[iu], ru.at[iu], (fs, ep + 2)).start()

                @pl.when(z > 0)
                def _():
                    rem(own.at[i], pin.at[i], su.at[iu], ru.at[iu], (fs, ep - 2)).wait_recv()

                @pl.when((z > 0) & (z < 3))
                def _():
                    pout[i] = pin[i] + own[i]
                    rem(pout.at[i], pin.at[i], su.at[iu], ru.at[iu], (fs, ep + 2)).start()

            on_item(iu, go)

        idn = t - 3 + z

        @pl.when(valid(idn))
        def _():
            def go(own, pin, pout, din, dout, tot, i):
                @pl.when(z == 3)
                def _():
                    rem(own.at[i], din.at[i], sd.at[idn], rd.at[idn], (fs, ep - 2)).start()

                @pl.when(z < 3)
                def _():
                    rem(own.at[i], din.at[i], sd.at[idn], rd.at[idn], (fs, ep + 2)).wait_recv()

                @pl.when((z > 0) & (z < 3))
                def _():
                    dout[i] = din[i] + own[i]
                    rem(dout.at[i], din.at[i], sd.at[idn], rd.at[idn], (fs, ep - 2)).start()

            on_item(idn, go)

        last = t - 3

        @pl.when(valid(last))
        def _():
            def go(own, pin, pout, din, dout, tot, i):
                @pl.when(z == 0)
                def _():
                    tot[i] = own[i] + din[i]

                @pl.when(z == 3)
                def _():
                    tot[i] = own[i] + pin[i]

                @pl.when((z == 1) | (z == 2))
                def _():
                    tot[i] = own[i] + pin[i] + din[i]

            on_item(last, go)

            def start(a, b):
                a.start()
                b.start()

            back(last, start)

    @pl.loop(0, items)
    def _(i):
        def finish(a, b):
            a.wait()
            b.wait()

        back(i, finish)

        def go(own, pin, pout, din, dout, tot, j):
            @pl.when(z < 3)
            def _():
                rem(own.at[j], pin.at[j], su.at[i], ru.at[i], (fs, ep + 2)).wait_send()

            @pl.when(z > 0)
            def _():
                rem(own.at[j], din.at[j], sd.at[i], rd.at[i], (fs, ep - 2)).wait_send()

        on_item(i, go)

    @pl.loop(0, wide_n)
    def _(i):
        give_w(i).wait_send()

    for s in range(4):
        give_q(s).wait_send()
        if s:
            pass_q(s).wait_send()


def reduce_parts(gw, gq, cid):
    wide_n = gw.shape[1]
    parts = gq.shape[2]
    slab_n = 4 * parts
    free = pl.BlockSpec(memory_space=pl.ANY)
    D = pltpu.SemaphoreType.DMA
    W = pltpu.VMEM((wide_n,) + gw.shape[2:], BF)
    Q = pltpu.VMEM((slab_n,) + gq.shape[3:], BF)
    Q4 = pltpu.VMEM((4, parts) + gq.shape[3:], BF)
    items = wide_n + slab_n
    return pl.pallas_call(
        partial(reduce_kernel, wide_n, slab_n),
        out_shape=[jax.ShapeDtypeStruct(gw.shape, BF), jax.ShapeDtypeStruct(gq.shape, BF)],
        in_specs=[free, free],
        out_specs=[free, free],
        scratch_shapes=[W, Q, Q4, W, Q4] + [W, Q] * 5
        + [D((wide_n,)), D((4,)), D((wide_n,)), D((wide_n,)), D((4,)), D((4,)), D((4,)), D((4,))]
        + [D((items,))] * 7,
        compiler_params=pltpu.CompilerParams(
            collective_id=cid, has_side_effects=True, vmem_limit_bytes=63 * 1024 * 1024
        ),
        name="reduce_parts",
    )(gw, gq)


def nn(left, right):
    return lax.dot_general(left, right, (((1,), (0,)), ((), ())), preferred_element_type=F32)


def nt(left, right):
    return lax.dot_general(left, right, (((1,), (1,)), ((), ())), preferred_element_type=F32)


def tn(left, right):
    return lax.dot_general(left, right, (((0,), (0,)), ((), ())), preferred_element_type=F32)


def strips(total, size):
    return [(at, min(size, total - at)) for at in range(0, total, size)]


def remote(src, dst, send, recv, device):
    return pltpu.make_async_remote_copy(
        src, dst, send, recv, device_id=device, device_id_type=MESH
    )


def line_order(z, i):
    code = jnp.where(z == 0, 228, jnp.where(z == 1, 225, jnp.where(z == 2, 54, 27)))
    power = jnp.where(i == 0, 1, jnp.where(i == 1, 4, jnp.where(i == 2, 16, 64)))
    return (code // power) % 4


class Gather:
    def __init__(self, full, sems):
        self.full = full
        self.sz, self.rz, self.s1, self.r1, self.s2, self.r2, self.sc, self.rc = sems
        self.fs, self.ep, self.y, self.x, self.z, self.c = spot()
        half = full.shape[3] // 2
        self.upper, self.lower = pl.ds(0, half), pl.ds(half, half)
        self.xn = (self.fs + 1 - 2 * self.x, self.ep)
        self.yn = (self.fs + 2 - 4 * self.y, self.ep)
        self.mate = (self.fs, self.ep + 1 - 2 * self.c)

    def item(self, t):
        return t // 4, line_order(self.z, t % 4)

    def along(self, a, zz, up):
        view = self.full.at[a, self.fs, zz * 2 + self.c]
        other = (self.fs, self.ep + (2 if up else -2))
        return remote(view, view, self.sz.at[a, zz, up], self.rz.at[a, zz], other)

    def first(self, a, zz):
        e = zz * 2 + self.c
        v = self.full.at[a, self.fs, e, self.upper]
        w = self.full.at[a, self.fs, e, self.lower]
        return (
            remote(v, v, self.s1.at[a, zz, 0], self.r1.at[a, zz, 0], self.xn),
            remote(w, w, self.s1.at[a, zz, 1], self.r1.at[a, zz, 1], self.yn),
        )

    def second(self, a, zz):
        e = zz * 2 + self.c
        v = self.full.at[a, pl.ds(self.y * 2, 2), e, self.upper]
        out = [remote(v, v, self.s2.at[a, zz, 0], self.r2.at[a, zz, 0], self.yn)]
        for j in range(2):
            w = self.full.at[a, 2 * j + self.x, e, self.lower]
            out.append(remote(w, w, self.s2.at[a, zz, 1 + j], self.r2.at[a, zz, 1 + j], self.xn))
        return out

    def across(self, a, zz, e):
        v = self.full.at[a, :, zz * 2 + e]
        return remote(v, v, self.sc.at[a, zz], self.rc.at[a, zz], self.mate)

    def step1(self, t):
        @pl.when(t < 8)
        def _():
            a, zz = self.item(t)

            @pl.when(zz != self.z)
            def _():
                self.along(a, zz, 0).wait_recv()

            @pl.when((zz <= self.z) & (self.z < 3))
            def _():
                self.along(a, zz, 1).start()

            @pl.when((zz >= self.z) & (self.z > 0))
            def _():
                self.along(a, zz, 0).start()

            for copy in self.first(a, zz):
                copy.start()

    def step2(self, t):
        @pl.when(t < 8)
        def _():
            a, zz = self.item(t)
            one, two = self.first(a, zz)
            copies = self.second(a, zz)
            one.wait_recv()
            copies[0].start()
            two.wait_recv()
            copies[1].start()
            copies[2].start()

    def step3(self, t):
        @pl.when(t < 8)
        def _():
            a, zz = self.item(t)
            for copy in self.second(a, zz):
                copy.wait_recv()
            self.across(a, zz, self.c).start()

    def step4(self, t):
        a, zz = self.item(t)
        self.across(a, zz, 1 - self.c).wait_recv()

    def finish(self):
        @pl.loop(0, 8)
        def _(t):
            a, zz = self.item(t)
            self.across(a, zz, self.c).wait_send()
            for copy in (*self.first(a, zz), *self.second(a, zz)):
                copy.wait_send()

            @pl.when((zz <= self.z) & (self.z < 3))
            def _():
                self.along(a, zz, 1).wait_send()

            @pl.when((zz >= self.z) & (self.z > 0))
            def _():
                self.along(a, zz, 0).wait_send()


def experts_kernel(
    cap, width,
    n_own, g_own, wg_hbm, wu_hbm, wd_hbm, bg_ref, bu_ref, bd_ref,
    full, out_hbm, row_hbm, xs_hbm, eg_hbm, mid_hbm, ug_hbm, gg_hbm, cu_hbm, cg_hbm,
    sum_g, sum_u, sum_d,
    wg_ref, wu_ref, wd_ref, bin_, meta, pmat, gates, xs, res, mid, ugb, ggb, cub, cgb, dots, stage,
    w_sem, own_sem, in_sem, st_sem, save_sem,
    *sems,
):
    gather = Gather(full, sems)
    fs, ep, z = gather.fs, gather.ep, gather.z
    card_rows, wpad = bin_.shape[1:]
    tail = wpad - 128
    off = width - tail
    first = jnp.where(fs == 0, 1.0, 0.0).astype(F32)
    nb = 8
    rows = nb * cap
    weights = [
        pltpu.make_async_copy(src, dst, w_sem.at[n])
        for n, (src, dst) in enumerate(((wg_hbm, wg_ref), (wu_hbm, wu_ref), (wd_hbm, wd_ref)))
    ]
    keep = [
        pltpu.make_async_copy(src, full.at[a, fs, ep], own_sem.at[a])
        for a, src in enumerate((n_own, g_own))
    ]
    for copy in keep + weights:
        copy.start()
    greet(fs, ep, z)
    for copy in keep:
        copy.wait()
    gather.step1(0)
    gather.step2(0)
    gather.step1(1)
    gather.step3(0)
    gather.step2(1)
    gather.step1(2)
    for copy in weights:
        copy.wait()

    def load(a, zz, b, slot):
        return pltpu.make_async_copy(full.at[a, b // 2, zz * 2 + b % 2], bin_.at[slot], in_sem.at[slot])

    def save(src, dst, k, i, n):
        return pltpu.make_async_copy(
            src.at[k], dst.at[k, pl.ds(pl.multiple_of(i * rows, 16), rows)], save_sem.at[n, k]
        )

    def fetch(src, dst, k, i, n):
        return pltpu.make_async_copy(
            src.at[k, pl.ds(pl.multiple_of(i * rows, 16), rows)], dst.at[k], save_sem.at[n, k]
        )

    def spread(a, i, zz, prepare):
        load(a, zz, 0, 0).start()

        @pl.loop(0, nb)
        def _(b):
            slot = lax.rem(b, 2)

            @pl.when(b + 1 < nb)
            def _():
                load(a, zz, b + 1, 1 - slot).start()

            load(a, zz, b, slot).wait()
            at = pl.ds(pl.multiple_of(b * cap, 16), cap)
            if prepare:
                meta[...] = jnp.transpose(bin_[slot, :, tail:].astype(F32))
                for k in range(2):
                    e = ep * 2 + k
                    place = meta[pl.ds(off + e, 1), :]
                    gate = meta[pl.ds(off + 16 + e, 1), :] + meta[pl.ds(off + 32 + e, 1), :]
                    hit = lax.broadcasted_iota(jnp.int32, (cap, card_rows), 0).astype(F32) == place
                    pmat[i, b, k * cap : (k + 1) * cap, :] = jnp.where(hit, 1.0, 0.0).astype(BF)
                    gates[i, k, at, :] = jnp.sum(jnp.where(hit, gate, 0.0), axis=1, keepdims=True)
            pick = pmat[i, b]
            for lo, n in strips(width, 768):
                got = nn(pick, bin_[slot, :, lo : lo + n]).astype(BF)
                xs[0, at, lo : lo + n] = got[:cap]
                xs[1, at, lo : lo + n] = got[cap:]

    def combine(dst, i, zz, with_dots):
        column = lax.broadcasted_iota(jnp.int32, (cap, wpad - width), 1)

        def store(b, slot):
            return pltpu.make_async_copy(
                stage.at[slot], dst.at[b // 2, zz * 2 + b % 2], st_sem.at[slot]
            )

        @pl.loop(0, nb)
        def _(b):
            slot = lax.rem(b, 2)

            @pl.when(b >= 2)
            def _():
                store(b - 2, slot).wait()

            pick = pmat[i, b]
            at = pl.ds(pl.multiple_of(b * cap, 16), cap)
            for lo, n in strips(width, 768):
                both = jnp.concatenate([res[0, at, lo : lo + n], res[1, at, lo : lo + n]], axis=0)
                stage[slot, :, lo : lo + n] = tn(pick, both).astype(BF)
            if with_dots:
                own_dots = jnp.concatenate(
                    [
                        jnp.where(column == ep * 2 + k, dots[k, at, :], 0.0).astype(BF)
                        for k in range(2)
                    ],
                    axis=0,
                )
                stage[slot, :, width:] = tn(pick, own_dots).astype(BF)
            else:
                stage[slot, :, width:] = jnp.zeros((card_rows, wpad - width), BF)
            store(b, slot).start()

        for b in (nb - 2, nb - 1):
            store(b, b % 2).wait()

    @pl.loop(0, 4)
    def _(i):
        zz = line_order(z, i)
        gather.step4(i)
        gather.step1(i + 3)
        spread(0, i, zz, True)
        for k in range(2):
            save(xs, xs_hbm, k, i, 0).start()
        gather.step2(i + 2)

        @pl.loop(0, 2)
        def _(k):
            @pl.when(k == 1)
            def _():
                gather.step3(i + 1)

            gate_soft = CLAMP_LIMIT * jnp.tanh((nt(xs[k], wg_ref[k]) + bg_ref[k]) * (1.0 / CLAMP_LIMIT))
            up_soft = CLAMP_LIMIT * jnp.tanh((nt(xs[k], wu_ref[k]) + bu_ref[k]) * (1.0 / CLAMP_LIMIT))
            sig = jax.nn.sigmoid(SWIGLU_ALPHA * gate_soft)
            glu = gate_soft * sig
            mid[k] = ((up_soft + 1.0) * glu).astype(BF)
            cub[k] = (glu * (1.0 - (up_soft * (1.0 / CLAMP_LIMIT)) ** 2)).astype(BF)
            cgb[k] = (
                (up_soft + 1.0)
                * (sig + SWIGLU_ALPHA * glu * (1.0 - sig))
                * (1.0 - (gate_soft * (1.0 / CLAMP_LIMIT)) ** 2)
            ).astype(BF)
            save(mid, mid_hbm, k, i, 1).start()
            save(cub, cu_hbm, k, i, 2).start()
            save(cgb, cg_hbm, k, i, 3).start()
            for lo, n in strips(width, 768):
                part = nn(mid[k], wd_ref[k, :, lo : lo + n]) + first * bd_ref[k, :, lo : lo + n]
                res[k, :, lo : lo + n] = (part * gates[i, k]).astype(BF)

        combine(out_hbm, i, zz, False)
        for k in range(2):
            save(xs, xs_hbm, k, i, 0).wait()
            save(mid, mid_hbm, k, i, 1).wait()
            save(cub, cu_hbm, k, i, 2).wait()
            save(cgb, cg_hbm, k, i, 3).wait()

    sum_g[...] = jnp.zeros_like(sum_g)
    sum_u[...] = jnp.zeros_like(sum_u)
    sum_d[...] = jnp.zeros_like(sum_d)

    @pl.loop(0, 4)
    def _(i):
        zz = line_order(z, i)
        for k in range(2):
            fetch(mid_hbm, mid, k, i, 1).start()
            fetch(cu_hbm, cub, k, i, 2).start()
            fetch(cg_hbm, cgb, k, i, 3).start()
        gather.step4(i + 4)
        gather.step1(i + 7)
        spread(1, i, zz, False)
        gather.step2(i + 6)
        ones = jnp.ones((8, rows), BF)

        @pl.loop(0, 2)
        def _(k):
            @pl.when(k == 1)
            def _():
                gather.step3(i + 5)

            fetch(mid_hbm, mid, k, i, 1).wait()
            fetch(cu_hbm, cub, k, i, 2).wait()
            fetch(cg_hbm, cgb, k, i, 3).wait()
            plain = nt(xs[k], wd_ref[k])
            gate = gates[i, k]
            grad = plain * gate
            dots[k] = jnp.sum(plain * mid[k].astype(F32), axis=1, keepdims=True) + first * jnp.sum(
                xs[k].astype(F32) * bd_ref[k], axis=1, keepdims=True
            )
            ugb[k] = (grad * cub[k].astype(F32)).astype(BF)
            ggb[k] = (grad * cgb[k].astype(F32)).astype(BF)
            xs[k] = (xs[k].astype(F32) * gate).astype(BF)
            save(xs, eg_hbm, k, i, 0).start()
            save(ugb, ug_hbm, k, i, 4).start()
            save(ggb, gg_hbm, k, i, 5).start()
            sum_g[k] += nn(ones, ggb[k])
            sum_u[k] += nn(ones, ugb[k])
            sum_d[k] += nn(ones, xs[k])
            for lo, n in strips(width, 768):
                part = nn(ggb[k], wg_ref[k, :, lo : lo + n]) + nn(ugb[k], wu_ref[k, :, lo : lo + n])
                res[k, :, lo : lo + n] = part.astype(BF)

        combine(row_hbm, i, zz, True)
        for k in range(2):
            save(xs, eg_hbm, k, i, 0).wait()
            save(ugb, ug_hbm, k, i, 4).wait()
            save(ggb, gg_hbm, k, i, 5).wait()

    gather.finish()


def experts(n_own, g_own, wg_t, b_gate, wu_t, b_up, w_down, b_down, cap, cid):
    rows, wpad = n_own.shape
    ff, width = w_down.shape[1:]
    n, m = 32 * cap, 8 * cap
    free = pl.BlockSpec(memory_space=pl.ANY)
    near = pl.BlockSpec(memory_space=pltpu.VMEM)
    shape = jax.ShapeDtypeStruct
    V = pltpu.VMEM
    D = pltpu.SemaphoreType.DMA
    biases = [b.astype(F32)[:, None] for b in (b_gate, b_up, b_down)]
    out = pl.pallas_call(
        partial(experts_kernel, cap, width),
        out_shape=[shape((2, 4, 8, rows, wpad), BF)]
        + [shape((4, 8, rows, wpad), BF)] * 2
        + [shape((2, n, width), BF)] * 2
        + [shape((2, n, ff), BF)] * 5
        + [shape((2, 8, ff), F32)] * 2
        + [shape((2, 8, width), F32)],
        in_specs=[free] * 5 + [near] * 3,
        out_specs=[free] * 10 + [near] * 3,
        scratch_shapes=[
            V((2, ff, width), BF), V((2, ff, width), BF), V((2, ff, width), BF),
            V((2, rows, wpad), BF), V((128, rows), F32), V((4, 8, 2 * cap, rows), BF),
            V((4, 2, m, 1), F32), V((2, m, width), BF), V((2, m, width), BF),
            V((2, m, ff), BF), V((2, m, ff), BF), V((2, m, ff), BF), V((2, m, ff), BF), V((2, m, ff), BF),
            V((2, m, 1), F32), V((2, rows, wpad), BF),
            D((3,)), D((2,)), D((2,)), D((2,)), D((6, 2)),
            D((2, 4, 2)), D((2, 4)), D((2, 4, 2)), D((2, 4, 2)), D((2, 4, 3)), D((2, 4, 3)), D((2, 4)), D((2, 4)),
        ],
        compiler_params=pltpu.CompilerParams(
            collective_id=cid, has_side_effects=True, vmem_limit_bytes=63 * 1024 * 1024
        ),
        cost_estimate=pl.CostEstimate(
            flops=24 * n * width * ff, bytes_accessed=300_000_000, transcendentals=6 * n * ff
        ),
        name="experts",
    )(n_own, g_own, wg_t, wu_t, w_down, *biases)
    return (*out[1:8], *(total[:, 0] for total in out[10:]))


def this_slice(
    tokens,
    seq_lengths,
    routes,
    attn_gain,
    w_query,
    b_query,
    w_key,
    b_key,
    w_value,
    b_value,
    sinks,
    w_out,
    b_out,
    ffn_gain,
    w_router,
    b_router,
    w_gate,
    b_gate,
    w_up,
    b_up,
    w_down,
    b_down,
    cotangent,
):
    rows, width = tokens.shape
    fs_size = lax.axis_size("fs")
    ep_size = lax.axis_size("ep")
    my_fs = lax.axis_index("fs")
    my_ep = lax.axis_index("ep")
    blocks = fs_size * ep_size
    expert_count = EXP_DEV * ep_size
    capacity = 3 * rows * TOP // (2 * expert_count)
    shard = w_query.shape[0]
    kv_heads = KEY_VALUE_HEADS // fs_size
    group = QUERY_HEADS // KEY_VALUE_HEADS
    q_cols = kv_heads * group * HEAD_SIZE
    kv_cols = kv_heads * HEAD_SIZE

    spare = (-width) % 128
    small = jnp.concatenate(
        [attn_gain, ffn_gain, b_out, w_router.reshape(-1), b_router, seq_lengths[0].astype(BF)]
    )
    extra = -(-small.shape[0] // (16 * width)) * 16
    small = jnp.pad(small, (0, extra * width - small.shape[0])).reshape(extra, width)
    packed = lax.all_gather(jnp.concatenate([tokens, small], axis=0), "fs", axis=0)
    x_group = packed[:, :rows].reshape(fs_size * rows, width).astype(F32)
    small = packed[:, rows:].reshape(fs_size, -1)
    gain_one = small[:, :shard].reshape(-1).astype(F32)
    gain_two = small[:, shard : 2 * shard].reshape(-1).astype(F32)
    bo = small[:, 2 * shard : 3 * shard].reshape(-1).astype(F32)
    at = (3 + expert_count) * shard
    wr = small[:, 3 * shard : at].reshape(width, expert_count)
    br = small[:, at : at + b_router.shape[0]].reshape(-1).astype(F32)
    at += b_router.shape[0]
    lengths = small[:, at : at + seq_lengths.shape[1]].astype(jnp.int32)

    w_qkv = jnp.concatenate(
        [
            w_query.reshape(shard, fs_size, q_cols),
            w_key.reshape(shard, fs_size, kv_cols),
            w_value.reshape(shard, fs_size, kv_cols),
        ],
        axis=2,
    )
    w_qkv = lax.all_to_all(w_qkv, "fs", split_axis=1, concat_axis=0, tiled=True)
    w_qkv = w_qkv.reshape(width, q_cols + 2 * kv_cols)
    b_qkv = jnp.concatenate([b_query, b_key, b_value]).astype(jnp.float32)
    sink_score = sinks.astype(jnp.float32).reshape(1, kv_heads, group, 1)

    x_float = tokens.astype(jnp.float32)
    scale_one = norm_scale(x_float)
    norm_attn = (x_group * norm_scale(x_group) * gain_one).astype(jnp.bfloat16)
    segment_ids, position = jax.vmap(lambda own: layout(own, rows))(lengths)
    cosine_table, sine_table = tables(position.reshape(-1), HEAD_SIZE // 2)
    qkv = jnp.dot(norm_attn, w_qkv, preferred_element_type=jnp.float32) + b_qkv
    many = fs_size * rows
    heads = kv_heads * group
    query = apply_rotation(
        qkv[:, :q_cols].reshape(many, heads, HEAD_SIZE), cosine_table, sine_table
    ).astype(jnp.bfloat16)
    query = query.reshape(fs_size, rows, kv_heads, group, HEAD_SIZE)
    key = apply_rotation(
        qkv[:, q_cols : q_cols + kv_cols].reshape(many, kv_heads, HEAD_SIZE),
        cosine_table,
        sine_table,
    ).astype(jnp.bfloat16)
    key = key.reshape(fs_size, rows, kv_heads, HEAD_SIZE)
    value = qkv[:, q_cols + kv_cols :].astype(jnp.bfloat16)
    value = value.reshape(fs_size, rows, kv_heads, HEAD_SIZE)
    places = jnp.arange(rows, dtype=jnp.int32)
    allowed = (segment_ids[:, :, None] == segment_ids[:, None, :]) & (
        places[:, None] >= places[None, :]
    )
    scores = mm("bqhgd,bkhd->bhgqk", query, key) * HEAD_SIZE ** (-0.5)
    masked = jnp.where(allowed[:, None, None], scores, MASKED_SCORE)
    top_score = jnp.maximum(jnp.max(masked, axis=-1), sink_score)
    exponent = jnp.exp(masked - top_score[..., None])
    sink_exp = jnp.exp(sink_score - top_score)
    denominator = jnp.sum(exponent, axis=-1) + sink_exp
    probs = exponent / denominator[..., None]
    sink_prob = sink_exp / denominator
    probs_b = probs.astype(jnp.bfloat16)
    mixed = mm("bhgqk,bkhd->bqhgd", probs_b, value).astype(jnp.bfloat16)
    mixed = mixed.reshape(many, q_cols)
    out_part = jnp.dot(mixed, w_out, preferred_element_type=jnp.float32)
    resid = x_float + scatter_fs(out_part.astype(jnp.bfloat16)).astype(jnp.float32) + bo
    scale_two = norm_scale(resid)
    norm_ffn = (resid * scale_two * gain_two).astype(jnp.bfloat16)

    logits = jnp.dot(norm_ffn, wr, preferred_element_type=F32) + br
    one_hot = (routes[:, :, None] == jnp.arange(expert_count, dtype=jnp.int32)).astype(F32)
    member = jnp.sum(one_hot, axis=1)
    peak = jnp.max(jnp.where(member > 0, logits, MASKED_SCORE), axis=-1, keepdims=True)
    gate_exp = jnp.where(member > 0, jnp.exp(logits - peak), 0.0)
    gates_here = gate_exp / jnp.sum(gate_exp, axis=-1, keepdims=True)
    place = jnp.where(member > 0, jnp.cumsum(member, axis=0) - member, -1.0)
    gate_high = lax.reduce_precision(gates_here, 8, 7)
    block = jnp.concatenate(
        [norm_ffn]
        + [v.astype(BF) for v in (place, gate_high, gates_here - gate_high)]
        + [jnp.zeros((rows, spare - 3 * expert_count), BF)],
        axis=1,
    )
    wg_t = jnp.swapaxes(w_gate, 1, 2)
    wu_t = jnp.swapaxes(w_up, 1, 2)
    (
        out_part,
        row_part,
        x_slots,
        expert_grad,
        middle,
        up_grad,
        gate_grad_pre,
        grad_b_gate,
        grad_b_up,
        grad_b_down,
    ) = experts(
        block,
        jnp.pad(cotangent, ((0, 0), (0, spare))),
        wg_t,
        b_gate,
        wu_t,
        b_up,
        w_down,
        b_down,
        capacity,
        1,
    )
    sums = scatter_blocks([out_part, row_part], 2)
    block_out = resid + sums[0, :, :width].astype(F32)
    grad_w_down = mm("erf,erd->efd", middle, expert_grad)
    grad_w_gate = jnp.swapaxes(mm("erf,erd->efd", gate_grad_pre, x_slots), 1, 2)
    grad_w_up = jnp.swapaxes(mm("erf,erd->efd", up_grad, x_slots), 1, 2)
    row_sum = sums[1].astype(F32)
    gate_grad = row_sum[:, width : width + expert_count]
    logit_grad = gates_here * (
        gate_grad - jnp.sum(gates_here * gate_grad, axis=-1, keepdims=True)
    )
    logit_grad = logit_grad.astype(jnp.bfloat16)
    grad_br = jnp.sum(logit_grad, axis=0, dtype=jnp.float32)
    grad_wr = left_dot(norm_ffn, logit_grad)
    norm_ffn_grad = row_sum[:, :width] + jnp.dot(
        logit_grad, wr.T, preferred_element_type=jnp.float32
    )
    resid_norm_grad, grad_gain_two = norm_back(resid, scale_two, gain_two, norm_ffn_grad)
    resid_grad = cotangent.astype(jnp.float32) + resid_norm_grad

    branch_grad = gather_fs(resid_grad.astype(jnp.bfloat16))
    grad_bo = jnp.sum(branch_grad, axis=0, dtype=jnp.float32)
    mixed_grad = mm("td,fd->tf", branch_grad, w_out).astype(jnp.bfloat16)
    mixed_grad = mixed_grad.reshape(fs_size, rows, kv_heads, group, HEAD_SIZE)
    grad_wo = left_dot(mixed, branch_grad)
    grad_probs = mm("bqhgd,bkhd->bhgqk", mixed_grad, value)
    value_grad = mm("bhgqk,bqhgd->bkhd", probs_b, mixed_grad)
    row_delta = jnp.sum(probs * grad_probs, axis=-1)
    score_grad = (probs * (grad_probs - row_delta[..., None])).astype(jnp.bfloat16)
    query_grad = mm("bhgqk,bkhd->bqhgd", score_grad, key) * HEAD_SIZE ** (-0.5)
    key_grad = mm("bhgqk,bqhgd->bkhd", score_grad, query) * HEAD_SIZE ** (-0.5)
    grad_sink = -jnp.sum(sink_prob * row_delta, axis=(0, 3)).reshape(-1)
    query_pre_grad = undo_rotation(
        query_grad.reshape(many, heads, HEAD_SIZE), cosine_table, sine_table
    ).reshape(many, q_cols)
    key_pre_grad = undo_rotation(
        key_grad.reshape(many, kv_heads, HEAD_SIZE), cosine_table, sine_table
    ).reshape(many, kv_cols)
    qkv_grad = jnp.concatenate(
        [query_pre_grad, key_pre_grad, value_grad.reshape(many, kv_cols)], axis=1
    ).astype(jnp.bfloat16)
    grad_b_qkv = jnp.sum(qkv_grad, axis=0, dtype=jnp.float32)
    norm_attn_grad = scatter_fs(
        mm("tf,df->td", qkv_grad, w_qkv).astype(jnp.bfloat16)
    ).astype(jnp.float32)
    input_norm_grad, grad_gain_one = norm_back(x_float, scale_one, gain_one, norm_attn_grad)
    grad_tokens = resid_grad + input_norm_grad
    by_shard = jnp.concatenate(
        [
            grad_wr.reshape(fs_size, -1),
            grad_gain_one.reshape(fs_size, -1),
            grad_gain_two.reshape(fs_size, -1),
            grad_br.reshape(fs_size, -1),
        ],
        axis=1,
    ).astype(BF)
    own = jnp.concatenate(
        [grad_b_qkv, grad_sink, lax.dynamic_slice_in_dim(grad_bo, my_fs * shard, shard)]
    ).astype(BF)
    cols = q_cols + 2 * kv_cols
    slab_rows, slab_part = 768, 128
    wide_rows, wide_part = 1056, 48
    spare_q = (slab_rows - shard) * cols - by_shard.shape[1]
    gq = jnp.concatenate(
        [
            left_dot(norm_attn, qkv_grad).astype(BF).reshape(fs_size, shard, cols),
            jnp.pad(by_shard, ((0, 0), (0, spare_q))).reshape(fs_size, slab_rows - shard, cols),
        ],
        axis=1,
    ).reshape(fs_size, 2, slab_rows // (2 * slab_part), slab_part, cols)
    spare_w = (wide_rows - q_cols) * width - own.shape[0]
    gw = jnp.concatenate(
        [grad_wo.astype(BF), jnp.pad(own, (0, spare_w)).reshape(wide_rows - q_cols, width)], axis=0
    ).reshape(2, wide_rows // (2 * wide_part), wide_part, width)
    tw, tq = reduce_parts(gw, gq, 3)
    tw = tw.reshape(wide_rows, width)
    tq = tq.reshape(fs_size, slab_rows, cols)
    sum_wo = tw[:q_cols].astype(F32)
    own = tw[q_cols:].reshape(-1)[: own.shape[0]].astype(F32)
    sums_q = tq[:, :shard].astype(F32).transpose(1, 0, 2)
    sum_wq = sums_q[:, :, :q_cols].reshape(shard, -1)
    sum_wk = sums_q[:, :, q_cols : q_cols + kv_cols].reshape(shard, -1)
    sum_wv = sums_q[:, :, q_cols + kv_cols :].reshape(shard, -1)
    by_shard = jnp.sum(
        tq[:, shard:].reshape(fs_size, -1)[:, : by_shard.shape[1]].astype(F32), axis=0
    )
    sum_wr = by_shard[: shard * expert_count].reshape(shard, expert_count)
    rest = by_shard[shard * expert_count :]
    sum_b = own[:cols]
    return (
        block_out.astype(jnp.bfloat16),
        grad_tokens,
        rest[:shard],
        sum_wq,
        sum_b[:q_cols],
        sum_wk,
        sum_b[q_cols : q_cols + kv_cols],
        sum_wv,
        sum_b[q_cols + kv_cols :],
        own[q_cols + 2 * kv_cols : q_cols + 2 * kv_cols + heads],
        sum_wo,
        own[q_cols + 2 * kv_cols + heads :],
        rest[shard : 2 * shard],
        sum_wr,
        rest[2 * shard :],
        grad_w_gate,
        grad_b_gate,
        grad_w_up,
        grad_b_up,
        grad_w_down,
        grad_b_down,
    )


def any_slice(
    tokens,
    seq_lengths,
    routes,
    attn_gain,
    w_query,
    b_query,
    w_key,
    b_key,
    w_value,
    b_value,
    sinks,
    w_out,
    b_out,
    ffn_gain,
    w_router,
    b_router,
    w_gate,
    b_gate,
    w_up,
    b_up,
    w_down,
    b_down,
    cotangent,
):
    rows, width = tokens.shape
    fs_size = lax.axis_size("fs")
    ep_size = lax.axis_size("ep")
    my_fs = lax.axis_index("fs")
    my_ep = lax.axis_index("ep")
    blocks = fs_size * ep_size
    expert_count = EXP_DEV * ep_size
    capacity = 3 * rows * TOP // (2 * expert_count)
    shard = w_query.shape[0]
    kv_heads = KEY_VALUE_HEADS // fs_size
    group = QUERY_HEADS // KEY_VALUE_HEADS
    q_cols = kv_heads * group * HEAD_SIZE
    kv_cols = kv_heads * HEAD_SIZE

    packed = jnp.concatenate(
        [attn_gain, ffn_gain, b_out, w_router.reshape(-1), b_router]
    )
    packed = lax.all_gather(packed, "fs", axis=0)
    gain_one = packed[:, :shard].reshape(-1).astype(jnp.float32)
    gain_two = packed[:, shard : 2 * shard].reshape(-1).astype(jnp.float32)
    bo = packed[:, 2 * shard : 3 * shard].reshape(-1).astype(jnp.float32)
    wr = packed[:, 3 * shard : (3 + expert_count) * shard].reshape(width, expert_count)
    br = packed[:, (3 + expert_count) * shard :].reshape(-1).astype(jnp.float32)
    whole_numbers = gather_all(
        jnp.concatenate([routes.reshape(-1), seq_lengths.reshape(-1)])[None]
    )
    routes_all = whole_numbers[:, : rows * TOP].reshape(blocks, rows, TOP)
    lengths_all = whole_numbers[:, rows * TOP :]
    lengths = lax.dynamic_index_in_dim(
        lengths_all.reshape(fs_size, ep_size, -1), my_ep, 1, keepdims=False
    )
    g_all = gather_all(cotangent)

    w_qkv = jnp.concatenate(
        [
            w_query.reshape(shard, fs_size, q_cols),
            w_key.reshape(shard, fs_size, kv_cols),
            w_value.reshape(shard, fs_size, kv_cols),
        ],
        axis=2,
    )
    w_qkv = lax.all_to_all(w_qkv, "fs", split_axis=1, concat_axis=0, tiled=True)
    w_qkv = w_qkv.reshape(width, q_cols + 2 * kv_cols)
    b_qkv = jnp.concatenate([b_query, b_key, b_value]).astype(jnp.float32)
    sink_score = sinks.astype(jnp.float32).reshape(1, kv_heads, group, 1)

    x_float = tokens.astype(jnp.float32)
    scale_one = norm_scale(x_float)
    norm_attn = gather_fs((x_float * scale_one * gain_one).astype(jnp.bfloat16))
    segment_ids, position = jax.vmap(lambda own: layout(own, rows))(lengths)
    cosine_table, sine_table = tables(position.reshape(-1), HEAD_SIZE // 2)
    qkv = jnp.dot(norm_attn, w_qkv, preferred_element_type=jnp.float32) + b_qkv
    many = fs_size * rows
    heads = kv_heads * group
    query = apply_rotation(
        qkv[:, :q_cols].reshape(many, heads, HEAD_SIZE), cosine_table, sine_table
    ).astype(jnp.bfloat16)
    query = query.reshape(fs_size, rows, kv_heads, group, HEAD_SIZE)
    key = apply_rotation(
        qkv[:, q_cols : q_cols + kv_cols].reshape(many, kv_heads, HEAD_SIZE),
        cosine_table,
        sine_table,
    ).astype(jnp.bfloat16)
    key = key.reshape(fs_size, rows, kv_heads, HEAD_SIZE)
    value = qkv[:, q_cols + kv_cols :].astype(jnp.bfloat16)
    value = value.reshape(fs_size, rows, kv_heads, HEAD_SIZE)
    places = jnp.arange(rows, dtype=jnp.int32)
    allowed = (segment_ids[:, :, None] == segment_ids[:, None, :]) & (
        places[:, None] >= places[None, :]
    )
    scores = mm("bqhgd,bkhd->bhgqk", query, key) * HEAD_SIZE ** (-0.5)
    masked = jnp.where(allowed[:, None, None], scores, MASKED_SCORE)
    top_score = jnp.maximum(jnp.max(masked, axis=-1), sink_score)
    exponent = jnp.exp(masked - top_score[..., None])
    sink_exp = jnp.exp(sink_score - top_score)
    denominator = jnp.sum(exponent, axis=-1) + sink_exp
    probs = exponent / denominator[..., None]
    sink_prob = sink_exp / denominator
    probs_b = probs.astype(jnp.bfloat16)
    mixed = mm("bhgqk,bkhd->bqhgd", probs_b, value).astype(jnp.bfloat16)
    mixed = mixed.reshape(many, q_cols)
    out_part = jnp.dot(mixed, w_out, preferred_element_type=jnp.float32)
    resid = x_float + scatter_fs(out_part.astype(jnp.bfloat16)).astype(jnp.float32) + bo
    scale_two = norm_scale(resid)
    norm_ffn = (resid * scale_two * gain_two).astype(jnp.bfloat16)

    n_all = gather_all(norm_ffn)
    logits = jnp.dot(n_all, wr, preferred_element_type=jnp.float32) + br
    logits = logits.reshape(blocks, rows, expert_count)
    one_hot = (
        routes_all[:, :, :, None] == jnp.arange(expert_count, dtype=jnp.int32)
    ).astype(jnp.float32)
    member = jnp.sum(one_hot, axis=2)
    peak = jnp.max(jnp.where(member > 0, logits, MASKED_SCORE), axis=-1, keepdims=True)
    gate_exp = jnp.where(member > 0, jnp.exp(logits - peak), 0.0)
    gates = gate_exp / jnp.sum(gate_exp, axis=-1, keepdims=True)
    own_member = lax.dynamic_slice_in_dim(member, my_ep * EXP_DEV, EXP_DEV, axis=2)
    own_gates = lax.dynamic_slice_in_dim(gates, my_ep * EXP_DEV, EXP_DEV, axis=2)
    rank = jnp.cumsum(own_member, axis=1) - own_member
    slots = jnp.arange(capacity, dtype=jnp.float32)
    pick = (rank.transpose(0, 2, 1)[:, :, None, :] == slots[:, None]) & (
        own_member.transpose(0, 2, 1)[:, :, None, :] > 0
    )
    pick_b = pick.astype(jnp.bfloat16)
    slot_gate = jnp.sum(
        jnp.where(pick, own_gates.transpose(0, 2, 1)[:, :, None, :], 0.0), axis=-1
    )
    slot_gate = slot_gate.transpose(1, 0, 2).reshape(EXP_DEV, blocks * capacity, 1)

    def spread(full):
        parts = mm("bekt,btd->ebkd", pick_b, full.reshape(blocks, rows, -1))
        return parts.astype(jnp.bfloat16).reshape(EXP_DEV, blocks * capacity, -1)

    def combine(parts):
        parts = parts.reshape(EXP_DEV, blocks, capacity, -1)
        return mm("bekt,ebkd->btd", pick_b, parts).reshape(blocks * rows, -1)

    x_slots = spread(n_all)
    g_slots = spread(g_all)
    gate_pre = mm("erd,edf->erf", x_slots, w_gate) + b_gate.astype(jnp.float32)[:, None]
    up_pre = mm("erd,edf->erf", x_slots, w_up) + b_up.astype(jnp.float32)[:, None]
    gate_soft = CLAMP_LIMIT * jnp.tanh(gate_pre / CLAMP_LIMIT)
    up_soft = CLAMP_LIMIT * jnp.tanh(up_pre / CLAMP_LIMIT)
    gate_sig = jax.nn.sigmoid(SWIGLU_ALPHA * gate_soft)
    glu_part = gate_soft * gate_sig
    middle = ((up_soft + 1.0) * glu_part).astype(jnp.bfloat16)
    first = (my_fs == 0).astype(jnp.float32)
    down_bias = b_down.astype(jnp.float32) * first
    expert_out = mm("erf,efd->erd", middle, w_down) + down_bias[:, None]
    expert_sum = scatter_all(
        combine((expert_out * slot_gate).astype(jnp.bfloat16)).astype(jnp.bfloat16)
    )
    block_out = resid + expert_sum.astype(jnp.float32)

    expert_grad = (g_slots.astype(jnp.float32) * slot_gate).astype(jnp.bfloat16)
    plain_grad = mm("erd,efd->erf", g_slots, w_down)
    middle_grad = plain_grad * slot_gate
    gate_dot = jnp.sum(plain_grad * middle.astype(jnp.float32), axis=-1) + jnp.sum(
        g_slots.astype(jnp.float32) * down_bias[:, None], axis=-1
    )
    grad_w_down = mm("erf,erd->efd", middle, expert_grad)
    grad_b_down = jnp.sum(expert_grad, axis=1, dtype=jnp.float32)
    up_grad = (middle_grad * glu_part * (1.0 - (up_soft / CLAMP_LIMIT) ** 2)).astype(jnp.bfloat16)
    gate_grad_pre = (
        middle_grad
        * (up_soft + 1.0)
        * (gate_sig + SWIGLU_ALPHA * gate_soft * gate_sig * (1.0 - gate_sig))
        * (1.0 - (gate_soft / CLAMP_LIMIT) ** 2)
    ).astype(jnp.bfloat16)
    grad_w_gate = mm("erd,erf->edf", x_slots, gate_grad_pre)
    grad_b_gate = jnp.sum(gate_grad_pre, axis=1, dtype=jnp.float32)
    grad_w_up = mm("erd,erf->edf", x_slots, up_grad)
    grad_b_up = jnp.sum(up_grad, axis=1, dtype=jnp.float32)
    row_part = mm("erf,edf->erd", gate_grad_pre, w_gate) + mm("erf,edf->erd", up_grad, w_up)
    row_sum = combine(row_part.astype(jnp.bfloat16))
    own_dot = jnp.sum(
        jnp.where(pick, gate_dot.reshape(EXP_DEV, blocks, capacity).transpose(1, 0, 2)[..., None], 0.0),
        axis=2,
    )
    dots = jnp.sum(
        own_dot[..., None]
        * (
            (my_ep * EXP_DEV + jnp.arange(EXP_DEV))[:, None] == jnp.arange(expert_count)[None]
        ).astype(jnp.float32)[None, :, None, :],
        axis=1,
    ).reshape(blocks * rows, expert_count)
    row_sum = scatter_all(jnp.concatenate([row_sum, dots], axis=1).astype(jnp.bfloat16))
    row_sum = row_sum.astype(jnp.float32)
    gate_grad = row_sum[:, width:]
    mine = my_fs * ep_size + my_ep
    gates_here = lax.dynamic_index_in_dim(gates, mine, 0, keepdims=False)
    logit_grad = gates_here * (
        gate_grad - jnp.sum(gates_here * gate_grad, axis=-1, keepdims=True)
    )
    logit_grad = logit_grad.astype(jnp.bfloat16)
    grad_br = jnp.sum(logit_grad, axis=0, dtype=jnp.float32)
    grad_wr = left_dot(norm_ffn, logit_grad)
    norm_ffn_grad = row_sum[:, :width] + jnp.dot(
        logit_grad, wr.T, preferred_element_type=jnp.float32
    )
    resid_norm_grad, grad_gain_two = norm_back(resid, scale_two, gain_two, norm_ffn_grad)
    resid_grad = cotangent.astype(jnp.float32) + resid_norm_grad

    branch_grad = gather_fs(resid_grad.astype(jnp.bfloat16))
    grad_bo = jnp.sum(branch_grad, axis=0, dtype=jnp.float32)
    mixed_grad = mm("td,fd->tf", branch_grad, w_out).astype(jnp.bfloat16)
    mixed_grad = mixed_grad.reshape(fs_size, rows, kv_heads, group, HEAD_SIZE)
    grad_wo = left_dot(mixed, branch_grad)
    grad_probs = mm("bqhgd,bkhd->bhgqk", mixed_grad, value)
    value_grad = mm("bhgqk,bqhgd->bkhd", probs_b, mixed_grad)
    row_delta = jnp.sum(probs * grad_probs, axis=-1)
    score_grad = (probs * (grad_probs - row_delta[..., None])).astype(jnp.bfloat16)
    query_grad = mm("bhgqk,bkhd->bqhgd", score_grad, key) * HEAD_SIZE ** (-0.5)
    key_grad = mm("bhgqk,bqhgd->bkhd", score_grad, query) * HEAD_SIZE ** (-0.5)
    grad_sink = -jnp.sum(sink_prob * row_delta, axis=(0, 3)).reshape(-1)
    query_pre_grad = undo_rotation(
        query_grad.reshape(many, heads, HEAD_SIZE), cosine_table, sine_table
    ).reshape(many, q_cols)
    key_pre_grad = undo_rotation(
        key_grad.reshape(many, kv_heads, HEAD_SIZE), cosine_table, sine_table
    ).reshape(many, kv_cols)
    qkv_grad = jnp.concatenate(
        [query_pre_grad, key_pre_grad, value_grad.reshape(many, kv_cols)], axis=1
    ).astype(jnp.bfloat16)
    grad_b_qkv = jnp.sum(qkv_grad, axis=0, dtype=jnp.float32)
    norm_attn_grad = scatter_fs(
        mm("tf,df->td", qkv_grad, w_qkv).astype(jnp.bfloat16)
    ).astype(jnp.float32)
    input_norm_grad, grad_gain_one = norm_back(x_float, scale_one, gain_one, norm_attn_grad)
    grad_tokens = resid_grad + input_norm_grad
    grad_qkv = left_dot(norm_attn, qkv_grad).astype(jnp.bfloat16)
    if shard % ep_size == 0:
        grad_qkv = grad_qkv.reshape(fs_size, ep_size, shard // ep_size, q_cols + 2 * kv_cols)
        grad_qkv = lax.psum_scatter(grad_qkv, "ep", scatter_dimension=1, tiled=False)
        grad_qkv = lax.all_to_all(grad_qkv, "fs", split_axis=0, concat_axis=1, tiled=False)
        grad_qkv = lax.all_gather(grad_qkv, "ep", axis=0, tiled=True).astype(jnp.float32)
    else:
        grad_qkv = lax.psum(grad_qkv.reshape(fs_size, shard, q_cols + 2 * kv_cols), "ep")
        grad_qkv = lax.all_to_all(grad_qkv, "fs", split_axis=0, concat_axis=1, tiled=False)
        grad_qkv = grad_qkv.astype(jnp.float32)
    sum_wq = grad_qkv[:, :, :q_cols].reshape(shard, -1)
    sum_wk = grad_qkv[:, :, q_cols : q_cols + kv_cols].reshape(shard, -1)
    sum_wv = grad_qkv[:, :, q_cols + kv_cols :].reshape(shard, -1)
    sum_wo = lax.psum(grad_wo.astype(jnp.bfloat16), "ep").astype(jnp.float32)
    by_shard = jnp.concatenate(
        [
            grad_wr.reshape(fs_size, -1),
            grad_gain_one.reshape(fs_size, -1),
            grad_gain_two.reshape(fs_size, -1),
            grad_br.reshape(fs_size, -1),
        ],
        axis=1,
    )
    by_shard = lax.psum(by_shard, ("fs", "ep"))
    by_shard = lax.dynamic_index_in_dim(by_shard, my_fs, 0, keepdims=False)
    sum_wr = by_shard[: shard * expert_count].reshape(shard, expert_count)
    rest = by_shard[shard * expert_count :]
    own = jnp.concatenate(
        [
            grad_b_qkv,
            grad_sink,
            lax.dynamic_slice_in_dim(grad_bo, my_fs * shard, shard),
        ]
    )
    own = lax.psum(own, "ep")
    sum_b = own[: q_cols + 2 * kv_cols]
    return (
        block_out.astype(jnp.bfloat16),
        grad_tokens,
        rest[:shard],
        sum_wq,
        sum_b[:q_cols],
        sum_wk,
        sum_b[q_cols : q_cols + kv_cols],
        sum_wv,
        sum_b[q_cols + kv_cols :],
        own[q_cols + 2 * kv_cols : q_cols + 2 * kv_cols + heads],
        sum_wo,
        own[q_cols + 2 * kv_cols + heads :],
        rest[shard : 2 * shard],
        sum_wr,
        rest[2 * shard :],
        grad_w_gate,
        grad_b_gate,
        grad_w_up,
        grad_b_up,
        grad_w_down,
        grad_b_down,
    )


def solution(mesh):
    in_specs = (
        P(("fs", "ep"), None),
        P(("fs", "ep"), None),
        P(("fs", "ep"), None),
        P("fs"),
        P("fs", None),
        P("fs"),
        P("fs", None),
        P("fs"),
        P("fs", None),
        P("fs"),
        P("fs"),
        P("fs", None),
        P("fs"),
        P("fs"),
        P("fs", None),
        P("fs"),
        P("ep", None, "fs"),
        P("ep", "fs"),
        P("ep", None, "fs"),
        P("ep", "fs"),
        P("ep", "fs", None),
        P("ep", None),
        P(("fs", "ep"), None),
    )
    out_specs = (
        P(("fs", "ep"), None),
        P(("fs", "ep"), None),
        P("fs"),
        P("fs", None),
        P("fs"),
        P("fs", None),
        P("fs"),
        P("fs", None),
        P("fs"),
        P("fs"),
        P("fs", None),
        P("fs"),
        P("fs"),
        P("fs", None),
        P("fs"),
        P("ep", None, "fs"),
        P("ep", "fs"),
        P("ep", None, "fs"),
        P("ep", "fs"),
        P("ep", "fs", None),
        P("ep", None),
    )
    run = this_slice if (mesh.shape["fs"], mesh.shape["ep"]) == (4, 8) else any_slice
    return jax.shard_map(
        run, mesh=mesh, in_specs=in_specs, out_specs=out_specs, check_vma=False
    )
```

time: 2460 us -> 1220 us (0.50)
  waiting for transfers between devices: 1610 us -> 121 us
  Pallas kernels: 0 us -> 749 us
  blocking collectives: 303 us -> 0 us
  matrix products: 315 us -> 122 us
    pallas_call x0 -> x3, Pallas kernels: none -> 749 us  [the longest x1 341 us: experts(): pl.pallas_call(partial(experts_kernel, cap, width), out_shape=[shape((2,...]
    all_gather x6 -> x2, waiting for transfers between devices: 635 us -> 76.4 us  [the longest x1 76.4 us: this_slice(): lax.all_gather(jnp.concatenate([tokens, small], axis=0), 'fs', axis=0)]
    reduce_scatter x5 -> x2, waiting for transfers between devices: 464 us -> 31.7 us  [scatter_fs(): return lax.psum_scatter(value, 'fs', scatter_dimension=0, tiled=True)]
    psum x1 -> x0, waiting for transfers between devices: 227 us -> none  [per_device(): lax.psum(shared[0].astype(jnp.bfloat16), 'ep').astype(jnp.float32)]
    all_to_all x2 -> x0, blocking collectives: 211 us -> none  [the longest x1 106 us: per_device(): lax.all_to_all(send_rows, 'ep', split_axis=0, concat_axis=0, tiled=True)]
    unnamed x16 -> x4, waiting for transfers between devices: 208 us -> 0.07 us
    dot_general x25 -> x15, matrix products: 286 us -> 107 us  [the longest x11 91.1 us: mm(): return jnp.einsum(spec, left, right, preferred_element_type=jnp.float32)]
    all_to_all x2 -> x1, waiting for transfers between devices: 75.6 us -> 13.2 us  [this_slice(): w_qkv = lax.all_to_all(w_qkv, 'fs', split_axis=1, concat_axis=0, tiled=True)]
  transfers between devices with their start and end apart: 16 -> 5, of which waited for: 11 -> 3; matrix products, arithmetic and copies ran while one was open for 12% -> 12% of each run, Pallas kernels for 0% -> 0%
where the time goes in v1:
time: 1220 us; the launch traced here: 1210 us
  Pallas kernels  749 us (61%)
  local copies, waits for them, and re-layouts  131 us (11%)
  matrix products  122 us (10%)
  waiting for transfers between devices  121 us (10%)
  other arithmetic  67.7 us (6%)
  between operations  15.5 us (1%)
    pallas_call x1, Pallas kernels, experts(): pl.pallas_call(partial(experts_kernel, cap, width), out_shape=[shape((2,...  341 us
    pallas_call x1, Pallas kernels, scatter_blocks(): pl.pallas_call(partial(scatter_kernel, na, parts), out_shape=[jax.ShapeDt...  219 us
    pallas_call x1, Pallas kernels, reduce_parts(): pl.pallas_call(partial(reduce_kernel, wide_n, slab_n), out_shape=[jax.Sha...  188 us
    dot_general x11, matrix products, mm(): return jnp.einsum(spec, left, right, preferred_element_type=jnp.float32)  91.1 us
    all_gather x1, waiting for transfers between devices, this_slice(): lax.all_gather(jnp.concatenate([tokens, small], axis=0), 'fs', axis=0)  76.4 us
    unnamed x155, local copies, waits for them, and re-layouts  37 us
    reduce_scatter x2, waiting for transfers between devices, scatter_fs(): return lax.psum_scatter(value, 'fs', scatter_dimension=0, tiled=True)  31.7 us
  transfers between devices with their start and end apart: 5, of which 3 were waited for; matrix products, arithmetic and copies ran while one was open for 12% of the time, Pallas kernels for 0%

profile of v1, /device:TPU:0, one launch (start us, length us, event | category | flops | bytes accessed | tf_op | source)
XLA Modules:
  0.0 1211.9 jit_solution(13125772347145796952)
XLA Ops:
  9.0 2.9 concatenate.63
  14.9 13.1 %reshape.401 = bf16[720,4,1024]{2,1,0:T(4,128)(2,1)} reshape(bf16[720,4096]{1,0:T(8,128)(2,1)} %param.27) | data formatting | bytes 11796480 | tf_op jit(solution)/shard_map/reshape | solution.py:936
  28.0 5.2 pad_maximum_fusion.1
  33.1 4.0 copy.268
  37.2 5.6 all-to-all-start
  43.0 76.4 %all-gather.6.cloned.1.call-done = bf16[576,2880]{1,0:T(8,128)(2,1)} async-done(((bf16[144,2880]{1,0:T(8,128)(2,1)}), bf16[576,2880]{1,0:T(8,128)(2,1)}) %all-gather.6.cloned.1.call-update) | async-done | bytes 3317776 | tf_op jit(solution)/shard_map/all_gather | solution.py:922
  121.4 2.5 multiply_reduce_fusion
  124.5 4.5 multiply_convert_fusion
  129.0 13.2 %all-to-all-done = bf16[720,4,1280]{2,0,1:T(8,128)(2,1)} async-done(((bf16[720,4,1280]{2,0,1:T(8,128)(2,1)}), bf16[720,4,1280]{2,0,1:T(8,128)(2,1)}, u32[]{:S(2)}, u32[]{:S(2)}) %all-to-all-start) | async-done | bytes 7372832 | tf_op jit(solution)/shard_map/all_to_all | solution.py:942
  142.2 8.2 convolution_add_fusion.1
  153.1 2.3 copy.275
  155.3 1.9 add_convert_fusion.1
  164.5 4.5 convolution_convert_fusion.3
  169.0 4.6 copy.281
  179.7 2.7 slice_convert_fusion
  182.4 2.5 fusion.1
  184.9 31.7 %reduce-scatter.3.cloned.1.call-done = bf16[128,2880]{1,0:T(8,128)(2,1)} async-done(((bf16[512,2880]{1,0:T(8,128)(2,1)}), bf16[128,2880]{1,0:T(8,128)(2,1)}) %reduce-scatter.3.cloned.1.call-update) | async-done | bytes 737296 | tf_op jit(solution)/shard_map/reduce_scatter | solution.py:104
  221.5 341.4 %experts.1 = (bf16[2,4,8,128,2944]{4,3,2,1,0:T(8,128)(2,1)}, bf16[4,8,128,2944]{3,2,1,0:T(8,128)(2,1)}, bf16[4,8,128,2944]{3,2,1,0:T(8,128)(2,1)}, bf16[2,1536,2...) custom-call(bf16[128,2944]{1,0:T(8,128)(2,1)} %concatenate.73.n_own,, ...), custom_call_target="tpu_custom_call" | custom-call | flops 76441190400 | bytes 300000000 | tf_op jit(solution)/shard_map/experts/pallas_call | solution.py:847
  562.9 219.5 %scatter_blocks.1 = (bf16[2,128,2944]{2,1,0:T(8,128)(2,1)}, bf16[16,4,64,2944]{3,2,1,0:T(8,128)(2,1)}) custom-call(bf16[4,8,128,2944]{3,2,1,0:T(8,128)(2,1)} %get-tuple-element.34.refs_0_, bf16[4,8,128,2944]{3,2,1,0:T(8,128)(2,1)} %get-tuple-element.35.refs_1_), custom_call_target="tpu_custom_call" | custom-call | tf_op jit(solution)/shard_map/scatter_blocks/pallas_call | solution.py:266
  784.0 2.4 multiply_reduce_fusion.1
  789.2 21.1 %fusion.50 = f32[2,2880,720]{1,2,0:T(8,128)} fusion(bf16[2,1536,2880]{2,1,0:T(8,128)(2,1)} %get-tuple-element.39, bf16[2,1536,720]{2,1,0:T(8,128)(2,1)} %get-tuple-element.40), kind=kOutput, calls=%fused_computation.156 | convolution fusion | flops 12740198400 | bytes 38707200 | tf_op jit(solution)/shard_map/erf,erd->efd/dot_general | solution.py:88
  816.2 23.5 %fusion.52 = f32[2,720,2880]{2,1,0:T(8,128)} fusion(bf16[2,1536,720]{2,1,0:T(8,128)(2,1)} %get-tuple-element.44, bf16[2,1536,2880]{2,1,0:T(8,128)(2,1)} %get-tuple-element.45), kind=kOutput, calls=%fused_computation.158 | convolution fusion | flops 12740198400 | bytes 38707200 | tf_op jit(solution)/shard_map/erf,erd->efd/dot_general | solution.py:88
  839.7 8.0 convolution_convert_fusion.5
  847.7 3.0 reshape.450
  850.6 2.5 copy.291
  853.2 3.9 fusion.22
  857.2 1.7 fusion.2
  858.9 1.8 fusion.4
  862.2 2.7 copy.293
  864.9 2.1 reshape.411
  867.6 8.4 convolution_convert_fusion.2
  876.0 4.6 copy.299
  880.6 21.2 %fusion.51 = f32[2,2880,720]{1,2,0:T(8,128)} fusion(bf16[2,1536,2880]{2,1,0:T(8,128)(2,1)} %get-tuple-element.39, bf16[2,1536,720]{2,1,0:T(8,128)(2,1)} %get-tuple-element.42), kind=kOutput, calls=%fused_computation.157 | convolution fusion | flops 12740198400 | bytes 38707200 | tf_op jit(solution)/shard_map/erf,erd->efd/dot_general | solution.py:88
  902.1 2.6 convert_reduce_fusion
  905.7 5.5 convolution_convert_fusion.1
  911.3 3.6 pad_maximum_fusion.2
  914.9 9.9 copy.301
  924.8 9.2 convolution_convert_fusion
  934.0 1.6 fusion.16
  936.1 6.9 pad_maximum_fusion
  942.9 188.5 %reduce_parts.1 = (bf16[2,11,48,2880]{3,2,1,0:T(8,128)(2,1)}, bf16[4,2,3,128,1280]{4,3,2,1,0:T(8,128)(2,1)}) custom-call(bf16[2,11,48,2880]{3,2,1,0:T(8,128)(2,1)} %bitcast.193, bf16[4,2,3,128,1280]{4,3,2,1,0:T(8,128)(2,1)} %bitcast.188), custom_call_target="tpu_custom_call" | custom-call | tf_op jit(solution)/shard_map/reduce_parts/pallas_call | solution.py:480
  1132.4 5.7 slice.219
  1143.4 9.6 convert_bitcast_fusion
  1153.0 3.6 slice_bitcast_fusion.1
  1156.7 11.4 slice_bitcast_fusion
  1172.3 8.4 copy.342
  1181.6 8.6 convert_element_type.252
  1190.2 11.5 copy.346
  (277 shorter events, 56.3 us)
Async XLA Ops:
  7.2 7.3 copy-start.26
  7.2 112.1 %all-gather.6.cloned.1.call-start = ((), (), s32[]{:S(2)}) async-start(), calls=%async_computation.6 | async-start | bytes 4239360 | tf_op jit(solution)/shard_map/all_gather | solution.py:922
  8.9 5.8 copy-start.27
  37.1 5.7 copy-start.66
  37.1 5.8 copy-start.59
  37.1 5.8 copy-start.64
  37.1 5.8 copy-start.65
  37.2 105.0 %all-to-all-start = ((bf16[720,4,1280]{2,0,1:T(8,128)(2,1)}), bf16[720,4,1280]{2,0,1:T(8,128)(2,1)}, u32[]{:S(2)}, u32[]{:S(2)}) async-start(bf16[720,4,1280]{2,0,1:T(8,128)(2,1)} %copy.268), calls=%async_computation | async-start | bytes 14745600 | tf_op jit(solution)/shard_map/all_to_all | solution.py:942
  42.8 173.9 %reduce-scatter.3.cloned.1.call-start = ((), (), s32[]{:S(2)}) async-start(), calls=%async_computation.3 | async-start | bytes 3768320 | tf_op jit(solution)/shard_map/reduce_scatter | solution.py:104
  42.9 118.2 %copy-start.52 = (f32[2,8]{1,0:T(2,128)}, f32[2,8]{1,0:T(2,128)S(1)}, u32[]{:S(2)}) copy-start(f32[2,8]{1,0:T(2,128)S(1)} %reshape.434) | copy-start | bytes 196
  120.7 8.2 copy-start.29
  121.4 61.1 %copy-start.38 = (f32[2880]{0:T(1024)}, f32[2880]{0:T(1024)S(1)}, u32[]{:S(2)}) copy-start(f32[2880]{0:T(1024)S(1)} %reshape.433) | copy-start | bytes 34564
  124.1 37.1 %copy-start.24 = (pred[4,128,128]{1,2,0:T(8,128)(4,1)}, pred[4,128,128]{1,2,0:T(8,128)(4,1)S(1)}, u32[]{:S(2)}) copy-start(pred[4,128,128]{1,2,0:T(8,128)(4,1)S(1)} %compare_and_fusion) | copy-start | bytes 196612
  124.5 33.0 %copy-start.17 = (f32[512,32]{0,1:T(8,128)}, f32[512,32]{0,1:T(8,128)S(1)}, u32[]{:S(2)}) copy-start(f32[512,32]{0,1:T(8,128)S(1)} %get-tuple-element.206) | copy-start | bytes 196612
  124.5 33.0 %copy-start.19 = (f32[512,32]{0,1:T(8,128)}, f32[512,32]{0,1:T(8,128)S(1)}, u32[]{:S(2)}) copy-start(f32[512,32]{0,1:T(8,128)S(1)} %get-tuple-element.207) | copy-start | bytes 196612
  159.9 4.6 slice-start.1
  169.0 4.7 copy-start.56
  169.0 5.3 copy-start.57
  173.6 666.1 %all-gather.4.cloned.1.call-start = ((), (), s32[]{:S(2)}) async-start(), calls=%async_computation.4 | async-start | bytes 3768320 | tf_op jit(solution)/shard_map/all_gather | solution.py:100
  176.0 6.4 copy-start.6
  179.1 607.3 %copy-start.36 = (f32[2880]{0:T(1024)}, f32[2880]{0:T(1024)S(1)}, u32[]{:S(2)}) copy-start(f32[2880]{0:T(1024)S(1)} %reshape.435) | copy-start | bytes 34564
  179.1 607.3 %copy-start.45 = (f32[2880]{0:T(1024)}, f32[2880]{0:T(1024)S(1)}, u32[]{:S(2)}) copy-start(f32[2880]{0:T(1024)S(1)} %reshape.436) | copy-start | bytes 34564
  179.7 39.9 %copy-start.16 = (bf16[2880,16]{1,0:T(8,128)(2,1)}, bf16[2880,16]{1,0:T(8,128)(2,1)S(1)}, u32[]{:S(2)}) copy-start(bf16[2880,16]{1,0:T(8,128)(2,1)S(1)} %reshape.409) | copy-start | bytes 276484
  218.1 568.3 %copy-start.54 = (f32[128]{0:T(128)}, f32[128]{0:T(128)S(1)}, u32[]{:S(2)}) copy-start(f32[128]{0:T(128)S(1)} %get-tuple-element.213) | copy-start | bytes 1540
  218.1 568.3 %copy-start.60 = (f32[128]{0:T(128)}, f32[128]{0:T(128)S(1)}, u32[]{:S(2)}) copy-start(f32[128]{0:T(128)S(1)} %get-tuple-element.212) | copy-start | bytes 1540
  786.4 24.0 %copy-start.62 = (f32[128]{0:T(128)}, f32[128]{0:T(128)S(1)}, u32[]{:S(2)}) copy-start(f32[128]{0:T(128)S(1)} %broadcast_multiply_fusion.1) | copy-start | bytes 1540
  789.1 144.9 %reduce-scatter.5.cloned.1.call-start = ((), (), s32[]{:S(2)}) async-start(), calls=%async_computation.5 | async-start | bytes 3768320 | tf_op jit(solution)/shard_map/reduce_scatter | solution.py:104
  789.2 25.7 %copy-start.3 = (bf16[128,2880]{1,0:T(8,128)(2,1)S(1)}, bf16[128,2880]{1,0:T(8,128)(2,1)}, u32[]{:S(2)}) copy-start(bf16[128,2880]{1,0:T(8,128)(2,1)} %copy-done.2) | copy-start | bytes 2211844
  847.6 5.5 copy-start.25
  847.6 5.5 copy-start.41
  847.6 5.5 copy-start.48
  880.6 21.2 %copy-start.35 = (f32[4,2,8,128]{3,2,1,0:T(8,128)S(1)}, f32[4,2,8,128]{3,2,1,0:T(8,128)}, u32[]{:S(2)}) copy-start(f32[4,2,8,128]{3,2,1,0:T(8,128)} %copy-done.34) | copy-start | bytes 98308
  880.6 21.2 %copy-start.43 = (f32[4,2,8,128]{3,2,1,0:T(8,128)S(1)}, f32[4,2,8,128]{3,2,1,0:T(8,128)}, u32[]{:S(2)}) copy-start(f32[4,2,8,128]{3,2,1,0:T(8,128)} %copy-done.42) | copy-start | bytes 98308
  880.6 21.2 %copy-start.53 = (f32[2,8]{1,0:T(2,128)S(1)}, f32[2,8]{1,0:T(2,128)}, u32[]{:S(2)}) copy-start(f32[2,8]{1,0:T(2,128)} %copy-done.52) | copy-start | bytes 196
  924.8 9.2 copy-start.39
  1142.2 10.8 copy-start.44
  1156.6 11.5 copy-start.5
  1156.6 11.5 copy-start.8
  1156.6 11.5 copy-start.12
  1156.6 11.5 copy-start.15
  1156.6 11.5 copy-start.21
  1156.7 11.5 copy-start.37
  1156.7 11.5 copy-start.46
  1156.7 11.5 copy-start.55
  1156.7 11.5 copy-start.61
  1156.7 11.5 copy-start.63
  1172.2 8.4 slice-start
  1190.2 11.5 copy-start.14
  (27 other events, 58.2 us)
Sparse Core Ops, SparseCore 0:
  14.6 104.6 all-gather.5
  173.7 42.8 reduce-scatter.2
  789.3 47.5 all-gather.3
  880.7 46.9 reduce-scatter.4

commit v2 on v1

--- a/solution.py
+++ b/solution.py
@@ -275,9 +275,9 @@
 
 
 def reduce_kernel(
-    wide_n, slab_n, gw, gq, tw, tq,
-    own_w, own_q, all_q, far_w, far_q, pin_w, pin_q, pout_w, pout_q, din_w, din_q, dout_w, dout_q, tot_w, tot_q,
-    wload, qload, s0w, r0w, s0q, r0q, sa, ra, su, ru, sd, rd, keep, sc, rc,
+    wide_n, slab_n, splits, gw, gq, tw, tq, tk, tv,
+    own_w, own_q, all_q, far_w, far_q, pin_w, pin_q, pout_w, pout_q, din_w, din_q, dout_w, dout_q, tot_w, tot_q, mate_q,
+    wload, qload, s0w, r0w, s0q, r0q, sa, ra, su, ru, sd, rd, keep, keep_q, keep_m, sc, rc,
 ):
     fs, ep, y, x, z, c = spot()
     mate = (fs, ep + 1 - 2 * c)
@@ -319,17 +319,27 @@
     def valid(i):
         return (i >= 0) & (i < items)
 
-    def back(i, f):
-        @pl.when(i < wide_n)
-        def _():
-            dst = tw.at[c, i]
-            f(pltpu.make_async_copy(tot_w.at[i], dst, keep.at[i]), rem(tot_w.at[i], dst, sc.at[i], rc.at[i], mate))
-
-        @pl.when(i >= wide_n)
-        def _():
-            j = i - wide_n
-            dst = tq.at[source(j // parts), c, j % parts]
-            f(pltpu.make_async_copy(tot_q.at[j], dst, keep.at[i]), rem(tot_q.at[j], dst, sc.at[i], rc.at[i], mate))
+    def place(buf, sem, j, core):
+        at = pl.ds(pl.multiple_of((core * parts + j % parts) * rows_q, 16), rows_q)
+        lo, out = 0, []
+        for n, (dst, size) in enumerate(zip((tq, tk, tv), splits)):
+            to = pl.ds(pl.multiple_of(source(j // parts) * size, 128), size)
+            out.append(
+                pltpu.make_async_copy(buf.at[j, :, pl.ds(lo, size)], dst.at[at, to], sem.at[j, n])
+            )
+            lo += size
+        return out
+
+    def share_w(i):
+        dst = tw.at[c, i]
+        return (
+            pltpu.make_async_copy(tot_w.at[i], dst, keep.at[i]),
+            rem(tot_w.at[i], dst, sc.at[i], rc.at[i], mate),
+        )
+
+    def share_q(j):
+        i = j + wide_n
+        return rem(tot_q.at[j], mate_q.at[j], sc.at[i], rc.at[i], mate)
 
     greet(fs, ep, z, 1)
 
@@ -432,19 +442,30 @@
 
             on_item(last, go)
 
-            def start(a, b):
-                a.start()
-                b.start()
-
-            back(last, start)
+            @pl.when(last < wide_n)
+            def _():
+                for copy in share_w(last):
+                    copy.start()
+
+            @pl.when(last >= wide_n)
+            def _():
+                j = last - wide_n
+                for copy in (share_q(j), *place(tot_q, keep_q, j, c)):
+                    copy.start()
 
     @pl.loop(0, items)
     def _(i):
-        def finish(a, b):
-            a.wait()
-            b.wait()
-
-        back(i, finish)
+        @pl.when(i < wide_n)
+        def _():
+            for copy in share_w(i):
+                copy.wait()
+
+        @pl.when(i >= wide_n)
+        def _():
+            j = i - wide_n
+            share_q(j).wait()
+            for copy in place(mate_q, keep_m, j, 1 - c):
+                copy.start()
 
         def go(own, pin, pout, din, dout, tot, j):
             @pl.when(z < 3)
@@ -457,6 +478,11 @@
 
         on_item(i, go)
 
+    @pl.loop(0, slab_n)
+    def _(j):
+        for copy in (*place(tot_q, keep_q, j, c), *place(mate_q, keep_m, j, 1 - c)):
+            copy.wait()
+
     @pl.loop(0, wide_n)
     def _(i):
         give_w(i).wait_send()
@@ -467,7 +493,7 @@
             pass_q(s).wait_send()
 
 
-def reduce_parts(gw, gq, cid):
+def reduce_parts(gw, gq, splits, cid):
     wide_n = gw.shape[1]
     parts = gq.shape[2]
     slab_n = 4 * parts
@@ -477,14 +503,16 @@
     Q = pltpu.VMEM((slab_n,) + gq.shape[3:], BF)
     Q4 = pltpu.VMEM((4, parts) + gq.shape[3:], BF)
     items = wide_n + slab_n
+    slab_rows = 2 * parts * gq.shape[3]
     return pl.pallas_call(
-        partial(reduce_kernel, wide_n, slab_n),
-        out_shape=[jax.ShapeDtypeStruct(gw.shape, BF), jax.ShapeDtypeStruct(gq.shape, BF)],
+        partial(reduce_kernel, wide_n, slab_n, splits),
+        out_shape=[jax.ShapeDtypeStruct(gw.shape, BF)]
+        + [jax.ShapeDtypeStruct((slab_rows, 4 * size), BF) for size in splits],
         in_specs=[free, free],
-        out_specs=[free, free],
-        scratch_shapes=[W, Q, Q4, W, Q4] + [W, Q] * 5
+        out_specs=[free] * 4,
+        scratch_shapes=[W, Q, Q4, W, Q4] + [W, Q] * 5 + [Q]
         + [D((wide_n,)), D((4,)), D((wide_n,)), D((wide_n,)), D((4,)), D((4,)), D((4,)), D((4,))]
-        + [D((items,))] * 7,
+        + [D((items,))] * 4 + [D((wide_n,)), D((slab_n, 3)), D((slab_n, 3)), D((items,)), D((items,))],
         compiler_params=pltpu.CompilerParams(
             collective_id=cid, has_side_effects=True, vmem_limit_bytes=63 * 1024 * 1024
         ),
@@ -492,6 +520,103 @@
     )(gw, gq)
 
 
+def start_kernel(
+    splits, own, wq, wk, wv, rows_out, w_out, here, own_w, sx, rx, sw, rw, sm, rm,
+):
+    fs, ep, y, x, z, c = spot()
+    mate = (fs, ep + 1 - 2 * c)
+    shard = wq.shape[0]
+    cut = -(-shard // 32) * 16
+    halves = ((0, cut), (cut, shard - cut))
+
+    def peer(s):
+        return ((y + s // 2) % 2) * 2 + (x + s) % 2
+
+    def rem(src, dst, s, r, dev):
+        return pltpu.make_async_remote_copy(src, dst, s, r, device_id=dev, device_id_type=MESH)
+
+    def columns(dev, at):
+        lo, out = 0, []
+        for src, size in zip((wq, wk, wv), splits):
+            cols = pl.ds(pl.multiple_of(dev * size, 128), size)
+            out.append((src.at[at, cols], pl.ds(lo, size)))
+            lo += size
+        return out
+
+    def send(s, lo, n):
+        at = pl.ds(lo, n)
+        return [
+            rem(src, w_out.at[fs, at, cols], sw.at[s, k], rw.at[s, k], (peer(s), ep))
+            for k, (src, cols) in enumerate(columns(peer(s), at))
+        ]
+
+    def arrive(s, lo, n):
+        at = pl.ds(lo, n)
+        return [
+            rem(w_out.at[peer(s), at, cols], w_out.at[peer(s), at, cols], sw.at[s, k], rw.at[s, k], mate)
+            for k, (_, cols) in enumerate(columns(fs, at))
+        ]
+
+    def share(s, lo, n):
+        v = w_out.at[peer(s), pl.ds(lo, n)]
+        return rem(v, v, sm.at[s], rm.at[s], mate)
+
+    def give(s):
+        return rem(own, rows_out.at[fs], sx.at[s], rx.at[s], (peer(s), ep))
+
+    locals_ = [pltpu.make_async_copy(own, rows_out.at[fs], here)]
+    for k, (src, cols) in enumerate(columns(fs, pl.ds(0, shard))):
+        locals_.append(pltpu.make_async_copy(src, w_out.at[fs, :, cols], own_w.at[k]))
+    for copy in locals_:
+        copy.start()
+    greet(fs, ep, z, 1)
+    for s in (3, 1, 2):
+        give(s).start()
+    for core in range(2):
+
+        @pl.when(c == core)
+        def _():
+            mine, other = halves[core], halves[1 - core]
+            for s in (3, 1, 2):
+                for copy in send(s, *mine):
+                    copy.start()
+            for s in (1, 2, 3):
+                for copy in arrive(s, *mine):
+                    copy.wait_recv()
+                share(s, *mine).start()
+            for s in (1, 2, 3):
+                share(s, *other).wait_recv()
+            for s in (1, 2, 3):
+                for copy in send(s, *mine):
+                    copy.wait_send()
+                share(s, *mine).wait_send()
+
+    for s in (1, 2, 3):
+        rem(own, rows_out.at[peer(s)], sx.at[s], rx.at[s], mate).wait_recv()
+        give(s).wait_send()
+    for copy in locals_:
+        copy.wait()
+
+
+def start_exchange(own, wq, wk, wv, cid):
+    shard = wq.shape[0]
+    splits = tuple(w.shape[1] // 4 for w in (wq, wk, wv))
+    free = pl.BlockSpec(memory_space=pl.ANY)
+    D = pltpu.SemaphoreType.DMA
+    return pl.pallas_call(
+        partial(start_kernel, splits),
+        out_shape=[
+            jax.ShapeDtypeStruct((4,) + own.shape, BF),
+            jax.ShapeDtypeStruct((4, shard, sum(splits)), BF),
+        ],
+        in_specs=[free] * 4,
+        out_specs=[free] * 2,
+        scratch_shapes=[D, D((3,)), D((4,)), D((4,)), D((4, 3)), D((4, 3)), D((4,)), D((4,))],
+        compiler_params=pltpu.CompilerParams(collective_id=cid, has_side_effects=True),
+        name="start_exchange",
+    )(own, wq, wk, wv)
+
+
 def nn(left, right):
     return lax.dot_general(left, right, (((1,), (0,)), ((), ())), preferred_element_type=F32)
 
@@ -515,7 +640,7 @@
 
 
 def line_order(z, i):
-    code = jnp.where(z == 0, 228, jnp.where(z == 1, 225, jnp.where(z == 2, 54, 27)))
+    code = jnp.where(z == 0, 228, jnp.where(z == 1, 225, jnp.where(z == 2, 30, 27)))
     power = jnp.where(i == 0, 1, jnp.where(i == 1, 4, jnp.where(i == 2, 16, 64)))
     return (code // power) % 4
 
@@ -543,25 +668,26 @@
         e = zz * 2 + self.c
         v = self.full.at[a, self.fs, e, self.upper]
         w = self.full.at[a, self.fs, e, self.lower]
+        s, r = self.s1.at[a, zz], self.r1.at[a, zz]
         return (
-            remote(v, v, self.s1.at[a, zz, 0], self.r1.at[a, zz, 0], self.xn),
-            remote(w, w, self.s1.at[a, zz, 1], self.r1.at[a, zz, 1], self.yn),
+            remote(v, v, s.at[0], r.at[0], self.xn),
+            remote(w, w, s.at[1], r.at[1], self.yn),
+            remote(w, w, s.at[2], r.at[2], self.xn),
+            remote(v, v, s.at[3], r.at[3], self.yn),
         )
 
     def second(self, a, zz):
         e = zz * 2 + self.c
-        v = self.full.at[a, pl.ds(self.y * 2, 2), e, self.upper]
-        out = [remote(v, v, self.s2.at[a, zz, 0], self.r2.at[a, zz, 0], self.yn)]
-        for j in range(2):
-            w = self.full.at[a, 2 * j + self.x, e, self.lower]
-            out.append(remote(w, w, self.s2.at[a, zz, 1 + j], self.r2.at[a, zz, 1 + j], self.xn))
-        return out
+        v = self.full.at[a, self.y * 2 + 1 - self.x, e, self.upper]
+        w = self.full.at[a, (1 - self.y) * 2 + self.x, e, self.lower]
+        s, r = self.s2.at[a, zz], self.r2.at[a, zz]
+        return remote(v, v, s.at[0], r.at[0], self.yn), remote(w, w, s.at[1], r.at[1], self.xn)
 
     def across(self, a, zz, e):
         v = self.full.at[a, :, zz * 2 + e]
         return remote(v, v, self.sc.at[a, zz], self.rc.at[a, zz], self.mate)
 
-    def step1(self, t):
+    def step0(self, t):
         @pl.when(t < 8)
         def _():
             a, zz = self.item(t)
@@ -578,26 +704,35 @@
             def _():
                 self.along(a, zz, 0).start()
 
-            for copy in self.first(a, zz):
+    def step0_if(self, t, inner):
+        inside = (self.z == 1) | (self.z == 2)
+
+        @pl.when(inside == inner)
+        def _():
+            self.step0(t)
+
+    def step1(self, t):
+        @pl.when(t < 8)
+        def _():
+            for copy in self.first(*self.item(t)):
                 copy.start()
 
     def step2(self, t):
         @pl.when(t < 8)
         def _():
             a, zz = self.item(t)
-            one, two = self.first(a, zz)
-            copies = self.second(a, zz)
-            one.wait_recv()
-            copies[0].start()
-            two.wait_recv()
-            copies[1].start()
-            copies[2].start()
+            from_x, from_y, _, _ = self.first(a, zz)
+            to_y, to_x = self.second(a, zz)
+            from_x.wait_recv()
+            to_y.start()
+            from_y.wait_recv()
+            to_x.start()
 
     def step3(self, t):
         @pl.when(t < 8)
         def _():
             a, zz = self.item(t)
-            for copy in self.second(a, zz):
+            for copy in (*self.first(a, zz)[2:], *self.second(a, zz)):
                 copy.wait_recv()
             self.across(a, zz, self.c).start()
 
@@ -627,13 +762,13 @@
     n_own, g_own, wg_hbm, wu_hbm, wd_hbm, bg_ref, bu_ref, bd_ref,
     full, out_hbm, row_hbm, xs_hbm, eg_hbm, mid_hbm, ug_hbm, gg_hbm, cu_hbm, cg_hbm,
     sum_g, sum_u, sum_d,
-    wg_ref, wu_ref, wd_ref, bin_, meta, pmat, gates, xs, res, mid, ugb, ggb, cub, cgb, dots, stage,
+    wg_ref, wu_ref, wd_ref, bin_, meta, pmat, pmat_t, gates, xs, res, mid, cub, cgb, dots, stage,
     w_sem, own_sem, in_sem, st_sem, save_sem,
     *sems,
 ):
     gather = Gather(full, sems)
     fs, ep, z = gather.fs, gather.ep, gather.z
-    card_rows, wpad = bin_.shape[1:]
+    card_rows, wpad = bin_.shape[2:]
     tail = wpad - 128
     off = width - tail
     first = jnp.where(fs == 0, 1.0, 0.0).astype(F32)
@@ -652,78 +787,75 @@
     greet(fs, ep, z)
     for copy in keep:
         copy.wait()
+    gather.step0(0)
     gather.step1(0)
+    gather.step0(1)
     gather.step2(0)
     gather.step1(1)
     gather.step3(0)
-    gather.step2(1)
-    gather.step1(2)
-    for copy in weights:
-        copy.wait()
-
-    def load(a, zz, b, slot):
-        return pltpu.make_async_copy(full.at[a, b // 2, zz * 2 + b % 2], bin_.at[slot], in_sem.at[slot])
+    gather.step0(2)
+
+    def load(t):
+        a, zz = gather.item(t)
+        return pltpu.make_async_copy(full.at[a, :, pl.ds(zz * 2, 2)], bin_, in_sem)
 
     def save(src, dst, k, i, n):
-        return pltpu.make_async_copy(
-            src.at[k], dst.at[k, pl.ds(pl.multiple_of(i * rows, 16), rows)], save_sem.at[n, k]
-        )
+        return pltpu.make_async_copy(src.at[k], dst.at[k, i], save_sem.at[n, k])
+
+    def save_rows(dst, k, i):
+        return pltpu.make_async_copy(xs.at[:, k], dst.at[k, i], save_sem.at[0, k])
 
     def fetch(src, dst, k, i, n):
-        return pltpu.make_async_copy(
-            src.at[k, pl.ds(pl.multiple_of(i * rows, 16), rows)], dst.at[k], save_sem.at[n, k]
-        )
-
-    def spread(a, i, zz, prepare):
-        load(a, zz, 0, 0).start()
-
+        return pltpu.make_async_copy(src.at[k, i], dst.at[k], save_sem.at[n, k])
+
+    def rows_of(ref, k, lo=0, n=width):
+        return ref[:, k, :, lo : lo + n].reshape(rows, n)
+
+    def next_load(t):
+        @pl.when(t < 8)
+        def _():
+            gather.step4(t)
+            load(t).start()
+
+    def spread(i, prepare):
         @pl.loop(0, nb)
         def _(b):
-            slot = lax.rem(b, 2)
-
-            @pl.when(b + 1 < nb)
-            def _():
-                load(a, zz, b + 1, 1 - slot).start()
-
-            load(a, zz, b, slot).wait()
-            at = pl.ds(pl.multiple_of(b * cap, 16), cap)
+            j, c = b // 2, b % 2
             if prepare:
-                meta[...] = jnp.transpose(bin_[slot, :, tail:].astype(F32))
+                meta[...] = jnp.transpose(bin_[j, c, :, tail:].astype(F32))
+                at = pl.ds(pl.multiple_of(b * cap, 16), cap)
+                hits = []
                 for k in range(2):
                     e = ep * 2 + k
                     place = meta[pl.ds(off + e, 1), :]
                     gate = meta[pl.ds(off + 16 + e, 1), :] + meta[pl.ds(off + 32 + e, 1), :]
                     hit = lax.broadcasted_iota(jnp.int32, (cap, card_rows), 0).astype(F32) == place
-                    pmat[i, b, k * cap : (k + 1) * cap, :] = jnp.where(hit, 1.0, 0.0).astype(BF)
                     gates[i, k, at, :] = jnp.sum(jnp.where(hit, gate, 0.0), axis=1, keepdims=True)
+                    hits.append(jnp.where(hit, 1.0, 0.0))
+                hits.append(jnp.zeros((card_rows - 2 * cap, card_rows), F32))
+                hits = jnp.concatenate(hits, axis=0)
+                pmat[i, b] = hits[: 2 * cap].astype(BF)
+                pmat_t[i, b] = jnp.transpose(hits).astype(BF)
             pick = pmat[i, b]
             for lo, n in strips(width, 768):
-                got = nn(pick, bin_[slot, :, lo : lo + n]).astype(BF)
-                xs[0, at, lo : lo + n] = got[:cap]
-                xs[1, at, lo : lo + n] = got[cap:]
-
-    def combine(dst, i, zz, with_dots):
+                got = nn(pick, bin_[j, c, :, lo : lo + n]).astype(BF)
+                xs[b, :, :, lo : lo + n] = got.reshape(2, cap, n)
+
+    def group_store(dst, zz):
+        return pltpu.make_async_copy(stage, dst.at[:, pl.ds(zz * 2, 2)], st_sem)
+
+    def combine(i, with_dots):
         column = lax.broadcasted_iota(jnp.int32, (cap, wpad - width), 1)
-
-        def store(b, slot):
-            return pltpu.make_async_copy(
-                stage.at[slot], dst.at[b // 2, zz * 2 + b % 2], st_sem.at[slot]
-            )
 
         @pl.loop(0, nb)
         def _(b):
-            slot = lax.rem(b, 2)
-
-            @pl.when(b >= 2)
-            def _():
-                store(b - 2, slot).wait()
-
-            pick = pmat[i, b]
-            at = pl.ds(pl.multiple_of(b * cap, 16), cap)
+            j, c = b // 2, b % 2
+            pick = pmat_t[i, b, :, : 2 * cap]
             for lo, n in strips(width, 768):
-                both = jnp.concatenate([res[0, at, lo : lo + n], res[1, at, lo : lo + n]], axis=0)
-                stage[slot, :, lo : lo + n] = tn(pick, both).astype(BF)
+                both = res[b, :, :, lo : lo + n].reshape(2 * cap, n)
+                stage[j, c, :, lo : lo + n] = nn(pick, both).astype(BF)
             if with_dots:
+                at = pl.ds(pl.multiple_of(b * cap, 16), cap)
                 own_dots = jnp.concatenate(
                     [
                         jnp.where(column == ep * 2 + k, dots[k, at, :], 0.0).astype(BF)
@@ -731,23 +863,24 @@
                     ],
                     axis=0,
                 )
-                stage[slot, :, width:] = tn(pick, own_dots).astype(BF)
+                stage[j, c, :, width:] = nn(pick, own_dots).astype(BF)
             else:
-                stage[slot, :, width:] = jnp.zeros((card_rows, wpad - width), BF)
-            store(b, slot).start()
-
-        for b in (nb - 2, nb - 1):
-            store(b, b % 2).wait()
+                stage[j, c, :, width:] = jnp.zeros((card_rows, wpad - width), BF)
+
+    next_load(0)
+    for copy in weights:
+        copy.wait()
 
     @pl.loop(0, 4)
     def _(i):
         zz = line_order(z, i)
-        gather.step4(i)
-        gather.step1(i + 3)
-        spread(0, i, zz, True)
+        gather.step2(i + 1)
+        gather.step1(i + 2)
+        gather.step0_if(i + 3, True)
+        load(i).wait()
+        spread(i, True)
         for k in range(2):
-            save(xs, xs_hbm, k, i, 0).start()
-        gather.step2(i + 2)
+            save_rows(xs_hbm, k, i).start()
 
         @pl.loop(0, 2)
         def _(k):
@@ -755,8 +888,9 @@
             def _():
                 gather.step3(i + 1)
 
-            gate_soft = CLAMP_LIMIT * jnp.tanh((nt(xs[k], wg_ref[k]) + bg_ref[k]) * (1.0 / CLAMP_LIMIT))
-            up_soft = CLAMP_LIMIT * jnp.tanh((nt(xs[k], wu_ref[k]) + bu_ref[k]) * (1.0 / CLAMP_LIMIT))
+            x = rows_of(xs, k)
+            gate_soft = CLAMP_LIMIT * jnp.tanh((nt(x, wg_ref[k]) + bg_ref[k]) * (1.0 / CLAMP_LIMIT))
+            up_soft = CLAMP_LIMIT * jnp.tanh((nt(x, wu_ref[k]) + bu_ref[k]) * (1.0 / CLAMP_LIMIT))
             sig = jax.nn.sigmoid(SWIGLU_ALPHA * gate_soft)
             glu = gate_soft * sig
             mid[k] = ((up_soft + 1.0) * glu).astype(BF)
@@ -771,15 +905,24 @@
             save(cgb, cg_hbm, k, i, 3).start()
             for lo, n in strips(width, 768):
                 part = nn(mid[k], wd_ref[k, :, lo : lo + n]) + first * bd_ref[k, :, lo : lo + n]
-                res[k, :, lo : lo + n] = (part * gates[i, k]).astype(BF)
-
-        combine(out_hbm, i, zz, False)
+                res[:, k, :, lo : lo + n] = (part * gates[i, k]).astype(BF).reshape(nb, cap, n)
+
+        gather.step0_if(i + 3, False)
+        next_load(i + 1)
+
+        @pl.when(i > 0)
+        def _():
+            group_store(out_hbm, line_order(z, i - 1)).wait()
+
+        combine(i, False)
+        group_store(out_hbm, zz).start()
         for k in range(2):
-            save(xs, xs_hbm, k, i, 0).wait()
+            save_rows(xs_hbm, k, i).wait()
             save(mid, mid_hbm, k, i, 1).wait()
             save(cub, cu_hbm, k, i, 2).wait()
             save(cgb, cg_hbm, k, i, 3).wait()
 
+    group_store(out_hbm, line_order(z, 3)).wait()
     sum_g[...] = jnp.zeros_like(sum_g)
     sum_u[...] = jnp.zeros_like(sum_u)
     sum_d[...] = jnp.zeros_like(sum_d)
@@ -791,11 +934,11 @@
             fetch(mid_hbm, mid, k, i, 1).start()
             fetch(cu_hbm, cub, k, i, 2).start()
             fetch(cg_hbm, cgb, k, i, 3).start()
-        gather.step4(i + 4)
-        gather.step1(i + 7)
-        spread(1, i, zz, False)
-        gather.step2(i + 6)
-        ones = jnp.ones((8, rows), BF)
+        gather.step2(i + 5)
+        gather.step1(i + 6)
+        gather.step0_if(i + 7, True)
+        load(i + 4).wait()
+        spread(i, False)
 
         @pl.loop(0, 2)
         def _(k):
@@ -806,31 +949,45 @@
             fetch(mid_hbm, mid, k, i, 1).wait()
             fetch(cu_hbm, cub, k, i, 2).wait()
             fetch(cg_hbm, cgb, k, i, 3).wait()
-            plain = nt(xs[k], wd_ref[k])
+            g_rows = rows_of(xs, k)
+            plain = nt(g_rows, wd_ref[k])
             gate = gates[i, k]
             grad = plain * gate
+            g_rows = g_rows.astype(F32)
             dots[k] = jnp.sum(plain * mid[k].astype(F32), axis=1, keepdims=True) + first * jnp.sum(
-                xs[k].astype(F32) * bd_ref[k], axis=1, keepdims=True
+                g_rows * bd_ref[k], axis=1, keepdims=True
             )
-            ugb[k] = (grad * cub[k].astype(F32)).astype(BF)
-            ggb[k] = (grad * cgb[k].astype(F32)).astype(BF)
-            xs[k] = (xs[k].astype(F32) * gate).astype(BF)
-            save(xs, eg_hbm, k, i, 0).start()
-            save(ugb, ug_hbm, k, i, 4).start()
-            save(ggb, gg_hbm, k, i, 5).start()
-            sum_g[k] += nn(ones, ggb[k])
-            sum_u[k] += nn(ones, ugb[k])
-            sum_d[k] += nn(ones, xs[k])
+            up_grad = (grad * cub[k].astype(F32)).astype(BF)
+            cub[k] = up_grad
+            sum_u[k] += jnp.sum(up_grad.astype(F32), axis=0, keepdims=True)
+            gate_grad = (grad * cgb[k].astype(F32)).astype(BF)
+            cgb[k] = gate_grad
+            sum_g[k] += jnp.sum(gate_grad.astype(F32), axis=0, keepdims=True)
+            scaled = (g_rows * gate).astype(BF)
+            xs[:, k] = scaled.reshape(nb, cap, width)
+            sum_d[k] += jnp.sum(scaled.astype(F32), axis=0, keepdims=True)
+            save_rows(eg_hbm, k, i).start()
+            save(cub, ug_hbm, k, i, 4).start()
+            save(cgb, gg_hbm, k, i, 5).start()
             for lo, n in strips(width, 768):
-                part = nn(ggb[k], wg_ref[k, :, lo : lo + n]) + nn(ugb[k], wu_ref[k, :, lo : lo + n])
-                res[k, :, lo : lo + n] = part.astype(BF)
-
-        combine(row_hbm, i, zz, True)
+                part = nn(cgb[k], wg_ref[k, :, lo : lo + n]) + nn(cub[k], wu_ref[k, :, lo : lo + n])
+                res[:, k, :, lo : lo + n] = part.astype(BF).reshape(nb, cap, n)
+
+        gather.step0_if(i + 7, False)
+        next_load(i + 5)
+
+        @pl.when(i > 0)
+        def _():
+            group_store(row_hbm, line_order(z, i - 1)).wait()
+
+        combine(i, True)
+        group_store(row_hbm, zz).start()
         for k in range(2):
-            save(xs, eg_hbm, k, i, 0).wait()
-            save(ugb, ug_hbm, k, i, 4).wait()
-            save(ggb, gg_hbm, k, i, 5).wait()
-
+            save_rows(eg_hbm, k, i).wait()
+            save(cub, ug_hbm, k, i, 4).wait()
+            save(cgb, gg_hbm, k, i, 5).wait()
+
+    group_store(row_hbm, line_order(z, 3)).wait()
     gather.finish()
 
 
@@ -848,20 +1005,21 @@
         partial(experts_kernel, cap, width),
         out_shape=[shape((2, 4, 8, rows, wpad), BF)]
         + [shape((4, 8, rows, wpad), BF)] * 2
-        + [shape((2, n, width), BF)] * 2
-        + [shape((2, n, ff), BF)] * 5
-        + [shape((2, 8, ff), F32)] * 2
-        + [shape((2, 8, width), F32)],
+        + [shape((2, 4, 8, cap, width), BF)] * 2
+        + [shape((2, 4, m, ff), BF)] * 5
+        + [shape((2, 1, ff), F32)] * 2
+        + [shape((2, 1, width), F32)],
         in_specs=[free] * 5 + [near] * 3,
         out_specs=[free] * 10 + [near] * 3,
         scratch_shapes=[
             V((2, ff, width), BF), V((2, ff, width), BF), V((2, ff, width), BF),
-            V((2, rows, wpad), BF), V((128, rows), F32), V((4, 8, 2 * cap, rows), BF),
-            V((4, 2, m, 1), F32), V((2, m, width), BF), V((2, m, width), BF),
-            V((2, m, ff), BF), V((2, m, ff), BF), V((2, m, ff), BF), V((2, m, ff), BF), V((2, m, ff), BF),
-            V((2, m, 1), F32), V((2, rows, wpad), BF),
-            D((3,)), D((2,)), D((2,)), D((2,)), D((6, 2)),
-            D((2, 4, 2)), D((2, 4)), D((2, 4, 2)), D((2, 4, 2)), D((2, 4, 3)), D((2, 4, 3)), D((2, 4)), D((2, 4)),
+            V((4, 2, rows, wpad), BF), V((128, rows), F32),
+            V((4, 8, 2 * cap, rows), BF), V((4, 8, rows, rows), BF), V((4, 2, m, 1), F32),
+            V((8, 2, cap, width), BF), V((8, 2, cap, width), BF),
+            V((2, m, ff), BF), V((2, m, ff), BF), V((2, m, ff), BF),
+            V((2, m, 1), F32), V((4, 2, rows, wpad), BF),
+            D((3,)), D((2,)), D, D, D((6, 2)),
+            D((2, 4, 2)), D((2, 4)), D((2, 4, 4)), D((2, 4, 4)), D((2, 4, 2)), D((2, 4, 2)), D((2, 4)), D((2, 4)),
         ],
         compiler_params=pltpu.CompilerParams(
             collective_id=cid, has_side_effects=True, vmem_limit_bytes=63 * 1024 * 1024
@@ -871,7 +1029,8 @@
         ),
         name="experts",
     )(n_own, g_own, wg_t, wu_t, w_down, *biases)
-    return (*out[1:8], *(total[:, 0] for total in out[10:]))
+    saved = [v.reshape(2, n, -1) for v in out[3:8]]
+    return (*out[1:3], *saved, *(total[:, 0] for total in out[10:]))
 
 
 def this_slice(
@@ -919,7 +1078,9 @@
     )
     extra = -(-small.shape[0] // (16 * width)) * 16
     small = jnp.pad(small, (0, extra * width - small.shape[0])).reshape(extra, width)
-    packed = lax.all_gather(jnp.concatenate([tokens, small], axis=0), "fs", axis=0)
+    packed, w_qkv = start_exchange(
+        jnp.concatenate([tokens, small], axis=0), w_query, w_key, w_value, 4
+    )
     x_group = packed[:, :rows].reshape(fs_size * rows, width).astype(F32)
     small = packed[:, rows:].reshape(fs_size, -1)
     gain_one = small[:, :shard].reshape(-1).astype(F32)
@@ -931,15 +1092,6 @@
     at += b_router.shape[0]
     lengths = small[:, at : at + seq_lengths.shape[1]].astype(jnp.int32)
 
-    w_qkv = jnp.concatenate(
-        [
-            w_query.reshape(shard, fs_size, q_cols),
-            w_key.reshape(shard, fs_size, kv_cols),
-            w_value.reshape(shard, fs_size, kv_cols),
-        ],
-        axis=2,
-    )
-    w_qkv = lax.all_to_all(w_qkv, "fs", split_axis=1, concat_axis=0, tiled=True)
     w_qkv = w_qkv.reshape(width, q_cols + 2 * kv_cols)
     b_qkv = jnp.concatenate([b_query, b_key, b_value]).astype(jnp.float32)
     sink_score = sinks.astype(jnp.float32).reshape(1, kv_heads, group, 1)
@@ -1046,7 +1198,6 @@
     grad_bo = jnp.sum(branch_grad, axis=0, dtype=jnp.float32)
     mixed_grad = mm("td,fd->tf", branch_grad, w_out).astype(jnp.bfloat16)
     mixed_grad = mixed_grad.reshape(fs_size, rows, kv_heads, group, HEAD_SIZE)
-    grad_wo = left_dot(mixed, branch_grad)
     grad_probs = mm("bqhgd,bkhd->bhgqk", mixed_grad, value)
     value_grad = mm("bhgqk,bqhgd->bkhd", probs_b, mixed_grad)
     row_delta = jnp.sum(probs * grad_probs, axis=-1)
@@ -1083,33 +1234,33 @@
     ).astype(BF)
     cols = q_cols + 2 * kv_cols
     slab_rows, slab_part = 768, 128
-    wide_rows, wide_part = 1056, 48
-    spare_q = (slab_rows - shard) * cols - by_shard.shape[1]
-    gq = jnp.concatenate(
-        [
-            left_dot(norm_attn, qkv_grad).astype(BF).reshape(fs_size, shard, cols),
-            jnp.pad(by_shard, ((0, 0), (0, spare_q))).reshape(fs_size, slab_rows - shard, cols),
-        ],
-        axis=1,
-    ).reshape(fs_size, 2, slab_rows // (2 * slab_part), slab_part, cols)
-    spare_w = (wide_rows - q_cols) * width - own.shape[0]
-    gw = jnp.concatenate(
-        [grad_wo.astype(BF), jnp.pad(own, (0, spare_w)).reshape(wide_rows - q_cols, width)], axis=0
-    ).reshape(2, wide_rows // (2 * wide_part), wide_part, width)
-    tw, tq = reduce_parts(gw, gq, 3)
-    tw = tw.reshape(wide_rows, width)
-    tq = tq.reshape(fs_size, slab_rows, cols)
-    sum_wo = tw[:q_cols].astype(F32)
-    own = tw[q_cols:].reshape(-1)[: own.shape[0]].astype(F32)
-    sums_q = tq[:, :shard].astype(F32).transpose(1, 0, 2)
-    sum_wq = sums_q[:, :, :q_cols].reshape(shard, -1)
-    sum_wk = sums_q[:, :, q_cols : q_cols + kv_cols].reshape(shard, -1)
-    sum_wv = sums_q[:, :, q_cols + kv_cols :].reshape(shard, -1)
+    wide_part = 144
+    own = jnp.where(jnp.arange(fs_size)[:, None] == my_fs, own, jnp.zeros((), BF))
+    by_shard = jnp.concatenate([by_shard, own], axis=1)
+    small_n = by_shard.shape[1]
+    small_rows = -(-small_n // q_cols)
+    by_shard = jnp.pad(by_shard, ((0, 0), (0, small_rows * q_cols - small_n)))
+    norm_pad = jnp.pad(
+        norm_attn.reshape(many, fs_size, shard), ((0, 0), (0, 0), (0, slab_rows - shard))
+    ).reshape(many, fs_size * slab_rows)
+    gq = left_dot(norm_pad, qkv_grad).astype(BF).reshape(fs_size, slab_rows, cols)
+    gq = gq.at[:, shard : shard + small_rows, :q_cols].set(
+        by_shard.reshape(fs_size, small_rows, q_cols)
+    )
+    gq = gq.reshape(fs_size, 2, slab_rows // (2 * slab_part), slab_part, cols)
+    gw = left_dot(branch_grad, mixed).astype(BF)
+    gw = gw.reshape(2, width // (2 * wide_part), wide_part, q_cols)
+    tw, tq, tk, tv = reduce_parts(gw, gq, (q_cols, kv_cols, kv_cols), 3)
+    sum_wo = jnp.swapaxes(tw.reshape(width, q_cols).astype(F32), 0, 1)
+    sum_wq = tq[:shard].astype(F32)
+    sum_wk = tk[:shard].astype(F32)
+    sum_wv = tv[:shard].astype(F32)
     by_shard = jnp.sum(
-        tq[:, shard:].reshape(fs_size, -1)[:, : by_shard.shape[1]].astype(F32), axis=0
-    )
+        tq[shard : shard + small_rows].astype(F32).reshape(small_rows, fs_size, q_cols), axis=1
+    ).reshape(-1)
     sum_wr = by_shard[: shard * expert_count].reshape(shard, expert_count)
-    rest = by_shard[shard * expert_count :]
+    rest = by_shard[shard * expert_count : small_n - own.shape[1]]
+    own = by_shard[small_n - own.shape[1] : small_n]
     sum_b = own[:cols]
     return (
         block_out.astype(jnp.bfloat16),

time: 1220 us -> 1090 us (0.89)
  waiting for transfers between devices: 121 us -> 26.5 us
  local copies, waits for them, and re-layouts: 131 us -> 77.1 us
  Pallas kernels: 749 us -> 780 us
    pallas_call x1 -> x2, Pallas kernels: 188 us -> 273 us  [the longest x1 187 us: reduce_parts(): pl.pallas_call(partial(reduce_kernel, wide_n, slab_n, splits), out_shape=...]
    all_gather x1 -> x0, waiting for transfers between devices: 76.4 us -> none  [this_slice(): lax.all_gather(jnp.concatenate([tokens, small], axis=0), 'fs', axis=0)]
    pallas_call x1, Pallas kernels: 341 us -> 287 us  [experts(): pl.pallas_call(partial(experts_kernel, cap, width), out_shape=[shape((2,...]
    reshape x10 -> x2, local copies, waits for them, and re-layouts: 28.6 us -> 0.18 us  [the longest x1 0.17 us: this_slice(): tq[shard:shard + small_rows].astype(F32)]
    unnamed x155, local copies, waits for them, and re-layouts: 37 us -> 12.1 us
    convert_element_type x0 -> x2, local copies, waits for them, and re-layouts: none -> 16.8 us  [this_slice(): x_group = packed[:, :rows].reshape(fs_size * rows, width).astype(F32)]
    concatenate x3 -> x0, other arithmetic: 15.7 us -> none  [the longest x1 6.87 us: this_slice(): jnp.concatenate([left_dot(norm_attn, qkv_grad).astype(BF).reshape(fs_size...]
    concatenate x3 -> x1, local copies, waits for them, and re-layouts: 14 us -> 0.15 us  [this_slice(): by_shard = jnp.concatenate([by_shard, own], axis=1)]
  transfers between devices with their start and end apart: 5 -> 3, of which waited for: 3 -> 3; matrix products, arithmetic and copies ran while one was open for 12% -> 11% of each run, Pallas kernels for 0% -> 0%
where the time goes in v2:
time: 1090 us; the launch traced here: 1080 us
  Pallas kernels  780 us (72%)
  matrix products  119 us (11%)
  local copies, waits for them, and re-layouts  77.1 us (7%)
  other arithmetic  60.3 us (6%)
  waiting for transfers between devices  26.5 us (2%)
  between operations  15.3 us (1%)
    pallas_call x1, Pallas kernels, experts(): pl.pallas_call(partial(experts_kernel, cap, width), out_shape=[shape((2,...  287 us
    pallas_call x1, Pallas kernels, scatter_blocks(): pl.pallas_call(partial(scatter_kernel, na, parts), out_shape=[jax.ShapeDt...  219 us
    pallas_call x1, Pallas kernels, reduce_parts(): pl.pallas_call(partial(reduce_kernel, wide_n, slab_n, splits), out_shape=...  187 us
    dot_general x11, matrix products, mm(): return jnp.einsum(spec, left, right, preferred_element_type=jnp.float32)  90.4 us
    pallas_call x1, Pallas kernels, start_exchange(): pl.pallas_call(partial(start_kernel, splits), out_shape=[jax.ShapeDtypeSt...  86.7 us
  transfers between devices with their start and end apart: 3, of which 3 were waited for; matrix products, arithmetic and copies ran while one was open for 11% of the time, Pallas kernels for 0%

profile of v2, /device:TPU:0, one launch (start us, length us, event | category | flops | bytes accessed | tf_op | source)
XLA Modules:
  0.0 1078.2 jit_solution(11384841607645165174)
XLA Ops:
  9.5 2.8 concatenate.59
  12.5 1.5 copy.155
  14.9 86.7 %start_exchange.1 = (bf16[4,144,2880]{2,1,0:T(8,128)(2,1)}, bf16[4,720,1280]{2,1,0:T(8,128)(2,1)}) custom-call(bf16[144,2880]{1,0:T(8,128)(2,1)} %pad_maximum_fusion.2.own, bf16[720,4096]{1,0:T(8,128)(2,1)} %wq.1, bf16[720,512]{1,0:T(8,128)(2,1)} %wk.1, bf16[720,512]{1,0:T(8,128)(2,1)} %wv.1), custom_call_target="tpu_custom_call" | custom-call | tf_op jit(solution)/shard_map/start_exchange/pallas_call | solution.py:606
  101.7 2.5 multiply_reduce_fusion
  106.5 2.8 multiply_convert_fusion
  109.4 7.3 convolution_add_fusion.1
  118.2 1.7 copy.158
  119.8 1.6 reshape.453
  121.4 2.3 copy.164
  124.7 1.9 add_convert_fusion.1
  134.0 4.5 convolution_convert_fusion.3
  138.5 4.6 copy.170
  148.0 5.2 slice_convert_fusion.1
  153.2 9.3 reshape.500
  162.5 7.5 copy.221
  170.0 3.1 multiply_convert_fusion.1
  173.1 2.0 pad.22
  175.7 10.7 reduce-scatter.3.cloned.1.call-done
  186.4 1.5 multiply_reduce_fusion.3
  191.3 287.1 %experts.1 = (bf16[2,4,8,128,2944]{4,3,2,1,0:T(8,128)(2,1)}, bf16[4,8,128,2944]{3,2,1,0:T(8,128)(2,1)}, bf16[4,8,128,2944]{3,2,1,0:T(8,128)(2,1)}, bf16[2,4,8,48...) custom-call(bf16[128,2944]{1,0:T(8,128)(2,1)} %concatenate.68.n_own,, ...), custom_call_target="tpu_custom_call" | custom-call | flops 76441190400 | bytes 300000000 | tf_op jit(solution)/shard_map/experts/pallas_call | solution.py:1004
  478.4 219.2 %scatter_blocks.1 = (bf16[2,128,2944]{2,1,0:T(8,128)(2,1)}, bf16[16,4,64,2944]{3,2,1,0:T(8,128)(2,1)}) custom-call(bf16[4,8,128,2944]{3,2,1,0:T(8,128)(2,1)} %get-tuple-element.52.refs_0_, bf16[4,8,128,2944]{3,2,1,0:T(8,128)(2,1)} %get-tuple-element.53.refs_1_), custom_call_target="tpu_custom_call" | custom-call | tf_op jit(solution)/shard_map/scatter_blocks/pallas_call | solution.py:266
  699.2 2.4 multiply_reduce_fusion.1
  702.7 1.6 fusion.41
  704.5 21.0 %fusion.49 = f32[2,2880,720]{1,2,0:T(8,128)} fusion(bf16[2,1536,2880]{2,1,0:T(8,128)(2,1)} %bitcast.197, bf16[2,1536,720]{2,1,0:T(8,128)(2,1)} %bitcast.200), kind=kOutput, calls=%fused_computation.149 | convolution fusion | flops 12740198400 | bytes 38707200 | tf_op jit(solution)/shard_map/erf,erd->efd/dot_general | solution.py:88
  729.9 23.0 %fusion.50 = f32[2,720,2880]{2,1,0:T(8,128)} fusion(bf16[2,1536,720]{2,1,0:T(8,128)(2,1)} %bitcast.164, bf16[2,1536,2880]{2,1,0:T(8,128)(2,1)} %bitcast.165), kind=kOutput, calls=%fused_computation.150 | convolution fusion | flops 12740198400 | bytes 38707200 | tf_op jit(solution)/shard_map/erf,erd->efd/dot_general | solution.py:88
  752.8 5.9 all-gather.2.cloned.1.call-done
  758.8 8.0 convolution_convert_fusion.5
  766.7 3.0 reshape.501
  769.7 2.5 copy.180
  772.2 3.9 fusion.20
  776.3 1.7 fusion
  778.0 1.8 fusion.2
  781.3 2.7 copy.182
  784.0 2.1 reshape.459
  786.7 8.4 convolution_convert_fusion.2
  795.1 4.6 copy.188
  799.7 21.1 %fusion.48 = f32[2,2880,720]{1,2,0:T(8,128)} fusion(bf16[2,1536,2880]{2,1,0:T(8,128)(2,1)} %bitcast.198, bf16[2,1536,720]{2,1,0:T(8,128)(2,1)} %bitcast.199), kind=kOutput, calls=%fused_computation.148 | convolution fusion | flops 12740198400 | bytes 38707200 | tf_op jit(solution)/shard_map/erf,erd->efd/dot_general | solution.py:88
  821.2 2.6 convert_reduce_fusion
  824.3 7.4 convolution_convert_fusion.1
  831.7 6.5 convolution_convert_fusion
  838.2 9.9 reduce-scatter.5.cloned.1.call-done
  848.1 2.1 fusion.14
  850.6 3.2 scatter.4
  853.8 186.6 %reduce_parts.1 = (bf16[2,10,144,1024]{3,2,1,0:T(8,128)(2,1)}, bf16[768,4096]{1,0:T(8,128)(2,1)}, bf16[768,512]{1,0:T(8,128)(2,1)}, bf16[768,512]{1,0:T(8,128)(2,1)}) custom-call(bf16[2,10,144,1024]{3,2,1,0:T(8,128)(2,1)} %bitcast.169, bf16[4,2,3,128,1280]{4,3,2,1,0:T(8,128)(2,1)} %bitcast.168), custom_call_target="tpu_custom_call" | custom-call | tf_op jit(solution)/shard_map/reduce_parts/pallas_call | solution.py:507
  1045.1 9.0 slice_convert_fusion
  1055.5 1.6 copy.198
  1059.0 2.4 slice_convert_fusion.3
  1062.8 8.6 convert_bitcast_fusion
  (262 shorter events, 43.6 us)
Async XLA Ops:
  7.2 179.2 %reduce-scatter.3.cloned.1.call-start = ((), (), s32[]{:S(2)}) async-start(), calls=%async_computation.2 | async-start | bytes 3768320 | tf_op jit(solution)/shard_map/reduce_scatter | solution.py:104
  106.4 2.9 copy-start.38
  106.4 2.9 copy-start.58
  106.4 2.9 copy-start.66
  106.4 2.9 copy-start.67
  117.7 12.9 %copy-start.48 = (f32[2,8]{1,0:T(2,128)}, f32[2,8]{1,0:T(2,128)S(1)}, u32[]{:S(2)}) copy-start(f32[2,8]{1,0:T(2,128)S(1)} %reshape.482) | copy-start | bytes 196
  127.3 3.4 copy-start.24
  129.4 4.6 slice-start
  130.8 3.2 slice-start.1
  143.1 615.6 %all-gather.2.cloned.1.call-start = ((), (), s32[]{:S(2)}) async-start(), calls=%async_computation.3 | async-start | bytes 3768320 | tf_op jit(solution)/shard_map/all_gather | solution.py:100
  146.1 7.1 copy-start.6
  148.0 41.4 %copy-start.15 = (bf16[2880,16]{1,0:T(8,128)(2,1)}, bf16[2880,16]{1,0:T(8,128)(2,1)S(1)}, u32[]{:S(2)}) copy-start(bf16[2880,16]{1,0:T(8,128)(2,1)S(1)} %reshape.457) | copy-start | bytes 276484
  162.5 7.5 copy-start.50
  187.9 513.7 %copy-start.59 = (f32[128]{0:T(128)}, f32[128]{0:T(128)S(1)}, u32[]{:S(2)}) copy-start(f32[128]{0:T(128)S(1)} %get-tuple-element.189) | copy-start | bytes 1540
  698.9 3.9 copy-start.4
  698.9 3.9 copy-start.7
  704.4 143.7 %reduce-scatter.5.cloned.1.call-start = ((), (), s32[]{:S(2)}) async-start(), calls=%async_computation.4 | async-start | bytes 3768320 | tf_op jit(solution)/shard_map/reduce_scatter | solution.py:104
  704.4 21.0 %copy-start.52 = (f32[2,1,720]{2,1,0:T(1,128)S(1)}, f32[2,1,720]{2,1,0:T(1,128)}, u32[]{:S(2)}) copy-start(f32[2,1,720]{2,1,0:T(1,128)} %get-tuple-element.61) | copy-start | bytes 17284
  704.4 21.6 %copy-start.51 = (f32[2,1,720]{2,1,0:T(1,128)S(1)}, f32[2,1,720]{2,1,0:T(1,128)}, u32[]{:S(2)}) copy-start(f32[2,1,720]{2,1,0:T(1,128)} %get-tuple-element.63) | copy-start | bytes 17284
  704.4 22.2 %copy-start.46 = (f32[2,1,2880]{2,1,0:T(1,128)S(1)}, f32[2,1,2880]{2,1,0:T(1,128)}, u32[]{:S(2)}) copy-start(f32[2,1,2880]{2,1,0:T(1,128)} %get-tuple-element.66) | copy-start | bytes 69124
  704.4 23.6 %copy-start.3 = (bf16[128,2880]{1,0:T(8,128)(2,1)S(1)}, bf16[128,2880]{1,0:T(8,128)(2,1)}, u32[]{:S(2)}) copy-start(bf16[128,2880]{1,0:T(8,128)(2,1)} %copy-done.2) | copy-start | bytes 2211844
  766.7 5.5 copy-start.25
  766.7 5.5 copy-start.35
  766.7 5.5 copy-start.41
  772.2 3.9 copy-start.1
  772.2 4.0 copy-start.21
  772.2 4.0 copy-start.45
  799.7 21.2 %copy-start.33 = (f32[4,2,8,128]{3,2,1,0:T(8,128)S(1)}, f32[4,2,8,128]{3,2,1,0:T(8,128)}, u32[]{:S(2)}) copy-start(f32[4,2,8,128]{3,2,1,0:T(8,128)} %copy-done.32) | copy-start | bytes 98308
  799.7 21.2 %copy-start.37 = (f32[4,2,8,128]{3,2,1,0:T(8,128)S(1)}, f32[4,2,8,128]{3,2,1,0:T(8,128)}, u32[]{:S(2)}) copy-start(f32[4,2,8,128]{3,2,1,0:T(8,128)} %copy-done.36) | copy-start | bytes 98308
  799.7 21.2 %copy-start.43 = (f32[4,2,8,128]{3,2,1,0:T(8,128)S(1)}, f32[4,2,8,128]{3,2,1,0:T(8,128)}, u32[]{:S(2)}) copy-start(f32[4,2,8,128]{3,2,1,0:T(8,128)} %copy-done.42) | copy-start | bytes 98308
  799.7 21.2 %copy-start.49 = (f32[2,8]{1,0:T(2,128)S(1)}, f32[2,8]{1,0:T(2,128)}, u32[]{:S(2)}) copy-start(f32[2,8]{1,0:T(2,128)} %copy-done.48) | copy-start | bytes 196
  820.9 3.3 copy-start.68
  820.9 3.4 copy-start.23
  824.3 7.4 copy-start.13
  831.7 16.4 %copy-start.39 = (f32[2880]{0:T(1024)S(1)}, f32[2880]{0:T(1024)}, u32[]{:S(2)}) copy-start(f32[2880]{0:T(1024)} %copy-done.38) | copy-start | bytes 34564
  831.7 16.4 %copy-start.55 = (f32[128]{0:T(128)S(1)}, f32[128]{0:T(128)}, u32[]{:S(2)}) copy-start(f32[128]{0:T(128)} %get-tuple-element.188) | copy-start | bytes 1540
  831.7 18.6 %copy-start.63 = (bf16[4,4]{1,0:T(4,128)(2,1)S(1)}, bf16[4,4]{1,0:T(4,128)(2,1)}, u32[]{:S(2)}) copy-start(bf16[4,4]{1,0:T(4,128)(2,1)} %reshape.470) | copy-start | bytes 100
  1045.0 9.1 copy-start.65
  1045.0 9.1 copy-start.5
  1045.0 9.1 copy-start.8
  1045.0 9.1 copy-start.12
  1045.0 9.1 copy-start.14
  1045.0 9.1 copy-start.20
  1045.0 9.1 copy-start.56
  1045.1 9.1 copy-start.60
  1045.1 9.1 copy-start.62
  1045.1 9.1 copy-start.64
  1057.1 4.4 copy-start.27
  (27 other events, 47.5 us)
Sparse Core Ops, SparseCore 0:
  143.3 43.0 reduce-scatter.2
  704.5 54.2 all-gather.1
  799.8 48.2 reduce-scatter.4

commit v3 on v2

--- a/solution.py
+++ b/solution.py
@@ -275,7 +275,7 @@
 
 
 def reduce_kernel(
-    wide_n, slab_n, splits, gw, gq, tw, tq, tk, tv,
+    wide_n, slab_n, splits, gw, gq, gs, tw, tq, tk, tv,
     own_w, own_q, all_q, far_w, far_q, pin_w, pin_q, pout_w, pout_q, din_w, din_q, dout_w, dout_q, tot_w, tot_q, mate_q,
     wload, qload, s0w, r0w, s0q, r0q, sa, ra, su, ru, sd, rd, keep, keep_q, keep_m, sc, rc,
 ):
@@ -294,14 +294,55 @@
     def give_w(i):
         return rem(gw.at[1 - c, i], far_w.at[i], s0w.at[i], r0w.at[i], mate)
 
-    def give_q(s):
-        return rem(gq.at[source(s), 1 - c], far_q.at[s], s0q.at[s], r0q.at[s], mate)
-
     def load_w(i):
         return pltpu.make_async_copy(gw.at[c, i], own_w.at[i], wload.at[i])
 
-    def load_q(s):
-        return pltpu.make_async_copy(gq.at[source(s), c], all_q.at[s], qload.at[s])
+    body = gq.shape[1] - (2 * parts - 1) * rows_q
+
+    def pieces(s, core, dst):
+        base = core * parts * rows_q
+        out = []
+        for p in range(parts):
+            n = rows_q if p < parts - 1 else body
+            at = pl.ds(pl.multiple_of(base + p * rows_q, 16), n)
+            out.append((gq.at[source(s), at], dst.at[s, p, pl.ds(0, n)]))
+        rest = dst.at[s, parts - 1, pl.ds(body, rows_q - body)]
+        at = pl.ds((parts - 1) * rows_q + body, rows_q - body)
+        return out + [(gq.at[source(s), at], rest)], (gs.at[source(s)], rest)
+
+    def give_q(s, do):
+        common, other = pieces(s, 1 - c, far_q)
+
+        def move(n, pair):
+            do(rem(*pair, s0q.at[s, n], r0q.at[s, n], mate))
+
+        for n, pair in enumerate(common[:-1]):
+            move(n, pair)
+
+        @pl.when(c == 1)
+        def _():
+            move(parts, common[-1])
+
+        @pl.when(c == 0)
+        def _():
+            move(parts, other)
+
+    def load_q(s, do):
+        common, other = pieces(s, c, all_q)
+
+        def move(n, pair):
+            do(pltpu.make_async_copy(*pair, qload.at[s, n]))
+
+        for n, pair in enumerate(common[:-1]):
+            move(n, pair)
+
+        @pl.when(c == 0)
+        def _():
+            move(parts, common[-1])
+
+        @pl.when(c == 1)
+        def _():
+            move(parts, other)
 
     def pass_q(s):
         dev = (source(s), ep)
@@ -349,8 +390,8 @@
         load_w(i).start()
 
     for s in (1, 2, 3, 0):
-        give_q(s).start()
-        load_q(s).start()
+        give_q(s, lambda copy: copy.start())
+        load_q(s, lambda copy: copy.start())
 
     @pl.loop(0, items + 4)
     def _(t):
@@ -362,10 +403,10 @@
 
         for n, s in enumerate((1, 2, 3, 0)):
 
-            @pl.when(t == n)
+            @pl.when(t == n + 3)
             def _():
-                load_q(s).wait()
-                give_q(s).wait_recv()
+                load_q(s, lambda copy: copy.wait())
+                give_q(s, lambda copy: copy.wait_recv())
 
                 @pl.loop(0, parts)
                 def _(j):
@@ -488,46 +529,53 @@
         give_w(i).wait_send()
 
     for s in range(4):
-        give_q(s).wait_send()
+        give_q(s, lambda copy: copy.wait_send())
         if s:
             pass_q(s).wait_send()
 
 
-def reduce_parts(gw, gq, splits, cid):
+def reduce_parts(gw, gq, gs, parts, splits, cid):
     wide_n = gw.shape[1]
-    parts = gq.shape[2]
+    slab_rows = gq.shape[1] + gs.shape[1]
+    rows_q, cols = slab_rows // (2 * parts), gq.shape[2]
     slab_n = 4 * parts
     free = pl.BlockSpec(memory_space=pl.ANY)
     D = pltpu.SemaphoreType.DMA
     W = pltpu.VMEM((wide_n,) + gw.shape[2:], BF)
-    Q = pltpu.VMEM((slab_n,) + gq.shape[3:], BF)
-    Q4 = pltpu.VMEM((4, parts) + gq.shape[3:], BF)
+    Q = pltpu.VMEM((slab_n, rows_q, cols), BF)
+    Q4 = pltpu.VMEM((4, parts, rows_q, cols), BF)
     items = wide_n + slab_n
-    slab_rows = 2 * parts * gq.shape[3]
     return pl.pallas_call(
         partial(reduce_kernel, wide_n, slab_n, splits),
         out_shape=[jax.ShapeDtypeStruct(gw.shape, BF)]
         + [jax.ShapeDtypeStruct((slab_rows, 4 * size), BF) for size in splits],
-        in_specs=[free, free],
+        in_specs=[free] * 3,
         out_specs=[free] * 4,
         scratch_shapes=[W, Q, Q4, W, Q4] + [W, Q] * 5 + [Q]
-        + [D((wide_n,)), D((4,)), D((wide_n,)), D((wide_n,)), D((4,)), D((4,)), D((4,)), D((4,))]
+        + [D((wide_n,)), D((4, parts + 1)), D((wide_n,)), D((wide_n,)), D((4, parts + 1)), D((4, parts + 1))]
+        + [D((4,)), D((4,))]
         + [D((items,))] * 4 + [D((wide_n,)), D((slab_n, 3)), D((slab_n, 3)), D((items,)), D((items,))],
         compiler_params=pltpu.CompilerParams(
             collective_id=cid, has_side_effects=True, vmem_limit_bytes=63 * 1024 * 1024
         ),
+        cost_estimate=pl.CostEstimate(flops=0, bytes_accessed=500_000_000, transcendentals=0),
         name="reduce_parts",
-    )(gw, gq)
+    )(gw, gq, gs)
 
 
 def start_kernel(
-    splits, own, wq, wk, wv, rows_out, w_out, here, own_w, sx, rx, sw, rw, sm, rm,
+    splits, own, few, wq, wk, wv, rows_out, few_out, w_out, own_cols,
+    here, here_few, own_w, sx, rx, sf, rf, sw, rw, sm, rm,
 ):
     fs, ep, y, x, z, c = spot()
     mate = (fs, ep + 1 - 2 * c)
     shard = wq.shape[0]
-    cut = -(-shard // 32) * 16
-    halves = ((0, cut), (cut, shard - cut))
+    pair = (fs, ep + 2 - 4 * (z % 2))
+    units = shard // 16
+    edges = [16 * (units * n // 4) for n in range(5)]
+    quarters = [(lo, hi - lo) for lo, hi in zip(edges, edges[1:])]
+    half = own.shape[0] // 2
+    bands = (pl.ds(0, half), pl.ds(half, half))
 
     def peer(s):
         return ((y + s // 2) % 2) * 2 + (x + s) % 2
@@ -557,48 +605,84 @@
             for k, (_, cols) in enumerate(columns(fs, at))
         ]
 
-    def share(s, lo, n):
+    def share(s, k, lo, n, dev):
         v = w_out.at[peer(s), pl.ds(lo, n)]
-        return rem(v, v, sm.at[s], rm.at[s], mate)
-
-    def give(s):
-        return rem(own, rows_out.at[fs], sx.at[s], rx.at[s], (peer(s), ep))
-
-    locals_ = [pltpu.make_async_copy(own, rows_out.at[fs], here)]
+        return rem(v, v, sm.at[s, k], rm.at[s, k], dev)
+
+    def give(s, band):
+        v = rows_out.at[fs, bands[band]]
+        return rem(v, v, sx.at[s, band], rx.at[s, band], (peer(s), ep))
+
+    def pass_on(s, band):
+        v = rows_out.at[peer(s), bands[band]]
+        return rem(v, v, sx.at[3, band], rx.at[3, band], (peer(3 - s), ep))
+
+    def give_few(s):
+        return rem(few, few_out.at[fs], sf.at[s], rf.at[s], (peer(s), ep))
+
+    keep = pltpu.make_async_copy(own, rows_out.at[fs], here)
+    keep.start()
+    keep_few = pltpu.make_async_copy(few, few_out.at[fs], here_few)
+    keep_few.start()
+    locals_ = []
     for k, (src, cols) in enumerate(columns(fs, pl.ds(0, shard))):
-        locals_.append(pltpu.make_async_copy(src, w_out.at[fs, :, cols], own_w.at[k]))
+        locals_.append(pltpu.make_async_copy(src, own_cols.at[:, cols], own_w.at[k]))
     for copy in locals_:
         copy.start()
     greet(fs, ep, z, 1)
-    for s in (3, 1, 2):
-        give(s).start()
-    for core in range(2):
-
-        @pl.when(c == core)
-        def _():
-            mine, other = halves[core], halves[1 - core]
+    keep.wait()
+    for copy in locals_:
+        copy.wait()
+    own_slab = pltpu.make_async_copy(own_cols, w_out.at[fs], here)
+    own_slab.start()
+    for s in (1, 2, 3):
+        give_few(s).start()
+    for quarter in range(4):
+
+        @pl.when((z % 2) * 2 + c == quarter)
+        def _():
+            mine, mates, pairs, last = (quarters[quarter ^ n] for n in (0, 1, 2, 3))
             for s in (3, 1, 2):
                 for copy in send(s, *mine):
                     copy.start()
+            for s, band in ((1, 0), (2, 1), (1, 1), (2, 0)):
+                give(s, band).start()
             for s in (1, 2, 3):
                 for copy in arrive(s, *mine):
                     copy.wait_recv()
-                share(s, *mine).start()
+                share(s, 0, *mine, pair).start()
+                share(s, 1, *mine, mate).start()
+            give(1, 0).wait_recv()
+            pass_on(1, 0).start()
+            give(2, 1).wait_recv()
+            pass_on(2, 1).start()
             for s in (1, 2, 3):
-                share(s, *other).wait_recv()
+                share(s, 0, *pairs, pair).wait_recv()
+                share(s, 2, *pairs, mate).start()
+            for s in (1, 2, 3):
+                share(s, 1, *mates, mate).wait_recv()
+                share(s, 2, *last, mate).wait_recv()
             for s in (1, 2, 3):
                 for copy in send(s, *mine):
                     copy.wait_send()
-                share(s, *mine).wait_send()
-
+                share(s, 0, *mine, pair).wait_send()
+                share(s, 1, *mine, mate).wait_send()
+                share(s, 2, *pairs, mate).wait_send()
+
+    for s in (1, 2):
+        give(s, 2 - s).wait_recv()
+        for band in range(2):
+            give(s, band).wait_send()
+    for s, band in ((1, 0), (2, 1)):
+        pass_on(s, band).wait()
     for s in (1, 2, 3):
-        rem(own, rows_out.at[peer(s)], sx.at[s], rx.at[s], mate).wait_recv()
-        give(s).wait_send()
-    for copy in locals_:
-        copy.wait()
-
-
-def start_exchange(own, wq, wk, wv, cid):
+        give_few(s).wait_send()
+        rem(few, few_out.at[peer(s)], sf.at[s], rf.at[s], mate).wait_recv()
+    own_slab.wait()
+    keep_few.wait()
+
+
+def start_exchange(own, few, wq, wk, wv, cid):
     shard = wq.shape[0]
     splits = tuple(w.shape[1] // 4 for w in (wq, wk, wv))
     free = pl.BlockSpec(memory_space=pl.ANY)
@@ -607,14 +691,15 @@
         partial(start_kernel, splits),
         out_shape=[
             jax.ShapeDtypeStruct((4,) + own.shape, BF),
+            jax.ShapeDtypeStruct((4,) + few.shape, BF),
             jax.ShapeDtypeStruct((4, shard, sum(splits)), BF),
         ],
-        in_specs=[free] * 4,
-        out_specs=[free] * 2,
-        scratch_shapes=[D, D((3,)), D((4,)), D((4,)), D((4, 3)), D((4, 3)), D((4,)), D((4,))],
+        in_specs=[pl.BlockSpec(memory_space=pltpu.VMEM)] * 2 + [free] * 3,
+        out_specs=[free] * 3,
+        scratch_shapes=[pltpu.VMEM((shard, sum(splits)), BF), D, D, D((3,)), D((4, 2)), D((4, 2)), D((4,)), D((4,)), D((4, 3)), D((4, 3)), D((4, 3)), D((4, 3))],
         compiler_params=pltpu.CompilerParams(collective_id=cid, has_side_effects=True),
         name="start_exchange",
-    )(own, wq, wk, wv)
+    )(own, few, wq, wk, wv)
 
 
 def nn(left, right):
@@ -1009,7 +1094,7 @@
         + [shape((2, 4, m, ff), BF)] * 5
         + [shape((2, 1, ff), F32)] * 2
         + [shape((2, 1, width), F32)],
-        in_specs=[free] * 5 + [near] * 3,
+        in_specs=[near] * 2 + [free] * 3 + [near] * 3,
         out_specs=[free] * 10 + [near] * 3,
         scratch_shapes=[
             V((2, ff, width), BF), V((2, ff, width), BF), V((2, ff, width), BF),
@@ -1031,6 +1116,143 @@
     )(n_own, g_own, wg_t, wu_t, w_down, *biases)
     saved = [v.reshape(2, n, -1) for v in out[3:8]]
     return (*out[1:3], *saved, *(total[:, 0] for total in out[10:]))
+
+
+def group_sum_kernel(parts, p_ref, out_ref, q, v1, v2, s1, r1, s2, r2):
+    fs, ep, y, x, z, c = spot()
+    rows = p_ref.shape[1]
+    step = rows // (2 * parts)
+    xn, yn = (fs + 1 - 2 * x, ep), (fs + 2 - 4 * y, ep)
+
+    def rem(src, dst, s, r, dev):
+        return pltpu.make_async_remote_copy(src, dst, s, r, device_id=dev, device_id_type=MESH)
+
+    def band(n, half):
+        return pl.ds((2 * n + half) * step, step)
+
+    def one(n):
+        a, b = band(n, 0), band(n, 1)
+        out = [
+            (rem(p_ref.at[2 * j + 1 - x, a], v1.at[n, 0, j], s1.at[n, 0, j], r1.at[n, 0, j], xn))
+            for j in range(2)
+        ]
+        return out + [
+            rem(p_ref.at[2 * (1 - y) + j, b], v1.at[n, 1, j], s1.at[n, 1, j], r1.at[n, 1, j], yn)
+            for j in range(2)
+        ]
+
+    def two(n):
+        return (
+            rem(q.at[n, 0], v2.at[n, 0], s2.at[n, 0], r2.at[n, 0], yn),
+            rem(q.at[n, 1], v2.at[n, 1], s2.at[n, 1], r2.at[n, 1], xn),
+        )
+
+    greet(fs, ep, z)
+    for n in range(parts):
+        for copy in one(n):
+            copy.start()
+    for n in range(parts):
+        a, b = band(n, 0), band(n, 1)
+        copies = one(n)
+        for copy in copies[:2]:
+            copy.wait_recv()
+        q[n, 0] = p_ref[2 * (1 - y) + x, a] + v1[n, 0, 1 - y]
+        two(n)[0].start()
+        for copy in copies[2:]:
+            copy.wait_recv()
+        q[n, 1] = p_ref[2 * y + 1 - x, b] + v1[n, 1, 1 - x]
+        two(n)[1].start()
+        out_ref[a, :] = p_ref[fs, a].astype(F32) + v1[n, 0, y].astype(F32)
+        out_ref[b, :] = p_ref[fs, b].astype(F32) + v1[n, 1, x].astype(F32)
+    for n in range(parts):
+        for half in range(2):
+            at = band(n, half)
+            two(n)[half].wait_recv()
+            out_ref[at, :] += v2[n, half].astype(F32)
+    for n in range(parts):
+        for copy in (*one(n), *two(n)):
+            copy.wait_send()
+
+
+def group_sum(part, cid, parts=2):
+    _, rows, width = part.shape
+    near = pl.BlockSpec(memory_space=pltpu.VMEM)
+    D = pltpu.SemaphoreType.DMA
+    step = rows // (2 * parts)
+    V = pltpu.VMEM
+    return pl.pallas_call(
+        partial(group_sum_kernel, parts),
+        out_shape=jax.ShapeDtypeStruct((rows, width), F32),
+        in_specs=[near],
+        out_specs=near,
+        scratch_shapes=[
+            V((parts, 2, step, width), BF), V((parts, 2, 2, step, width), BF), V((parts, 2, step, width), BF),
+            D((parts, 2, 2)), D((parts, 2, 2)), D((parts, 2)), D((parts, 2)),
+        ],
+        compiler_params=pltpu.CompilerParams(
+            collective_id=cid, has_side_effects=True, vmem_limit_bytes=32 * 1024 * 1024
+        ),
+        name="group_sum",
+    )(part)
+
+
+def weight_grads_kernel(xs, eg, mid, ug, gg, down, gate, up, rows, left, out, r_sem, l_sem, o_sem):
+    width = xs.shape[2]
+    jobs = [(k, w) for k in range(2) for w in range(3)]
+    lefts, outs = (mid, gg, ug), (down, gate, up)
+
+    def load_rows(n):
+        return pltpu.make_async_copy((eg, xs)[n % 2].at[n // 2], rows.at[n % 2], r_sem.at[n % 2])
+
+    def load_left(j):
+        k, w = jobs[j]
+        return pltpu.make_async_copy(lefts[w].at[k], left.at[j % 2], l_sem.at[j % 2])
+
+    def store(j):
+        k, w = jobs[j]
+        return pltpu.make_async_copy(out.at[j % 2], outs[w].at[k], o_sem.at[j % 2])
+
+    load_rows(0).start()
+    load_left(0).start()
+    load_rows(1).start()
+    for j, (k, w) in enumerate(jobs):
+        if j + 1 < len(jobs):
+            load_left(j + 1).start()
+        load_left(j).wait()
+        if w < 2:
+            load_rows(2 * k + w).wait()
+        if j >= 2:
+            store(j - 2).wait()
+        right = rows.at[min(w, 1)]
+        for lo, n in strips(width, 768):
+            out[j % 2, :, lo : lo + n] = tn(left[j % 2], right[:, lo : lo + n])
+        store(j).start()
+        if k == 0 and w in (0, 2):
+            load_rows(2 + (w > 0)).start()
+    for j in (len(jobs) - 2, len(jobs) - 1):
+        store(j).wait()
+
+
+def weight_grads(xs, eg, mid, ug, gg):
+    _, n, width = xs.shape
+    ff = mid.shape[2]
+    free = pl.BlockSpec(memory_space=pl.ANY)
+    D = pltpu.SemaphoreType.DMA
+    return pl.pallas_call(
+        weight_grads_kernel,
+        out_shape=[jax.ShapeDtypeStruct((2, ff, width), F32)] * 3,
+        in_specs=[free] * 5,
+        out_specs=[free] * 3,
+        scratch_shapes=[
+            pltpu.VMEM((2, n, width), BF), pltpu.VMEM((2, n, ff), BF), pltpu.VMEM((2, ff, width), F32),
+            D((2,)), D((2,)), D((2,)),
+        ],
+        compiler_params=pltpu.CompilerParams(vmem_limit_bytes=60 * 1024 * 1024),
+        cost_estimate=pl.CostEstimate(
+            flops=12 * n * ff * width, bytes_accessed=100_000_000, transcendentals=0
+        ),
+        name="weight_grads",
+    )(xs, eg, mid, ug, gg)
 
 
 def this_slice(
@@ -1078,11 +1300,9 @@
     )
     extra = -(-small.shape[0] // (16 * width)) * 16
     small = jnp.pad(small, (0, extra * width - small.shape[0])).reshape(extra, width)
-    packed, w_qkv = start_exchange(
-        jnp.concatenate([tokens, small], axis=0), w_query, w_key, w_value, 4
-    )
-    x_group = packed[:, :rows].reshape(fs_size * rows, width).astype(F32)
-    small = packed[:, rows:].reshape(fs_size, -1)
+    x_group, small, w_qkv = start_exchange(tokens, small, w_query, w_key, w_value, 4)
+    x_group = x_group.reshape(fs_size * rows, width).astype(F32)
+    small = small.reshape(fs_size, -1)
     gain_one = small[:, :shard].reshape(-1).astype(F32)
     gain_two = small[:, shard : 2 * shard].reshape(-1).astype(F32)
     bo = small[:, 2 * shard : 3 * shard].reshape(-1).astype(F32)
@@ -1098,7 +1318,8 @@
 
     x_float = tokens.astype(jnp.float32)
     scale_one = norm_scale(x_float)
-    norm_attn = (x_group * norm_scale(x_group) * gain_one).astype(jnp.bfloat16)
+    scale_group = norm_scale(x_group)
+    norm_attn = (x_group * scale_group * gain_one).astype(jnp.bfloat16)
     segment_ids, position = jax.vmap(lambda own: layout(own, rows))(lengths)
     cosine_table, sine_table = tables(position.reshape(-1), HEAD_SIZE // 2)
     qkv = jnp.dot(norm_attn, w_qkv, preferred_element_type=jnp.float32) + b_qkv
@@ -1132,7 +1353,8 @@
     mixed = mm("bhgqk,bkhd->bqhgd", probs_b, value).astype(jnp.bfloat16)
     mixed = mixed.reshape(many, q_cols)
     out_part = jnp.dot(mixed, w_out, preferred_element_type=jnp.float32)
-    resid = x_float + scatter_fs(out_part.astype(jnp.bfloat16)).astype(jnp.float32) + bo
+    out_part = out_part.astype(BF).reshape(fs_size, rows, width)
+    resid = x_float + group_sum(out_part, 5) + bo
     scale_two = norm_scale(resid)
     norm_ffn = (resid * scale_two * gain_two).astype(jnp.bfloat16)
 
@@ -1177,9 +1399,11 @@
     )
     sums = scatter_blocks([out_part, row_part], 2)
     block_out = resid + sums[0, :, :width].astype(F32)
-    grad_w_down = mm("erf,erd->efd", middle, expert_grad)
-    grad_w_gate = jnp.swapaxes(mm("erf,erd->efd", gate_grad_pre, x_slots), 1, 2)
-    grad_w_up = jnp.swapaxes(mm("erf,erd->efd", up_grad, x_slots), 1, 2)
+    grad_w_down, gate_t, up_t = weight_grads(
+        x_slots, expert_grad, middle, up_grad, gate_grad_pre
+    )
+    grad_w_gate = jnp.swapaxes(gate_t, 1, 2)
+    grad_w_up = jnp.swapaxes(up_t, 1, 2)
     row_sum = sums[1].astype(F32)
     gate_grad = row_sum[:, width : width + expert_count]
     logit_grad = gates_here * (
@@ -1215,10 +1439,10 @@
         [query_pre_grad, key_pre_grad, value_grad.reshape(many, kv_cols)], axis=1
     ).astype(jnp.bfloat16)
     grad_b_qkv = jnp.sum(qkv_grad, axis=0, dtype=jnp.float32)
-    norm_attn_grad = scatter_fs(
-        mm("tf,df->td", qkv_grad, w_qkv).astype(jnp.bfloat16)
-    ).astype(jnp.float32)
-    input_norm_grad, grad_gain_one = norm_back(x_float, scale_one, gain_one, norm_attn_grad)
+    part = mm("tf,df->td", qkv_grad, w_qkv)
+    grad_gain_one = jnp.sum(part * (x_group * scale_group), axis=0)
+    norm_attn_grad = scatter_fs(part.astype(BF)).astype(F32)
+    input_norm_grad, _ = norm_back(x_float, scale_one, gain_one, norm_attn_grad)
     grad_tokens = resid_grad + input_norm_grad
     by_shard = jnp.concatenate(
         [
@@ -1233,24 +1457,21 @@
         [grad_b_qkv, grad_sink, lax.dynamic_slice_in_dim(grad_bo, my_fs * shard, shard)]
     ).astype(BF)
     cols = q_cols + 2 * kv_cols
-    slab_rows, slab_part = 768, 128
+    slab_rows = 768
     wide_part = 144
     own = jnp.where(jnp.arange(fs_size)[:, None] == my_fs, own, jnp.zeros((), BF))
     by_shard = jnp.concatenate([by_shard, own], axis=1)
     small_n = by_shard.shape[1]
     small_rows = -(-small_n // q_cols)
     by_shard = jnp.pad(by_shard, ((0, 0), (0, small_rows * q_cols - small_n)))
-    norm_pad = jnp.pad(
-        norm_attn.reshape(many, fs_size, shard), ((0, 0), (0, 0), (0, slab_rows - shard))
-    ).reshape(many, fs_size * slab_rows)
-    gq = left_dot(norm_pad, qkv_grad).astype(BF).reshape(fs_size, slab_rows, cols)
-    gq = gq.at[:, shard : shard + small_rows, :q_cols].set(
-        by_shard.reshape(fs_size, small_rows, q_cols)
-    )
-    gq = gq.reshape(fs_size, 2, slab_rows // (2 * slab_part), slab_part, cols)
+    by_shard = jnp.pad(
+        by_shard.reshape(fs_size, small_rows, q_cols),
+        ((0, 0), (0, slab_rows - shard - small_rows), (0, cols - q_cols)),
+    )
+    gq = left_dot(norm_attn, qkv_grad).astype(BF).reshape(fs_size, shard, cols)
     gw = left_dot(branch_grad, mixed).astype(BF)
     gw = gw.reshape(2, width // (2 * wide_part), wide_part, q_cols)
-    tw, tq, tk, tv = reduce_parts(gw, gq, (q_cols, kv_cols, kv_cols), 3)
+    tw, tq, tk, tv = reduce_parts(gw, gq, by_shard, 3, (q_cols, kv_cols, kv_cols), 3)
     sum_wo = jnp.swapaxes(tw.reshape(width, q_cols).astype(F32), 0, 1)
     sum_wq = tq[:shard].astype(F32)
     sum_wk = tk[:shard].astype(F32)

time: 1090 us -> 992 us (0.910)
  matrix products: 119 us -> 62.1 us
  waiting for transfers between devices: 26.5 us -> 0.06 us
  Pallas kernels: 780 us -> 801 us
  local copies, waits for them, and re-layouts: 77.1 us -> 61 us
  other arithmetic: 60.3 us -> 44.6 us
    pallas_call x0 -> x2, Pallas kernels: none -> 78.1 us  [the longest x1 50.6 us: weight_grads(): pl.pallas_call(weight_grads_kernel, out_shape=[jax.ShapeDtypeStruct((2, f...]
    dot_general x11 -> x8, matrix products: 90.4 us -> 27.6 us  [mm(): return jnp.einsum(spec, left, right, preferred_element_type=jnp.float32)]
    pallas_call x1, Pallas kernels: 287 us -> 242 us  [experts(): pl.pallas_call(partial(experts_kernel, cap, width), out_shape=[shape((2,...]
    reduce_scatter x2 -> x1, waiting for transfers between devices: 20.6 us -> 0.01 us  [scatter_fs(): return lax.psum_scatter(value, 'fs', scatter_dimension=0, tiled=True)]
    pallas_call x1, Pallas kernels: 86.7 us -> 66.3 us  [start_exchange(): pl.pallas_call(partial(start_kernel, splits), out_shape=[jax.ShapeDtypeSt...]
    convert_element_type x4 -> x3, local copies, waits for them, and re-layouts: 26 us -> 11.5 us  [the longest x1 4.57 us: this_slice(): norm_attn_grad = scatter_fs(part.astype(BF)).astype(F32)]
  transfers between devices with their start and end apart: 3 -> 2, of which waited for: 3 -> 0; matrix products, arithmetic and copies ran while one was open for 11% -> 6% of each run, Pallas kernels for 0% -> 25%
where the time goes in v3:
time: 992 us; the launch traced here: 984 us
  Pallas kernels  801 us (81%)
  matrix products  62.1 us (6%)
  local copies, waits for them, and re-layouts  61 us (6%)
  other arithmetic  44.6 us (4%)
  between operations  15.5 us (2%)
    pallas_call x1, Pallas kernels, experts(): pl.pallas_call(partial(experts_kernel, cap, width), out_shape=[shape((2,...  242 us
    pallas_call x1, Pallas kernels, scatter_blocks(): pl.pallas_call(partial(scatter_kernel, na, parts), out_shape=[jax.ShapeDt...  219 us
    pallas_call x1, Pallas kernels, reduce_parts(): pl.pallas_call(partial(reduce_kernel, wide_n, slab_n, splits), out_shape=...  195 us
    pallas_call x1, Pallas kernels, start_exchange(): pl.pallas_call(partial(start_kernel, splits), out_shape=[jax.ShapeDtypeSt...  66.3 us
    pallas_call x1, Pallas kernels, weight_grads(): pl.pallas_call(weight_grads_kernel, out_shape=[jax.ShapeDtypeStruct((2, f...  50.6 us
    dot_general x8, matrix products, mm(): return jnp.einsum(spec, left, right, preferred_element_type=jnp.float32)  27.6 us
    pallas_call x1, Pallas kernels, group_sum(): pl.pallas_call(partial(group_sum_kernel, parts), out_shape=jax.ShapeDtype...  27.5 us
  transfers between devices with their start and end apart: 2, of which 0 were waited for; matrix products, arithmetic and copies ran while one was open for 6% of the time, Pallas kernels for 25%

profile of v3, /device:TPU:0, one launch (start us, length us, event | category | flops | bytes accessed | tf_op | source)
XLA Modules:
  0.0 984.5 jit_solution(14204717875086894573)
XLA Ops:
  7.2 2.3 copy.138.own
  11.2 2.8 concatenate.53
  14.8 66.3 %start_exchange.1 = (bf16[4,128,2880]{2,1,0:T(8,128)(2,1)}, bf16[4,16,2880]{2,1,0:T(8,128)(2,1)}, bf16[4,720,1280]{2,1,0:T(8,128)(2,1)}) custom-call(bf16[128,2880]{1,0:T(8,128)(2,1)} %copy.138.own, bf16[16,2880]{1,0:T(8,128)(2,1)} %reshape.397.few, bf16[720,4096]{1,0:T(8,128)(2,1)} %wq.1, bf16[720,512]{1,0:T(8,128)(2,1)} %wk.1, bf16[720,512]{1,0:T(8,128)(2,1)} %wv.1), custom_call_target="tpu_custom_call" | custom-call | tf_op jit(solution)/shard_map/start_exchange/pallas_call | solution.py:690
  81.2 1.5 reshape.398
  82.9 2.5 multiply_reduce_fusion
  87.1 7.3 convolution_add_fusion.1
  95.6 2.0 copy.147
  97.9 1.9 add_convert_fusion.1
  101.6 1.9 copy-done.1
  103.5 1.2 fusion.4
  105.0 3.5 fusion.15
  110.4 7.3 convolution_convert_fusion.2
  117.7 3.3 copy.153
  121.1 27.5 %group_sum.1 = f32[128,2880]{1,0:T(8,128)S(1)} custom-call(bf16[4,128,2880]{2,1,0:T(8,128)(2,1)S(1)} %bitcast.160), custom_call_target="tpu_custom_call" | custom-call | tf_op jit(solution)/shard_map/group_sum/pallas_call | solution.py:1183
  148.5 1.1 copy-done
  149.7 1.9 multiply_reduce_fusion.4
  154.3 1.5 copy.158
  159.6 242.5 %experts.1 = (bf16[2,4,8,128,2944]{4,3,2,1,0:T(8,128)(2,1)}, bf16[4,8,128,2944]{3,2,1,0:T(8,128)(2,1)}, bf16[4,8,128,2944]{3,2,1,0:T(8,128)(2,1)}, bf16[2,4,8,48...) custom-call(bf16[128,2944]{1,0:T(8,128)(2,1)} %concatenate.61.n_own,, ...), custom_call_target="tpu_custom_call" | custom-call | flops 76441190400 | bytes 300000000 | tf_op jit(solution)/shard_map/experts/pallas_call | solution.py:1089
  402.0 219.0 %scatter_blocks.1 = (bf16[2,128,2944]{2,1,0:T(8,128)(2,1)}, bf16[16,4,64,2944]{3,2,1,0:T(8,128)(2,1)}) custom-call(bf16[4,8,128,2944]{3,2,1,0:T(8,128)(2,1)} %get-tuple-element.45.refs_0_, bf16[4,8,128,2944]{3,2,1,0:T(8,128)(2,1)} %get-tuple-element.46.refs_1_), custom_call_target="tpu_custom_call" | custom-call | tf_op jit(solution)/shard_map/scatter_blocks/pallas_call | solution.py:266
  621.1 1.4 bitcast_convert_fusion
  624.0 2.2 fusion.44
  626.2 1.5 convolution_convert_fusion.3
  627.7 1.2 copy.173
  628.9 2.3 reshape.414
  631.2 3.6 copy.172
  635.0 2.3 copy.174
  639.1 50.6 %weight_grads.1 = (f32[2,720,2880]{2,1,0:T(8,128)}, f32[2,720,2880]{2,1,0:T(8,128)}, f32[2,720,2880]{2,1,0:T(8,128)}) custom-call(bf16[2,1536,2880]{2,1,0:T(8,128)(2,1)} %bitcast.191, bf16[2,1536,2880]{2,1,0:T(8,128)(2,1)} %bitcast.192, bf16[2,1536,720]{2,1,0:T(8,128)(2,1)} %bitcast.195, bf16[2,1536,720]{2,1,0:T(8,128)(2,1)} %bitcast.196, ...), custom_call_target="tpu_custom_call" | custom-call | flops 38220595200 | bytes 100000000 | tf_op jit(solution)/shard_map/weight_grads/pallas_call | solution.py:1241
  689.7 7.0 convolution_convert_fusion.4
  696.8 1.3 reshape.446
  698.1 1.9 copy.163
  700.1 3.8 fusion
  704.1 1.8 fusion.2
  708.0 1.9 fusion.19
  710.0 2.7 copy.165
  712.7 2.1 reshape.407
  716.3 9.4 multiply_reduce_fusion.1
  725.7 4.6 copy.171
  730.3 2.5 convert_reduce_fusion
  733.0 7.5 convolution_convert_fusion.1
  741.7 9.8 convolution_convert_fusion
  751.5 195.2 %reduce_parts.1 = (bf16[2,10,144,1024]{3,2,1,0:T(8,128)(2,1)}, bf16[768,4096]{1,0:T(8,128)(2,1)}, bf16[768,512]{1,0:T(8,128)(2,1)}, bf16[768,512]{1,0:T(8,128)(2,1)}) custom-call(bf16[2,10,144,1024]{3,2,1,0:T(8,128)(2,1)} %bitcast.164, bf16[4,720,1280]{2,1,0:T(8,128)(2,1)} %bitcast.163, bf16[4,48,1280]{2,1,0:T(8,128)(2,1)} %pad.19.gs), custom_call_target="tpu_custom_call" | custom-call | bytes 500000000 | tf_op jit(solution)/shard_map/reduce_parts/pallas_call | solution.py:548
  952.2 1.3 slice_convert_fusion.1
  953.5 1.3 slice_convert_fusion.2
  954.8 9.1 convert_bitcast_fusion
  964.0 6.1 slice_convert_fusion
  970.1 1.6 fusion.9
  971.7 2.7 fusion.12
  974.4 2.9 copy.175
  (230 shorter events, 30.1 us)
Async XLA Ops:
  7.2 682.5 %all-gather.2.cloned.1.call-start = ((), (), s32[]{:S(2)}) async-start(), calls=%async_computation.1 | async-start | bytes 3768320 | tf_op jit(solution)/shard_map/all_gather | solution.py:100
  81.2 4.9 copy-start.3
  82.9 4.1 copy-start.36
  97.9 2.0 copy-start.14
  97.9 2.0 copy-start.16
  97.9 2.3 copy-start.58
  100.3 4.4 copy-start.44
  100.5 4.2 copy-start.11
  100.7 4.3 copy-start.21
  101.5 2.0 copy-start.1
  101.5 3.2 copy-start.29
  101.6 7.0 copy-start.32
  104.7 3.8 copy-start.34
  104.8 3.7 copy-start.38
  105.0 3.6 copy-start.40
  149.6 3.3 copy-start.52
  151.6 4.1 copy-start.5
  153.5 6.1 copy-start.8
  153.5 3.2 copy-start.43
  153.5 3.8 copy-start.50
  153.5 4.4 copy-start.51
  402.0 220.8 %copy-start.49 = (f32[128]{0:T(128)S(1)}, f32[128]{0:T(128)}, u32[]{:S(2)}) copy-start(f32[128]{0:T(128)} %copy-done.48) | copy-start | bytes 1540
  621.1 1.8 copy-start.10
  626.1 5.1 copy-start.4
  626.1 344.0 %reduce-scatter.2.cloned.1.call-start = ((), (), s32[]{:S(2)}) async-start(), calls=%async_computation.2 | async-start | bytes 3768320 | tf_op jit(solution)/shard_map/reduce_scatter | solution.py:104
  631.2 6.0 copy-start.42
  631.2 6.7 copy-start.47
  631.2 7.3 copy-start.46
  696.7 3.3 copy-start.22
  696.7 3.3 copy-start.33
  696.8 3.3 copy-start.39
  700.1 3.8 copy-start.30
  700.1 3.8 copy-start.35
  700.1 3.8 copy-start.45
  700.1 4.0 copy-start.2
  704.1 1.8 copy-start.26
  704.1 1.8 copy-start.28
  712.7 2.1 copy-start.15
  712.7 2.2 copy-start.17
  730.3 2.7 copy-start.20
  733.0 7.7 copy-start.31
  733.0 8.8 copy-start.37
  946.7 5.5 copy-start.24
  946.7 6.8 copy-start.23
  953.5 10.4 %slice-start = ((s8[6291456]{0:T(1024)(128)(4,1)}), s8[4194304]{0:T(1024)(128)(4,1)S(1)}, s32[]{:S(2)}) async-start(s8[6291456]{0:T(1024)(128)(4,1)} %bitcast.165), calls=%async_computation.3 | async-start | bytes 8388608
  954.8 9.1 slice-start.1
  964.0 6.2 copy-start.7
  964.0 7.7 copy-start.13
  (15 other events, 18.3 us)
Sparse Core Ops, SparseCore 0:
  626.3 54.7 all-gather.1
  730.4 63.4 reduce-scatter.1

commit v4 on v3

--- a/solution.py
+++ b/solution.py
@@ -1118,7 +1118,7 @@
     return (*out[1:3], *saved, *(total[:, 0] for total in out[10:]))
 
 
-def group_sum_kernel(parts, p_ref, out_ref, q, v1, v2, s1, r1, s2, r2):
+def project_sum_kernel(parts, m_ref, w_ref, out_ref, p_ref, q, v1, v2, s1, r1, s2, r2):
     fs, ep, y, x, z, c = spot()
     rows = p_ref.shape[1]
     step = rows // (2 * parts)
@@ -1147,10 +1147,35 @@
             rem(q.at[n, 1], v2.at[n, 1], s2.at[n, 1], r2.at[n, 1], xn),
         )
 
+    def project(dev):
+        m = m_ref[dev]
+        for lo, n in strips(w_ref.shape[0], 768):
+            p_ref[dev, :, lo : lo + n] = nt(m, w_ref[lo : lo + n, :]).astype(BF)
+
+    def send(dx, dy):
+        for n in range(parts):
+            copies = one(n)
+            for j in range(2):
+                if dx:
+
+                    @pl.when(y == (j + dy) % 2)
+                    def _():
+                        copies[j].start()
+
+                if dy:
+
+                    @pl.when(x == (j + dx) % 2)
+                    def _():
+                        copies[2 + j].start()
+
+    project(3 - fs)
     greet(fs, ep, z)
-    for n in range(parts):
-        for copy in one(n):
-            copy.start()
+    send(1, 1)
+    project(2 * y + 1 - x)
+    send(1, 0)
+    project(2 * (1 - y) + x)
+    send(0, 1)
+    project(fs)
     for n in range(parts):
         a, b = band(n, 0), band(n, 1)
         copies = one(n)
@@ -1174,26 +1199,31 @@
             copy.wait_send()
 
 
-def group_sum(part, cid, parts=2):
-    _, rows, width = part.shape
+def project_sum(mixed, w_t, cid, parts=2):
+    _, rows, features = mixed.shape
+    width = w_t.shape[0]
     near = pl.BlockSpec(memory_space=pltpu.VMEM)
     D = pltpu.SemaphoreType.DMA
     step = rows // (2 * parts)
     V = pltpu.VMEM
     return pl.pallas_call(
-        partial(group_sum_kernel, parts),
+        partial(project_sum_kernel, parts),
         out_shape=jax.ShapeDtypeStruct((rows, width), F32),
-        in_specs=[near],
+        in_specs=[near, near],
         out_specs=near,
         scratch_shapes=[
-            V((parts, 2, step, width), BF), V((parts, 2, 2, step, width), BF), V((parts, 2, step, width), BF),
+            V((4, rows, width), BF), V((parts, 2, step, width), BF),
+            V((parts, 2, 2, step, width), BF), V((parts, 2, step, width), BF),
             D((parts, 2, 2)), D((parts, 2, 2)), D((parts, 2)), D((parts, 2)),
         ],
         compiler_params=pltpu.CompilerParams(
-            collective_id=cid, has_side_effects=True, vmem_limit_bytes=32 * 1024 * 1024
+            collective_id=cid, has_side_effects=True, vmem_limit_bytes=40 * 1024 * 1024
         ),
-        name="group_sum",
-    )(part)
+        cost_estimate=pl.CostEstimate(
+            flops=8 * rows * features * width, bytes_accessed=20_000_000, transcendentals=0
+        ),
+        name="project_sum",
+    )(mixed, w_t)
 
 
 def weight_grads_kernel(xs, eg, mid, ug, gg, down, gate, up, rows, left, out, r_sem, l_sem, o_sem):
@@ -1352,9 +1382,10 @@
     probs_b = probs.astype(jnp.bfloat16)
     mixed = mm("bhgqk,bkhd->bqhgd", probs_b, value).astype(jnp.bfloat16)
     mixed = mixed.reshape(many, q_cols)
-    out_part = jnp.dot(mixed, w_out, preferred_element_type=jnp.float32)
-    out_part = out_part.astype(BF).reshape(fs_size, rows, width)
-    resid = x_float + group_sum(out_part, 5) + bo
+    projected = project_sum(
+        mixed.reshape(fs_size, rows, q_cols), jnp.swapaxes(w_out, 0, 1), 5
+    )
+    resid = x_float + projected + bo
     scale_two = norm_scale(resid)
     norm_ffn = (resid * scale_two * gain_two).astype(jnp.bfloat16)
 

time: 992 us -> 986 us (level)
  no operation moved by 1% of the time
where the time goes in v4:
time: 986 us; the launch traced here: 979 us
  Pallas kernels  803 us (81%)
  local copies, waits for them, and re-layouts  61.7 us (6%)
  matrix products  54.9 us (6%)
  other arithmetic  43.1 us (4%)
  between operations  15.7 us (2%)
    pallas_call x1, Pallas kernels, experts(): pl.pallas_call(partial(experts_kernel, cap, width), out_shape=[shape((2,...  243 us
    pallas_call x1, Pallas kernels, scatter_blocks(): pl.pallas_call(partial(scatter_kernel, na, parts), out_shape=[jax.ShapeDt...  219 us
    pallas_call x1, Pallas kernels, reduce_parts(): pl.pallas_call(partial(reduce_kernel, wide_n, slab_n, splits), out_shape=...  194 us
    pallas_call x1, Pallas kernels, start_exchange(): pl.pallas_call(partial(start_kernel, splits), out_shape=[jax.ShapeDtypeSt...  66.3 us
    pallas_call x1, Pallas kernels, weight_grads(): pl.pallas_call(weight_grads_kernel, out_shape=[jax.ShapeDtypeStruct((2, f...  51.3 us
    pallas_call x1, Pallas kernels, project_sum(): pl.pallas_call(partial(project_sum_kernel, parts), out_shape=jax.ShapeDty...  29.5 us
    dot_general x8, matrix products, mm(): return jnp.einsum(spec, left, right, preferred_element_type=jnp.float32)  27.6 us
    unnamed x135, local copies, waits for them, and re-layouts  19.8 us
  transfers between devices with their start and end apart: 2, of which 0 were waited for; matrix products, arithmetic and copies ran while one was open for 6% of the time, Pallas kernels for 25%

profile of v4, /device:TPU:0, one launch (start us, length us, event | category | flops | bytes accessed | tf_op | source)
XLA Modules:
  0.0 978.8 jit_solution(15525184302347001176)
XLA Ops:
  7.2 2.3 copy.138.own
  11.3 2.8 concatenate.53
  14.9 66.3 %start_exchange.1 = (bf16[4,128,2880]{2,1,0:T(8,128)(2,1)}, bf16[4,16,2880]{2,1,0:T(8,128)(2,1)}, bf16[4,720,1280]{2,1,0:T(8,128)(2,1)}) custom-call(bf16[128,2880]{1,0:T(8,128)(2,1)} %copy.138.own, bf16[16,2880]{1,0:T(8,128)(2,1)} %reshape.394.few, bf16[720,4096]{1,0:T(8,128)(2,1)} %wq.1, bf16[720,512]{1,0:T(8,128)(2,1)} %wk.1, bf16[720,512]{1,0:T(8,128)(2,1)} %wv.1), custom_call_target="tpu_custom_call" | custom-call | tf_op jit(solution)/shard_map/start_exchange/pallas_call | solution.py:690
  81.2 1.5 reshape.395
  83.0 2.5 multiply_reduce_fusion
  87.1 7.3 convolution_add_fusion.1
  95.6 2.0 copy.147
  98.0 1.9 add_convert_fusion.1
  101.7 1.9 copy-done.1
  103.6 1.2 fusion.4
  105.4 3.5 convolution_convert_fusion.4
  109.9 2.7 copy-done
  112.6 29.5 %project_sum.1 = f32[128,2880]{1,0:T(8,128)S(1)} custom-call(bf16[4,128,1024]{2,1,0:T(8,128)(2,1)S(1)} %copy.152.m_ref, bf16[2880,1024]{1,0:T(8,128)(2,1)S(1)} %bitcast.158), custom_call_target="tpu_custom_call" | custom-call | flops 3019898880 | bytes 20000000 | tf_op jit(solution)/shard_map/project_sum/pallas_call | solution.py:1209
  145.1 1.5 copy.157
  149.3 1.0 concatenate.61.n_own
  150.4 243.3 %experts.1 = (bf16[2,4,8,128,2944]{4,3,2,1,0:T(8,128)(2,1)}, bf16[4,8,128,2944]{3,2,1,0:T(8,128)(2,1)}, bf16[4,8,128,2944]{3,2,1,0:T(8,128)(2,1)}, bf16[2,4,8,48...) custom-call(bf16[128,2944]{1,0:T(8,128)(2,1)} %concatenate.61.n_own,, ...), custom_call_target="tpu_custom_call" | custom-call | flops 76441190400 | bytes 300000000 | tf_op jit(solution)/shard_map/experts/pallas_call | solution.py:1089
  393.7 219.3 %scatter_blocks.1 = (bf16[2,128,2944]{2,1,0:T(8,128)(2,1)}, bf16[16,4,64,2944]{3,2,1,0:T(8,128)(2,1)}) custom-call(bf16[4,8,128,2944]{3,2,1,0:T(8,128)(2,1)} %get-tuple-element.45.refs_0_, bf16[4,8,128,2944]{3,2,1,0:T(8,128)(2,1)} %get-tuple-element.46.refs_1_), custom_call_target="tpu_custom_call" | custom-call | tf_op jit(solution)/shard_map/scatter_blocks/pallas_call | solution.py:266
  613.0 1.4 bitcast_convert_fusion
  615.9 2.2 fusion.41
  618.2 1.5 convolution_convert_fusion.2
  619.7 1.2 copy.173
  620.8 2.3 reshape.410
  623.2 3.4 copy.172
  626.8 3.1 copy.171
  629.9 2.3 copy.174
  634.0 51.3 %weight_grads.1 = (f32[2,720,2880]{2,1,0:T(8,128)}, f32[2,720,2880]{2,1,0:T(8,128)}, f32[2,720,2880]{2,1,0:T(8,128)}) custom-call(bf16[2,1536,2880]{2,1,0:T(8,128)(2,1)} %bitcast.190, bf16[2,1536,2880]{2,1,0:T(8,128)(2,1)} %bitcast.191, bf16[2,1536,720]{2,1,0:T(8,128)(2,1)} %bitcast.194, bf16[2,1536,720]{2,1,0:T(8,128)(2,1)} %bitcast.195, ...), custom_call_target="tpu_custom_call" | custom-call | flops 38220595200 | bytes 100000000 | tf_op jit(solution)/shard_map/weight_grads/pallas_call | solution.py:1271
  685.3 7.0 convolution_convert_fusion.3
  692.4 1.3 reshape.442
  693.7 2.0 copy.162
  695.8 3.8 fusion
  699.8 1.8 fusion.2
  703.6 1.9 fusion.18
  705.7 2.7 copy.164
  708.4 2.1 reshape.402
  712.0 9.4 multiply_reduce_fusion.1
  721.3 4.6 copy.170
  725.9 2.5 convert_reduce_fusion
  728.6 7.5 convolution_convert_fusion.1
  737.4 9.8 %convolution_convert_fusion = bf16[2880,1280]{1,0:T(8,128)(2,1)} fusion(f32[512,2880]{0,1:T(8,128)} %copy.172, f32[2880]{0:T(1024)S(1)} %copy-done.38, f32[512]{0:T(512)S(1)} %copy-done.54, bf16[512,128]{0,1:T(8,128)(2,1)S(1)} %bitcast.176, bf16[512,128]{0,1:T(8,128)(2,1)S(1)} %bitcast.179, bf16[512,1024]{0,1:T(8,128)(2,1)S(1)} %bitcast.167), kind=kOutput, calls=%fused_computation.1 | convolution fusion | flops 3786915840 | bytes 14595328 | tf_op jit(solution)/shard_map/dot_general | solution.py:84
  747.2 193.6 %reduce_parts.1 = (bf16[2,10,144,1024]{3,2,1,0:T(8,128)(2,1)}, bf16[768,4096]{1,0:T(8,128)(2,1)}, bf16[768,512]{1,0:T(8,128)(2,1)}, bf16[768,512]{1,0:T(8,128)(2,1)}) custom-call(bf16[2,10,144,1024]{3,2,1,0:T(8,128)(2,1)} %bitcast.162, bf16[4,720,1280]{2,1,0:T(8,128)(2,1)} %bitcast.161, bf16[4,48,1280]{2,1,0:T(8,128)(2,1)} %pad.19.gs), custom_call_target="tpu_custom_call" | custom-call | bytes 500000000 | tf_op jit(solution)/shard_map/reduce_parts/pallas_call | solution.py:548
  940.8 1.0 slice_convert_fusion.4
  946.3 1.3 slice_convert_fusion.1
  947.6 1.3 slice_convert_fusion.2
  948.9 9.1 convert_bitcast_fusion
  958.0 6.1 slice_convert_fusion
  964.2 1.6 fusion.9
  965.8 2.7 fusion.12
  968.5 2.9 copy.175
  (231 shorter events, 27.7 us)
Async XLA Ops:
  7.2 678.1 %all-gather.2.cloned.1.call-start = ((), (), s32[]{:S(2)}) async-start(), calls=%async_computation.1 | async-start | bytes 3768320 | tf_op jit(solution)/shard_map/all_gather | solution.py:100
  81.2 4.9 copy-start.3
  83.0 4.1 copy-start.37
  97.9 2.0 copy-start.16
  97.9 2.0 copy-start.18
  98.0 2.3 copy-start.59
  100.4 4.4 copy-start.45
  100.6 4.2 copy-start.12
  100.8 4.7 copy-start.22
  101.6 2.0 copy-start.1
  101.6 3.5 copy-start.30
  101.7 7.3 copy-start.33
  104.9 4.0 copy-start.39
  105.4 3.5 copy-start.41
  109.9 2.7 copy-start
  112.6 29.5 %copy-start.7 = (bf16[128,2880]{1,0:T(8,128)(2,1)S(1)}, bf16[128,2880]{1,0:T(8,128)(2,1)}, u32[]{:S(2)}) copy-start(bf16[128,2880]{1,0:T(8,128)(2,1)} %copy.138.own) | copy-start | bytes 2211844
  142.5 4.1 copy-start.5
  144.3 6.1 copy-start.9
  144.3 3.2 copy-start.44
  144.3 3.8 copy-start.51
  144.3 4.4 copy-start.52
  393.7 221.0 %copy-start.50 = (f32[128]{0:T(128)S(1)}, f32[128]{0:T(128)}, u32[]{:S(2)}) copy-start(f32[128]{0:T(128)} %copy-done.49) | copy-start | bytes 1540
  613.0 1.8 copy-start.11
  618.1 5.1 copy-start.4
  618.1 346.1 %reduce-scatter.2.cloned.1.call-start = ((), (), s32[]{:S(2)}) async-start(), calls=%async_computation.2 | async-start | bytes 3768320 | tf_op jit(solution)/shard_map/reduce_scatter | solution.py:104
  626.6 5.5 copy-start.43
  626.6 6.1 copy-start.48
  626.6 6.7 copy-start.47
  692.3 3.4 copy-start.23
  692.4 3.4 copy-start.34
  692.4 3.4 copy-start.40
  695.7 3.8 copy-start.31
  695.7 3.8 copy-start.36
  695.8 3.8 copy-start.46
  695.8 4.0 copy-start.2
  699.8 1.8 copy-start.27
  699.8 1.8 copy-start.29
  708.4 2.1 copy-start.17
  708.4 2.2 copy-start.19
  725.9 2.7 copy-start.21
  728.6 7.7 copy-start.32
  728.6 8.8 copy-start.38
  940.8 5.5 copy-start.25
  940.8 6.8 copy-start.24
  947.6 10.4 %slice-start = ((s8[6291456]{0:T(1024)(128)(4,1)}), s8[4194304]{0:T(1024)(128)(4,1)S(1)}, s32[]{:S(2)}) async-start(s8[6291456]{0:T(1024)(128)(4,1)} %bitcast.163), calls=%async_computation.3 | async-start | bytes 8388608
  948.9 9.1 slice-start.1
  958.0 6.2 copy-start.8
  958.0 7.7 copy-start.14
  (16 other events, 18.8 us)
Sparse Core Ops, SparseCore 0:
  618.2 53.8 all-gather.1
  726.1 61.1 reduce-scatter.1

commit v5 on v4

--- a/solution.py
+++ b/solution.py
@@ -162,6 +162,8 @@
                 rem(q.at[i,y*2+1-x,B],v2.at[i,1],s2.at[i,1],r2.at[i,1],xn))
     def up(i): return rem(q.at[i,fs],vu.at[i],su.at[i],ru.at[i],(fs,ep+2))
     def down(i): return rem(q.at[i,fs],vd.at[i],sd.at[i],rd.at[i],(fs,ep-2))
+    def from_below(i): return rem(q.at[i,fs],vu.at[i],su.at[i],ru.at[i],(fs,ep-2))
+    def from_above(i): return rem(q.at[i,fs],vd.at[i],sd.at[i],rd.at[i],(fs,ep+2))
     greet(fs,ep,z)
     @pl.loop(0,items)
     def _(i):
@@ -219,7 +221,7 @@
             def _():
                 @pl.when(z>0)
                 def _():
-                    up(iu).wait_recv()
+                    from_below(iu).wait_recv()
                     q[iu,fs]=q[iu,fs]+vu[iu]
                 @pl.when(zz>z)
                 def _(): up(iu).start()
@@ -231,7 +233,7 @@
             def _():
                 @pl.when(z<3)
                 def _():
-                    down(idn).wait_recv()
+                    from_above(idn).wait_recv()
                     q[idn,fs]=q[idn,fs]+vd[idn]
                 @pl.when(zz<z)
                 def _(): down(idn).start()
@@ -749,6 +751,11 @@
         other = (self.fs, self.ep + (2 if up else -2))
         return remote(view, view, self.sz.at[a, zz, up], self.rz.at[a, zz], other)
 
+    def arriving(self, a, zz):
+        view = self.full.at[a, self.fs, zz * 2 + self.c]
+        other = (self.fs, self.ep + jnp.where(self.z == 0, 2, -2))
+        return remote(view, view, self.sz.at[a, zz, 0], self.rz.at[a, zz], other)
+
     def first(self, a, zz):
         e = zz * 2 + self.c
         v = self.full.at[a, self.fs, e, self.upper]
@@ -779,7 +786,7 @@
 
             @pl.when(zz != self.z)
             def _():
-                self.along(a, zz, 0).wait_recv()
+                self.arriving(a, zz).wait_recv()
 
             @pl.when((zz <= self.z) & (self.z < 3))
             def _():

time: 986 us -> 986 us (level)
  no operation moved by 1% of the time
where the time goes in v5:
time: 986 us; the launch traced here: 979 us
  Pallas kernels  803 us (81%)
  local copies, waits for them, and re-layouts  61.7 us (6%)
  matrix products  54.9 us (6%)
  other arithmetic  43.1 us (4%)
  between operations  15.7 us (2%)
    pallas_call x1, Pallas kernels, experts(): pl.pallas_call(partial(experts_kernel, cap, width), out_shape=[shape((2,...  243 us
    pallas_call x1, Pallas kernels, scatter_blocks(): pl.pallas_call(partial(scatter_kernel, na, parts), out_shape=[jax.ShapeDt...  219 us
    pallas_call x1, Pallas kernels, reduce_parts(): pl.pallas_call(partial(reduce_kernel, wide_n, slab_n, splits), out_shape=...  194 us
    pallas_call x1, Pallas kernels, start_exchange(): pl.pallas_call(partial(start_kernel, splits), out_shape=[jax.ShapeDtypeSt...  66.3 us
    pallas_call x1, Pallas kernels, weight_grads(): pl.pallas_call(weight_grads_kernel, out_shape=[jax.ShapeDtypeStruct((2, f...  51.3 us
    pallas_call x1, Pallas kernels, project_sum(): pl.pallas_call(partial(project_sum_kernel, parts), out_shape=jax.ShapeDty...  29.5 us
    dot_general x8, matrix products, mm(): return jnp.einsum(spec, left, right, preferred_element_type=jnp.float32)  27.6 us
    unnamed x135, local copies, waits for them, and re-layouts  19.8 us
  transfers between devices with their start and end apart: 2, of which 0 were waited for; matrix products, arithmetic and copies ran while one was open for 6% of the time, Pallas kernels for 25%

profile of v5, /device:TPU:0, one launch (start us, length us, event | category | flops | bytes accessed | tf_op | source)
XLA Modules:
  0.0 978.8 jit_solution(15525184302347001176)
XLA Ops:
  7.2 2.3 copy.138.own
  11.3 2.8 concatenate.53
  14.9 66.3 %start_exchange.1 = (bf16[4,128,2880]{2,1,0:T(8,128)(2,1)}, bf16[4,16,2880]{2,1,0:T(8,128)(2,1)}, bf16[4,720,1280]{2,1,0:T(8,128)(2,1)}) custom-call(bf16[128,2880]{1,0:T(8,128)(2,1)} %copy.138.own, bf16[16,2880]{1,0:T(8,128)(2,1)} %reshape.394.few, bf16[720,4096]{1,0:T(8,128)(2,1)} %wq.1, bf16[720,512]{1,0:T(8,128)(2,1)} %wk.1, bf16[720,512]{1,0:T(8,128)(2,1)} %wv.1), custom_call_target="tpu_custom_call" | custom-call | tf_op jit(solution)/shard_map/start_exchange/pallas_call | solution.py:692
  81.2 1.5 reshape.395
  83.0 2.5 multiply_reduce_fusion
  87.1 7.3 convolution_add_fusion.1
  95.6 2.0 copy.147
  98.0 1.9 add_convert_fusion.1
  101.7 1.9 copy-done.1
  103.6 1.2 fusion.4
  105.4 3.5 convolution_convert_fusion.4
  109.9 2.7 copy-done
  112.6 29.5 %project_sum.1 = f32[128,2880]{1,0:T(8,128)S(1)} custom-call(bf16[4,128,1024]{2,1,0:T(8,128)(2,1)S(1)} %copy.152.m_ref, bf16[2880,1024]{1,0:T(8,128)(2,1)S(1)} %bitcast.158), custom_call_target="tpu_custom_call" | custom-call | flops 3019898880 | bytes 20000000 | tf_op jit(solution)/shard_map/project_sum/pallas_call | solution.py:1216
  145.1 1.5 copy.157
  149.3 1.0 concatenate.61.n_own
  150.4 243.3 %experts.1 = (bf16[2,4,8,128,2944]{4,3,2,1,0:T(8,128)(2,1)}, bf16[4,8,128,2944]{3,2,1,0:T(8,128)(2,1)}, bf16[4,8,128,2944]{3,2,1,0:T(8,128)(2,1)}, bf16[2,4,8,48...) custom-call(bf16[128,2944]{1,0:T(8,128)(2,1)} %concatenate.61.n_own,, ...), custom_call_target="tpu_custom_call" | custom-call | flops 76441190400 | bytes 300000000 | tf_op jit(solution)/shard_map/experts/pallas_call | solution.py:1096
  393.7 219.3 %scatter_blocks.1 = (bf16[2,128,2944]{2,1,0:T(8,128)(2,1)}, bf16[16,4,64,2944]{3,2,1,0:T(8,128)(2,1)}) custom-call(bf16[4,8,128,2944]{3,2,1,0:T(8,128)(2,1)} %get-tuple-element.45.refs_0_, bf16[4,8,128,2944]{3,2,1,0:T(8,128)(2,1)} %get-tuple-element.46.refs_1_), custom_call_target="tpu_custom_call" | custom-call | tf_op jit(solution)/shard_map/scatter_blocks/pallas_call | solution.py:268
  613.0 1.4 bitcast_convert_fusion
  615.9 2.2 fusion.41
  618.2 1.5 convolution_convert_fusion.2
  619.7 1.2 copy.173
  620.8 2.3 reshape.410
  623.2 3.4 copy.172
  626.8 3.1 copy.171
  629.9 2.3 copy.174
  634.0 51.3 %weight_grads.1 = (f32[2,720,2880]{2,1,0:T(8,128)}, f32[2,720,2880]{2,1,0:T(8,128)}, f32[2,720,2880]{2,1,0:T(8,128)}) custom-call(bf16[2,1536,2880]{2,1,0:T(8,128)(2,1)} %bitcast.190, bf16[2,1536,2880]{2,1,0:T(8,128)(2,1)} %bitcast.191, bf16[2,1536,720]{2,1,0:T(8,128)(2,1)} %bitcast.194, bf16[2,1536,720]{2,1,0:T(8,128)(2,1)} %bitcast.195, ...), custom_call_target="tpu_custom_call" | custom-call | flops 38220595200 | bytes 100000000 | tf_op jit(solution)/shard_map/weight_grads/pallas_call | solution.py:1278
  685.3 7.0 convolution_convert_fusion.3
  692.4 1.3 reshape.442
  693.7 2.0 copy.162
  695.8 3.8 fusion
  699.8 1.8 fusion.2
  703.6 1.9 fusion.18
  705.7 2.7 copy.164
  708.4 2.1 reshape.402
  712.0 9.4 multiply_reduce_fusion.1
  721.3 4.6 copy.170
  725.9 2.5 convert_reduce_fusion
  728.6 7.5 convolution_convert_fusion.1
  737.4 9.8 %convolution_convert_fusion = bf16[2880,1280]{1,0:T(8,128)(2,1)} fusion(f32[512,2880]{0,1:T(8,128)} %copy.172, f32[2880]{0:T(1024)S(1)} %copy-done.38, f32[512]{0:T(512)S(1)} %copy-done.54, bf16[512,128]{0,1:T(8,128)(2,1)S(1)} %bitcast.176, bf16[512,128]{0,1:T(8,128)(2,1)S(1)} %bitcast.179, bf16[512,1024]{0,1:T(8,128)(2,1)S(1)} %bitcast.167), kind=kOutput, calls=%fused_computation.1 | convolution fusion | flops 3786915840 | bytes 14595328 | tf_op jit(solution)/shard_map/dot_general | solution.py:84
  747.2 193.6 %reduce_parts.1 = (bf16[2,10,144,1024]{3,2,1,0:T(8,128)(2,1)}, bf16[768,4096]{1,0:T(8,128)(2,1)}, bf16[768,512]{1,0:T(8,128)(2,1)}, bf16[768,512]{1,0:T(8,128)(2,1)}) custom-call(bf16[2,10,144,1024]{3,2,1,0:T(8,128)(2,1)} %bitcast.162, bf16[4,720,1280]{2,1,0:T(8,128)(2,1)} %bitcast.161, bf16[4,48,1280]{2,1,0:T(8,128)(2,1)} %pad.19.gs), custom_call_target="tpu_custom_call" | custom-call | bytes 500000000 | tf_op jit(solution)/shard_map/reduce_parts/pallas_call | solution.py:550
  940.8 1.0 slice_convert_fusion.4
  946.3 1.3 slice_convert_fusion.1
  947.6 1.3 slice_convert_fusion.2
  948.9 9.1 convert_bitcast_fusion
  958.0 6.1 slice_convert_fusion
  964.2 1.6 fusion.9
  965.8 2.7 fusion.12
  968.5 2.9 copy.175
  (231 shorter events, 27.7 us)
Async XLA Ops:
  7.2 678.1 %all-gather.2.cloned.1.call-start = ((), (), s32[]{:S(2)}) async-start(), calls=%async_computation.1 | async-start | bytes 3768320 | tf_op jit(solution)/shard_map/all_gather | solution.py:100
  81.2 4.9 copy-start.3
  83.0 4.1 copy-start.37
  97.9 2.0 copy-start.16
  97.9 2.0 copy-start.18
  98.0 2.3 copy-start.59
  100.4 4.4 copy-start.45
  100.6 4.2 copy-start.12
  100.8 4.7 copy-start.22
  101.6 2.0 copy-start.1
  101.6 3.5 copy-start.30
  101.7 7.3 copy-start.33
  104.9 4.0 copy-start.39
  105.4 3.5 copy-start.41
  109.9 2.7 copy-start
  112.6 29.5 %copy-start.7 = (bf16[128,2880]{1,0:T(8,128)(2,1)S(1)}, bf16[128,2880]{1,0:T(8,128)(2,1)}, u32[]{:S(2)}) copy-start(bf16[128,2880]{1,0:T(8,128)(2,1)} %copy.138.own) | copy-start | bytes 2211844
  142.5 4.1 copy-start.5
  144.3 6.1 copy-start.9
  144.3 3.2 copy-start.44
  144.3 3.8 copy-start.51
  144.3 4.4 copy-start.52
  393.7 221.0 %copy-start.50 = (f32[128]{0:T(128)S(1)}, f32[128]{0:T(128)}, u32[]{:S(2)}) copy-start(f32[128]{0:T(128)} %copy-done.49) | copy-start | bytes 1540
  613.0 1.8 copy-start.11
  618.1 5.1 copy-start.4
  618.1 346.1 %reduce-scatter.2.cloned.1.call-start = ((), (), s32[]{:S(2)}) async-start(), calls=%async_computation.2 | async-start | bytes 3768320 | tf_op jit(solution)/shard_map/reduce_scatter | solution.py:104
  626.6 5.5 copy-start.43
  626.6 6.1 copy-start.48
  626.6 6.7 copy-start.47
  692.3 3.4 copy-start.23
  692.4 3.4 copy-start.34
  692.4 3.4 copy-start.40
  695.7 3.8 copy-start.31
  695.7 3.8 copy-start.36
  695.8 3.8 copy-start.46
  695.8 4.0 copy-start.2
  699.8 1.8 copy-start.27
  699.8 1.8 copy-start.29
  708.4 2.1 copy-start.17
  708.4 2.2 copy-start.19
  725.9 2.7 copy-start.21
  728.6 7.7 copy-start.32
  728.6 8.8 copy-start.38
  940.8 5.5 copy-start.25
  940.8 6.8 copy-start.24
  947.6 10.4 %slice-start = ((s8[6291456]{0:T(1024)(128)(4,1)}), s8[4194304]{0:T(1024)(128)(4,1)S(1)}, s32[]{:S(2)}) async-start(s8[6291456]{0:T(1024)(128)(4,1)} %bitcast.163), calls=%async_computation.3 | async-start | bytes 8388608
  948.9 9.1 slice-start.1
  958.0 6.2 copy-start.8
  958.0 7.7 copy-start.14
  (16 other events, 18.8 us)
Sparse Core Ops, SparseCore 0:
  618.2 53.8 all-gather.1
  726.1 61.1 reduce-scatter.1
